TPU v7x, 32 devices: a whole 2x2x4 slice. The times are simulated.
32 devices in a mesh: groups: 2 (over y), row: 4 (over z), col: 4 (over x, core).
Axes of the slice: x: 2, y: 2, z: 4, core: 2. Of those that a mesh axis runs over, the one named last changes fastest.
Arguments:
- tokens: bfloat16 [256, 4096], P(('groups', 'row'), 'col'), parts along dimension 0, may hold values from -6 to 6
- out_grad: bfloat16 [256, 4096], P(('groups', 'row'), 'col'), parts along dimension 0, may hold values from -6 to 6
- gate_weight: bfloat16 [8192, 14336], P(('groups', 'col'), 'row'), parts along dimension 0, may hold values from -0.1875 to 0.1875
- up_weight: bfloat16 [8192, 14336], P(('groups', 'col'), 'row'), parts along dimension 0, may hold values from -0.1875 to 0.1875
- down_weight: bfloat16 [28672, 4096], P(('groups', 'row'), 'col'), parts along dimension 0, may hold values from -0.09375 to 0.09375
- gate_mask: int32 [64, 112], P('groups'), parts along dimension 0, may hold values 0 or 1
- up_mask: int32 [64, 112], P('groups'), parts along dimension 0, may hold values 0 or 1
- down_mask: int32 [224, 32], P('groups'), parts along dimension 0, may hold values 0 or 1
Outputs:
- grad_tokens: bfloat16 [256, 4096], P(('groups', 'row'), 'col'), parts along dimension 0
- grad_gate: bfloat16 [8192, 14336], P(('groups', 'col'), 'row'), parts along dimension 0
- grad_up: bfloat16 [8192, 14336], P(('groups', 'col'), 'row'), parts along dimension 0
- grad_down: bfloat16 [28672, 4096], P(('groups', 'row'), 'col'), parts along dimension 0
There are 2 independent parts, one for each index of `groups`. A program takes and returns all parts, laid end to end along the dimension named above; each array names one. Nothing has to cross between parts.
All inputs are finite; a program needn't handle non-finite values.
Results may differ from a plain program's by a relative error of at most 0.019.
Values may be sent and summed in bfloat16 or wider, within the bound.
No kernel may reach another device: no remote copies, remote signals or barrier semaphores. Data moves between devices by JAX's collectives and lax.ppermute only.
A program may use at most 128 MiB of HBM per device.

v0:
```python
import jax
import jax.numpy as jnp
from jax import lax
from jax.sharding import PartitionSpec as P

BLK = 128


def block_keep(block_table, row_first, row_count, col_first, col_count):
    row_blocks = (row_first + jnp.arange(row_count, dtype=jnp.int32)) // BLK
    col_blocks = (col_first + jnp.arange(col_count, dtype=jnp.int32)) // BLK
    pick_rows = (
        row_blocks[:, None] == jnp.arange(block_table.shape[0], dtype=jnp.int32)[None, :]
    ).astype(jnp.float32)
    pick_cols = (
        jnp.arange(block_table.shape[1], dtype=jnp.int32)[:, None] == col_blocks[None, :]
    ).astype(jnp.float32)
    spread = jnp.dot(jnp.dot(pick_rows, block_table.astype(jnp.float32)), pick_cols)
    return spread.astype(jnp.bfloat16)


def contract_rows(left, right):
    return lax.dot_general(
        left, right, (((0,), (0,)), ((), ())), preferred_element_type=jnp.float32
    )


def contract_cols(left, right):
    return lax.dot_general(
        left, right, (((1,), (1,)), ((), ())), preferred_element_type=jnp.float32
    )


def pointwise(gate_pre, up_pre, hidden_grad):
    sigmoid_gate = jax.nn.sigmoid(gate_pre)
    active = gate_pre * sigmoid_gate
    hidden = (active * up_pre).astype(jnp.bfloat16)
    grad_gate_act = (
        hidden_grad * up_pre * sigmoid_gate * (1.0 + gate_pre * (1.0 - sigmoid_gate))
    ).astype(jnp.bfloat16)
    grad_up_act = (hidden_grad * active).astype(jnp.bfloat16)
    return (hidden, grad_gate_act, grad_up_act)


def local(tokens, out_grad, gate_weight, up_weight, down_weight, gate_mask, up_mask, down_mask):
    rank_row = lax.axis_index("row")
    rank_col = lax.axis_index("col")
    feat_width = gate_weight.shape[0]
    unit_width = gate_weight.shape[1]
    gate_keep = block_keep(
        gate_mask, rank_col * feat_width, feat_width, rank_row * unit_width, unit_width
    )
    up_keep = block_keep(
        up_mask, rank_col * feat_width, feat_width, rank_row * unit_width, unit_width
    )
    down_keep = block_keep(
        down_mask, rank_row * unit_width, unit_width, rank_col * feat_width, feat_width
    )
    gate_live = gate_weight * gate_keep
    up_live = up_weight * up_keep
    down_live = down_weight * down_keep
    tokens_all, grads_all = (
        lax.all_gather(tokens, "row", axis=0, tiled=True),
        lax.all_gather(out_grad, "row", axis=0, tiled=True),
    )
    summed = lax.psum_scatter(
        jnp.concatenate(
            [
                jnp.dot(tokens_all, gate_live, preferred_element_type=jnp.float32),
                jnp.dot(tokens_all, up_live, preferred_element_type=jnp.float32),
                contract_cols(grads_all, down_live),
            ],
            axis=1,
        ).astype(jnp.bfloat16),
        "col",
        scatter_dimension=0,
        tiled=True,
    ).astype(jnp.float32)
    local_parts = pointwise(
        summed[:, :unit_width], summed[:, unit_width : 2 * unit_width], summed[:, 2 * unit_width :]
    )
    hidden, grad_gate_act, grad_up_act = (
        lax.all_gather(local_parts[0], "col", axis=0, tiled=True),
        lax.all_gather(local_parts[1], "col", axis=0, tiled=True),
        lax.all_gather(local_parts[2], "col", axis=0, tiled=True),
    )
    grad_tokens = lax.psum_scatter(
        (contract_cols(grad_gate_act, gate_live) + contract_cols(grad_up_act, up_live)).astype(
            jnp.bfloat16
        ),
        "row",
        scatter_dimension=0,
        tiled=True,
    )
    grad_gate = (contract_rows(tokens_all, grad_gate_act) * gate_keep).astype(jnp.bfloat16)
    grad_up = (contract_rows(tokens_all, grad_up_act) * up_keep).astype(jnp.bfloat16)
    grad_down = (contract_rows(hidden, grads_all) * down_keep).astype(jnp.bfloat16)
    return (grad_tokens, grad_gate, grad_up, grad_down)


def solution(mesh):
    in_specs = (
        P(("groups", "row"), "col"),
        P(("groups", "row"), "col"),
        P(("groups", "col"), "row"),
        P(("groups", "col"), "row"),
        P(("groups", "row"), "col"),
        P("groups", None),
        P("groups", None),
        P("groups", None),
    )
    out_specs = (
        P(("groups", "row"), "col"),
        P(("groups", "col"), "row"),
        P(("groups", "col"), "row"),
        P(("groups", "row"), "col"),
    )
    return jax.shard_map(local, mesh=mesh, in_specs=in_specs, out_specs=out_specs, check_vma=False)
```

profile of v0, /device:TPU:0, one launch (start us, length us, event | category | flops | bytes accessed | tf_op | source)
XLA Modules:
  0.0 209.6 jit_solution(17590268652883622031)
XLA Ops:
  7.2 0.0 copy-start.1
  7.2 0.0 reduce-scatter.7.cloned.1.call-start
  7.3 15.8 %all_gather.15 = bf16[128,1024]{1,0:T(8,128)(2,1)S(1)} all-gather(bf16[32,1024]{1,0:T(8,128)(2,1)} %param.8), channel_id=1, replica_groups=mesh['groups'=2,'row'=4,'col'=4] {'row'}, dimensions={0}, use_global_device_ids=true | all-gather | bytes 327680 | tf_op jit(solution)/shard_map/all_gather | solution.py:63
  23.1 14.8 %all_gather.16 = bf16[128,1024]{1,0:T(8,128)(2,1)S(1)} all-gather(bf16[32,1024]{1,0:T(8,128)(2,1)} %param.9), channel_id=1, replica_groups=mesh['groups'=2,'row'=4,'col'=4] {'row'}, dimensions={0}, use_global_device_ids=true | all-gather | bytes 327680 | tf_op jit(solution)/shard_map/all_gather | solution.py:64
  37.9 6.3 %convolution_convert_fusion = bf16[3584,1024]{1,0:T(8,128)(2,1)} fusion(s32[3584]{0:T(1024)S(1)} %add_select_fusion, s32[1024]{0:T(1024)S(1)} %add_select_fusion.1, s32[112,32]{0,1:T(8,128)} %param.15), kind=kOutput, calls=%fused_computation.5 | convolution fusion | flops 264678912 | bytes 7372800 | tf_op jit(solution)/shard_map/dot_general | solution.py:18
  44.2 0.0 copy-done.1
  44.2 9.0 %fusion.40 = (bf16[1024,3584]{1,0:T(8,128)(2,1)}, bf16[1024,3584]{1,0:T(8,128)(2,1)}) fusion(bf16[1024,3584]{1,0:T(8,128)(2,1)} %param.11, s32[3584]{0:T(1024)S(1)} %add_select_fusion, s32[1024]{0:T(1024)S(1)} %add_select_fusion.1, s32[32,112]{1,0:T(8,128)S(1)} %copy-done.1), kind=kOutput, calls=%fused_computation.58 | convolution fusion | flops 848211456 | bytes 22052864 | tf_op jit(solution)/shard_map/dot_general | solution.py:18
  53.2 0.0 copy-start.2
  53.2 6.2 %fusion.8 = bf16[128,3584]{0,1:T(8,128)(2,1)} fusion(bf16[1024,3584]{1,0:T(8,128)(2,1)} %get-tuple-element.7, bf16[128,1024]{1,0:T(8,128)(2,1)S(1)} %all_gather.15), kind=kOutput, calls=%fused_computation.14 | convolution fusion | flops 939982848 | bytes 8519680 | tf_op jit(solution)/shard_map/dot_general | solution.py:70
  59.3 0.0 copy-done.2
  59.4 9.0 %fusion.43 = (bf16[1024,3584]{1,0:T(8,128)(2,1)}, bf16[1024,3584]{1,0:T(8,128)(2,1)}) fusion(bf16[1024,3584]{1,0:T(8,128)(2,1)} %param.10, s32[3584]{0:T(1024)S(1)} %add_select_fusion, s32[1024]{0:T(1024)S(1)} %add_select_fusion.1, s32[32,112]{1,0:T(8,128)S(1)} %copy-done.2), kind=kOutput, calls=%fused_computation.59 | convolution fusion | flops 848211456 | bytes 22052864 | tf_op jit(solution)/shard_map/dot_general | solution.py:18
  68.3 5.2 %fusion.7 = bf16[128,3584]{0,1:T(8,128)(2,1)S(1)} fusion(bf16[1024,3584]{1,0:T(8,128)(2,1)} %get-tuple-element.9, bf16[128,1024]{1,0:T(8,128)(2,1)S(1)} %all_gather.15), kind=kOutput, calls=%fused_computation.13 | convolution fusion | flops 939982848 | bytes 8519680 | tf_op jit(solution)/shard_map/dot_general | solution.py:69
  73.5 0.0 copy-start
  73.5 7.3 %fusion.9 = bf16[128,3584]{0,1:T(8,128)(2,1)S(1)} fusion(bf16[128,1024]{1,0:T(8,128)(2,1)S(1)} %all_gather.16, bf16[3584,1024]{1,0:T(8,128)(2,1)} %param.12, bf16[3584,1024]{1,0:T(8,128)(2,1)} %convolution_convert_fusion), kind=kOutput, calls=%fused_computation.15 | convolution fusion | flops 943652864 | bytes 15859712 | tf_op jit(solution)/shard_map/dot_general | solution.py:29
  80.9 0.0 copy-done
  80.9 13.6 %pad_maximum_fusion = bf16[128,10752]{0,1:T(8,128)(2,1)S(1)} fusion(bf16[128,3584]{0,1:T(8,128)(2,1)S(1)} %fusion.9, bf16[128,3584]{0,1:T(8,128)(2,1)S(1)} %copy-done, bf16[128,3584]{0,1:T(8,128)(2,1)S(1)} %fusion.7), kind=kLoop, calls=%fused_computation.16 | loop fusion | flops 8257536 | bytes 5505024 | tf_op jit(solution)/shard_map/concatenate | solution.py:67
  94.5 2.7 %copy.29 = bf16[128,10752]{1,0:T(8,128)(2,1)} copy(bf16[128,10752]{0,1:T(8,128)(2,1)S(1)} %pad_maximum_fusion) | data formatting | bytes 5505024
  97.2 0.0 reduce-scatter.7.cloned.1.call-update
  97.2 0.0 reduce-scatter.5.cloned.1.call-start
  97.3 36.5 %reduce-scatter.7.cloned.1.call-done = bf16[32,10752]{1,0:T(8,128)(2,1)} async-done(((bf16[128,10752]{1,0:T(8,128)(2,1)}), bf16[32,10752]{1,0:T(8,128)(2,1)}) %reduce-scatter.7.cloned.1.call-update) | async-done | bytes 688144 | tf_op jit(solution)/shard_map/reduce_scatter | solution.py:66
  133.8 1.2 convert_element_type.64
  135.0 0.2 multiply_convert_fusion.1
  135.2 0.0 slice-start.4
  135.2 0.0 slice-start
  135.2 9.1 %all_gather.19 = bf16[128,3584]{1,0:T(8,128)(2,1)S(1)} all-gather(bf16[32,3584]{1,0:T(8,128)(2,1)S(1)} %get-tuple-element.4), channel_id=1, replica_groups=mesh['groups'=2,'row'=4,'col'=4] {'col'}, dimensions={0}, use_global_device_ids=true | all-gather | bytes 1146880 | tf_op jit(solution)/shard_map/all_gather | solution.py:83
  144.3 0.0 slice-start.5
  144.3 0.0 slice-start.1
  144.3 8.4 %multiply_convert_fusion = bf16[3584,1024]{1,0:T(8,128)(2,1)} fusion(bf16[3584,1024]{1,0:T(8,128)(2,1)} %convolution_convert_fusion, bf16[128,3584]{1,0:T(8,128)(2,1)S(1)} %all_gather.19, bf16[128,1024]{1,0:T(8,128)(2,1)S(1)} %all_gather.16), kind=kOutput, calls=%fused_computation.4 | convolution fusion | flops 950534144 | bytes 15859712 | tf_op jit(solution)/shard_map/dot_general | solution.py:23
  152.7 9.6 %all_gather.17 = bf16[128,3584]{1,0:T(8,128)(2,1)S(1)} all-gather(bf16[32,3584]{1,0:T(8,128)(2,1)S(1)} %get-tuple-element.5), channel_id=1, replica_groups=mesh['groups'=2,'row'=4,'col'=4] {'col'}, dimensions={0}, use_global_device_ids=true | all-gather | bytes 1146880 | tf_op jit(solution)/shard_map/all_gather | solution.py:84
  162.3 0.0 slice-done.4
  162.3 0.0 slice-done.5
  162.3 0.0 slice-start.2
  162.3 2.4 %fusion.46 = f32[128,1024]{1,0:T(8,128)S(1)} fusion(bf16[128,3584]{1,0:T(8,128)(2,1)S(1)} %all_gather.17, bf16[1024,3584]{1,0:T(8,128)(2,1)S(1)} %bitcast.35), kind=kOutput, calls=%fused_computation.60 | convolution fusion | flops 939524096 | bytes 8781824 | tf_op jit(solution)/shard_map/dot_general | solution.py:29
  164.8 0.0 slice-done
  164.8 0.0 slice-done.1
  164.8 0.0 slice-start.3
  164.8 5.2 %fusion.1 = bf16[1024,3584]{1,0:T(8,128)(2,1)} fusion(bf16[1024,3584]{1,0:T(8,128)(2,1)S(1)} %bitcast.31, bf16[128,3584]{1,0:T(8,128)(2,1)S(1)} %all_gather.17, bf16[128,1024]{1,0:T(8,128)(2,1)S(1)} %all_gather.15), kind=kOutput, calls=%fused_computation.3 | convolution fusion | flops 950534144 | bytes 15859712 | tf_op jit(solution)/shard_map/dot_general | solution.py:23
  170.0 9.4 %all_gather.18 = bf16[128,3584]{1,0:T(8,128)(2,1)S(1)} all-gather(bf16[32,3584]{1,0:T(8,128)(2,1)S(1)} %get-tuple-element.6), channel_id=1, replica_groups=mesh['groups'=2,'row'=4,'col'=4] {'col'}, dimensions={0}, use_global_device_ids=true | all-gather | bytes 1146880 | tf_op jit(solution)/shard_map/all_gather | solution.py:85
  179.4 0.0 slice-done.2
  179.4 0.0 slice-done.3
  179.4 3.1 %fusion.17 = bf16[128,1024]{1,0:T(8,128)(2,1)} fusion(f32[128,1024]{1,0:T(8,128)S(1)} %fusion.46, bf16[128,3584]{1,0:T(8,128)(2,1)S(1)} %all_gather.18, bf16[1024,3584]{1,0:T(8,128)(2,1)S(1)} %bitcast.33), kind=kOutput, calls=%fused_computation.23 | convolution fusion | flops 939786240 | bytes 9043968 | tf_op jit(solution)/shard_map/dot_general | solution.py:29
  182.5 0.0 reduce-scatter.5.cloned.1.call-update
  182.6 8.2 %fusion = bf16[1024,3584]{1,0:T(8,128)(2,1)} fusion(bf16[1024,3584]{1,0:T(8,128)(2,1)} %get-tuple-element.8, bf16[128,3584]{1,0:T(8,128)(2,1)S(1)} %all_gather.18, bf16[128,1024]{1,0:T(8,128)(2,1)S(1)} %all_gather.15), kind=kOutput, calls=%fused_computation.1 | convolution fusion | flops 950534144 | bytes 15859712 | tf_op jit(solution)/shard_map/dot_general | solution.py:23
  190.8 12.0 %reduce-scatter.5.cloned.1.call-done = bf16[32,1024]{1,0:T(8,128)(2,1)} async-done(((bf16[128,1024]{1,0:T(8,128)(2,1)}), bf16[32,1024]{1,0:T(8,128)(2,1)}) %reduce-scatter.5.cloned.1.call-update) | async-done | bytes 65552 | tf_op jit(solution)/shard_map/reduce_scatter | solution.py:87
  (5 shorter events, 0.0 us)
Async XLA Ops:
  7.2 37.1 %copy-start.1 = (s32[32,112]{1,0:T(8,128)S(1)}, s32[32,112]{1,0:T(8,128)}, u32[]{:S(2)}) copy-start(s32[32,112]{1,0:T(8,128)} %param.14) | copy-start | bytes 43012
  7.2 126.6 %reduce-scatter.7.cloned.1.call-start = ((), (), s32[]{:S(2)}) async-start(), calls=%async_computation.3 | async-start | bytes 3440640 | tf_op jit(solution)/shard_map/reduce_scatter | solution.py:66
  53.2 6.2 %copy-start.2 = (s32[32,112]{1,0:T(8,128)S(1)}, s32[32,112]{1,0:T(8,128)}, u32[]{:S(2)}) copy-start(s32[32,112]{1,0:T(8,128)} %param.13) | copy-start | bytes 43012
  73.5 7.3 %copy-start = (bf16[128,3584]{0,1:T(8,128)(2,1)S(1)}, bf16[128,3584]{0,1:T(8,128)(2,1)}, u32[]{:S(2)}) copy-start(bf16[128,3584]{0,1:T(8,128)(2,1)} %fusion.8) | copy-start | bytes 2752516
  97.2 105.6 %reduce-scatter.5.cloned.1.call-start = ((), (), s32[]{:S(2)}) async-start(), calls=%async_computation.2 | async-start | bytes 327680 | tf_op jit(solution)/shard_map/reduce_scatter | solution.py:87
  135.2 27.1 %slice-start.4 = ((s8[7340032]{0:T(1024)(128)(4,1)}), s8[4194304]{0:T(1024)(128)(4,1)S(1)}, s32[]{:S(2)}) async-start(s8[7340032]{0:T(1024)(128)(4,1)} %bitcast.34), calls=%async_computation.8 | async-start | bytes 8388608
  135.2 29.5 %slice-start = ((s8[7340032]{0:T(1024)(128)(4,1)}), s8[4194304]{0:T(1024)(128)(4,1)S(1)}, s32[]{:S(2)}) async-start(s8[7340032]{0:T(1024)(128)(4,1)} %bitcast.30), calls=%async_computation.4 | async-start | bytes 8388608
  144.3 18.0 %slice-start.5 = ((s8[7340032]{0:T(1024)(128)(4,1)}), s8[3145728]{0:T(1024)(128)(4,1)S(1)}, s32[]{:S(2)}) async-start(s8[7340032]{0:T(1024)(128)(4,1)} %bitcast.34), calls=%async_computation.9 | async-start | bytes 6291456
  144.3 20.5 %slice-start.1 = ((s8[7340032]{0:T(1024)(128)(4,1)}), s8[3145728]{0:T(1024)(128)(4,1)S(1)}, s32[]{:S(2)}) async-start(s8[7340032]{0:T(1024)(128)(4,1)} %bitcast.30), calls=%async_computation.5 | async-start | bytes 6291456
  162.3 17.1 %slice-start.2 = ((s8[7340032]{0:T(1024)(128)(4,1)}), s8[4194304]{0:T(1024)(128)(4,1)S(1)}, s32[]{:S(2)}) async-start(s8[7340032]{0:T(1024)(128)(4,1)} %bitcast.32), calls=%async_computation.6 | async-start | bytes 8388608
  164.8 14.6 %slice-start.3 = ((s8[7340032]{0:T(1024)(128)(4,1)}), s8[3145728]{0:T(1024)(128)(4,1)S(1)}, s32[]{:S(2)}) async-start(s8[7340032]{0:T(1024)(128)(4,1)} %bitcast.32), calls=%async_computation.7 | async-start | bytes 6291456
Sparse Core Ops, SparseCore 0:
  97.3 36.4 reduce-scatter.6
  182.7 20.0 reduce-scatter.4
where the time goes:
time: 210 us
  matrix products  70.2 us (33%)
  blocking collectives  58.8 us (28%)
  waiting for transfers between devices  48.5 us (23%)
  other arithmetic  15 us (7%)
  between operations  14.2 us (7%)
  local copies, waits for them, and re-layouts  2.77 us (1%)
    reduce_scatter x1, waiting for transfers between devices, local(): lax.psum_scatter(jnp.concatenate([jnp.dot(tokens_all, gate_live, preferre...  36.5 us
    dot_general x3, matrix products, block_keep(): jnp.dot(jnp.dot(pick_rows, block_table.astype(jnp.float32)), pick_cols)  24.2 us
    dot_general x3, matrix products, contract_rows(): lax.dot_general(left, right, (((0,), (0,)), ((), ())), preferred_element_...  21.8 us
    all_gather x1, blocking collectives, local(): lax.all_gather(tokens, 'row', axis=0, tiled=True)  15.8 us
    all_gather x1, blocking collectives, local(): lax.all_gather(out_grad, 'row', axis=0, tiled=True)  14.8 us
    concatenate x1, other arithmetic, local(): jnp.concatenate([jnp.dot(tokens_all, gate_live, preferred_element_type=jn...  13.6 us
    dot_general x3, matrix products, contract_cols(): lax.dot_general(left, right, (((1,), (1,)), ((), ())), preferred_element_...  12.9 us
    reduce_scatter x1, waiting for transfers between devices, local(): lax.psum_scatter((contract_cols(grad_gate_act, gate_live) + contract_cols...  12 us
  transfers between devices with their start and end apart: 2, of which 2 were waited for; matrix products, arithmetic and copies ran while one was open for 4% of the time, Pallas kernels for 0%

commit v1 on v0

v1 whole, which is shorter than its diff:
```python
import functools

import jax
import jax.numpy as jnp
from jax import lax
from jax.experimental import pallas as pl
from jax.experimental.pallas import tpu as pltpu
from jax.sharding import PartitionSpec as P

BLK = 128
TILE = 512
VMEM_LIMIT = 40 * 1024 * 1024
BF = jnp.bfloat16
F32 = jnp.float32


def params():
    return pltpu.CompilerParams(vmem_limit_bytes=VMEM_LIMIT)


def gcd_of(a, b):
    while b:
        a, b = b, a % b
    return a


def block_index(first, count, step):
    return (first + jnp.arange(count, dtype=jnp.int32) * step) // BLK


def pick(table, row_index, col_index):
    rows = (row_index[:, None] == jnp.arange(table.shape[0], dtype=jnp.int32)[None, :]).astype(BF)
    cols = (jnp.arange(table.shape[1], dtype=jnp.int32)[:, None] == col_index[None, :]).astype(BF)
    part = jnp.dot(rows, (table > 0).astype(BF), preferred_element_type=F32).astype(BF)
    return jnp.dot(part, cols, preferred_element_type=F32).astype(BF)


def mask_rows(weight, keep, rows):
    return jnp.concatenate(
        [weight[i * rows : (i + 1) * rows, :] * keep[i : i + 1, :] for i in range(keep.shape[0])], axis=0
    )


def dot_nt(left, right):
    return lax.dot_general(left, right, (((1,), (1,)), ((), ())), preferred_element_type=F32)


def dot_tn(left, right):
    return lax.dot_general(left, right, (((0,), (0,)), ((), ())), preferred_element_type=F32)


def forward_kernel(x_ref, og_ref, gate_ref, up_ref, down_ref, gk_ref, uk_ref, dk_ref, keep_ref, send_ref):
    half = keep_ref.shape[1]
    granule = down_ref.shape[0] // dk_ref.shape[1]
    x = x_ref[...]
    gate = jnp.dot(x, mask_rows(gate_ref[...], gk_ref[...], BLK), preferred_element_type=F32).astype(BF)
    up = jnp.dot(x, mask_rows(up_ref[...], uk_ref[...], BLK), preferred_element_type=F32).astype(BF)
    grad = dot_nt(og_ref[...], mask_rows(down_ref[...], dk_ref[0], granule)).astype(BF)
    for i, part in enumerate((gate, up, grad)):
        keep_ref[i] = part[:half]
        send_ref[i] = part[half:]


def forward(x, og, gate_w, up_w, down_w, gk, uk, dk, first, tiles, tile):
    rows, feats = x.shape
    half = rows // 2
    span = tiles * tile
    out = jax.ShapeDtypeStruct((3, half, span), BF)
    return pl.pallas_call(
        forward_kernel,
        out_shape=(out, out),
        grid=(tiles,),
        in_specs=[
            pl.BlockSpec((rows, feats), lambda i: (0, 0)),
            pl.BlockSpec((rows, feats), lambda i: (0, 0)),
            pl.BlockSpec((feats, tile), lambda i: (0, first + i)),
            pl.BlockSpec((feats, tile), lambda i: (0, first + i)),
            pl.BlockSpec((tile, feats), lambda i: (first + i, 0)),
            pl.BlockSpec((gk.shape[0], tile), lambda i: (0, first + i)),
            pl.BlockSpec((uk.shape[0], tile), lambda i: (0, first + i)),
            pl.BlockSpec((1,) + dk.shape[1:], lambda i: (first + i, 0, 0)),
        ],
        out_specs=[pl.BlockSpec((3, half, tile), lambda i: (0, 0, i))] * 2,
        compiler_params=params(),
        cost_estimate=pl.CostEstimate(
            flops=6 * rows * feats * span, bytes_accessed=6 * feats * span + 4 * rows * feats, transcendentals=0
        ),
        name="forward",
    )(x, og, gate_w, up_w, down_w, gk, uk, dk)


def grad_tokens_kernel(n_parts, prev_ref, gate_ref, up_ref, gk_ref, uk_ref, *rest):
    parts, out_ref = rest[:n_parts], rest[n_parts]

    @pl.when(pl.program_id(0) == 0)
    def _():
        out_ref[...] = prev_ref[...]

    gate_act = jnp.concatenate([p[1] for p in parts], axis=0)
    up_act = jnp.concatenate([p[2] for p in parts], axis=0)
    out_ref[...] += dot_nt(gate_act, mask_rows(gate_ref[...], gk_ref[...], BLK)) + dot_nt(
        up_act, mask_rows(up_ref[...], uk_ref[...], BLK)
    )


def grad_tokens_of(prev, gate_w, up_w, gk, uk, parts, starts, first, tiles, tile):
    rows, feats = prev.shape
    span = tiles * tile
    return pl.pallas_call(
        functools.partial(grad_tokens_kernel, len(parts)),
        out_shape=jax.ShapeDtypeStruct((rows, feats), F32),
        grid=(tiles,),
        in_specs=[
            pl.BlockSpec((rows, feats), lambda i: (0, 0)),
            pl.BlockSpec((feats, tile), lambda i: (0, first + i)),
            pl.BlockSpec((feats, tile), lambda i: (0, first + i)),
            pl.BlockSpec((gk.shape[0], tile), lambda i: (0, first + i)),
            pl.BlockSpec((uk.shape[0], tile), lambda i: (0, first + i)),
        ]
        + [
            pl.BlockSpec((3, p.shape[1], tile), functools.partial(lambda s, i: (0, 0, first - s + i), s))
            for p, s in zip(parts, starts)
        ],
        out_specs=pl.BlockSpec((rows, feats), lambda i: (0, 0)),
        compiler_params=params(),
        cost_estimate=pl.CostEstimate(
            flops=4 * rows * feats * span, bytes_accessed=4 * feats * span + 8 * rows * feats, transcendentals=0
        ),
        name="grad_tokens",
    )(prev, gate_w, up_w, gk, uk, *parts)


def weight_grads_kernel(n_parts, n_prev, xt_ref, og_ref, gk_ref, uk_ref, dk_ref, *rest):
    parts = rest[:n_parts]
    gate_ref, up_ref, down_ref = rest[n_parts + n_prev :]
    granule = down_ref.shape[0] // dk_ref.shape[1]
    xt = xt_ref[...]
    hidden = jnp.concatenate([p[0] for p in parts], axis=0)
    gate_act = jnp.concatenate([p[1] for p in parts], axis=0)
    up_act = jnp.concatenate([p[2] for p in parts], axis=0)
    gate_ref[...] = mask_rows(
        jnp.dot(xt, gate_act, preferred_element_type=F32).astype(BF), gk_ref[...], BLK
    )
    up_ref[...] = mask_rows(jnp.dot(xt, up_act, preferred_element_type=F32).astype(BF), uk_ref[...], BLK)
    down_ref[...] = mask_rows(dot_tn(hidden, og_ref[...]).astype(BF), dk_ref[0], granule)


def weight_grads(prev, xt, og, gk, uk, dk, parts, starts, first, tiles, tile, units):
    feats, rows = xt.shape
    span = tiles * tile
    n_prev = 0 if prev is None else 3
    base = 5 + len(parts)
    return pl.pallas_call(
        functools.partial(weight_grads_kernel, len(parts), n_prev),
        out_shape=(
            jax.ShapeDtypeStruct((feats, units), BF),
            jax.ShapeDtypeStruct((feats, units), BF),
            jax.ShapeDtypeStruct((units, feats), BF),
        ),
        grid=(tiles,),
        in_specs=[
            pl.BlockSpec((feats, rows), lambda i: (0, 0)),
            pl.BlockSpec((rows, feats), lambda i: (0, 0)),
            pl.BlockSpec((gk.shape[0], tile), lambda i: (0, first + i)),
            pl.BlockSpec((uk.shape[0], tile), lambda i: (0, first + i)),
            pl.BlockSpec((1,) + dk.shape[1:], lambda i: (first + i, 0, 0)),
        ]
        + [
            pl.BlockSpec((3, p.shape[1], tile), functools.partial(lambda s, i: (0, 0, first - s + i), s))
            for p, s in zip(parts, starts)
        ]
        + [pl.BlockSpec(memory_space=pl.ANY)] * n_prev,
        out_specs=[
            pl.BlockSpec((feats, tile), lambda i: (0, first + i)),
            pl.BlockSpec((feats, tile), lambda i: (0, first + i)),
            pl.BlockSpec((tile, feats), lambda i: (first + i, 0)),
        ],
        input_output_aliases={base + k: k for k in range(n_prev)},
        compiler_params=params(),
        cost_estimate=pl.CostEstimate(
            flops=6 * rows * feats * span, bytes_accessed=6 * feats * span + 4 * rows * feats, transcendentals=0
        ),
        name="weight_grads",
    )(xt, og, gk, uk, dk, *parts, *(() if prev is None else prev))


def pointwise(total):
    gate_pre, up_pre, hidden_grad = total[0], total[1], total[2]
    sigmoid_gate = jax.nn.sigmoid(gate_pre)
    active = gate_pre * sigmoid_gate
    hidden = (active * up_pre).astype(BF)
    grad_gate_act = (
        hidden_grad * up_pre * sigmoid_gate * (1.0 + gate_pre * (1.0 - sigmoid_gate))
    ).astype(BF)
    grad_up_act = (hidden_grad * active).astype(BF)
    return jnp.stack([hidden, grad_gate_act, grad_up_act])


def chunks_of(tiles, sizes):
    out, first = [], 0
    for size in sizes:
        size = min(size, tiles - first)
        if size > 0:
            out.append((first, size))
            first += size
    if first < tiles:
        out.append((first, tiles - first))
    return out


def local(n_row, n_col, tokens, out_grad, gate_w, up_w, down_w, gate_mask, up_mask, down_mask):
    rank_row, rank_col = lax.axis_index("row"), lax.axis_index("col")
    own, feats = tokens.shape
    units = gate_w.shape[1]
    half = own // 2
    n_chip = n_col // 2
    second_core = rank_col % 2 == 1
    tile = TILE if units % TILE == 0 else units
    tiles = units // tile
    granule = gcd_of(units, BLK)
    core_swap = [(i, i ^ 1) for i in range(n_col)]

    def swap_cores(value):
        return lax.ppermute(value, "col", core_swap)

    def swap_chips(value):
        total = value.astype(F32)
        for d in range(1, n_chip):
            other = lax.ppermute(value, "col", [(i, (i + 2 * d) % n_col) for i in range(n_col)])
            total = total + other.astype(F32)
        return total

    def mine_first(value):
        blocks = value.reshape(-1, 2, half, value.shape[1])
        first = jnp.where(second_core, blocks[:, 1], blocks[:, 0])
        last = jnp.where(second_core, blocks[:, 0], blocks[:, 1])
        return jnp.concatenate([first, last], axis=0).reshape(value.shape)

    def shifted(value, d):
        return lax.ppermute(value, "row", [(i, (i + d) % n_row) for i in range(n_row)])

    def gather_others(value):
        if n_row <= 8:
            return jnp.concatenate([shifted(value, d) for d in range(1, n_row)], axis=0)
        whole = lax.all_gather(value, "row", axis=0, tiled=True)
        others = [lax.rem(rank_row - d + n_row, n_row) for d in range(1, n_row)]
        return jnp.concatenate([lax.dynamic_slice_in_dim(whole, o * own, own, 0) for o in others], axis=0)

    col_first, row_first = rank_col * feats, rank_row * units
    feat_index = block_index(col_first, feats // BLK, BLK)
    lane_index = block_index(col_first, feats, 1)
    unit_lanes = block_index(row_first, units, 1)
    unit_index = block_index(row_first, units // granule, granule)
    gk = pick(gate_mask, feat_index, unit_lanes)
    uk = pick(up_mask, feat_index, unit_lanes)
    dk = pick(down_mask, unit_index, lane_index).reshape(tiles, tile // granule, feats)

    weights = (gate_w, up_w, down_w, gk, uk, dk)

    def exchange(x, og, first, size):
        keep, send = forward(x, og, *weights, first, size, tile)
        chip_sum = (keep.astype(F32) + swap_cores(send).astype(F32)).astype(BF)
        mine = pointwise(swap_chips(chip_sum))
        return mine, swap_cores(mine)

    x_own, og_own = mine_first(tokens), mine_first(out_grad)
    x_far, og_far = mine_first(gather_others(tokens)), mine_first(gather_others(out_grad))

    own_chunks = chunks_of(tiles, (2, 5))
    far_chunks = chunks_of(tiles, (2, 2, 2, 1))
    own_parts = [exchange(x_own, og_own, first, size) for first, size in own_chunks]
    far_parts = [exchange(x_far, og_far, first, size) for first, size in far_chunks]

    x_all = jnp.concatenate([x_own, x_far], axis=0)
    og_all = jnp.concatenate([og_own, og_far], axis=0)
    xt_all = x_all.T
    grads = None
    gt = jnp.zeros((x_all.shape[0], feats), F32)
    for own_first, own_size in own_chunks:
        pass

    def parts_at(first):
        for (f, s), pair in zip(own_chunks, own_parts):
            if f <= first < f + s:
                own_pair, own_start = pair, f
        for (f, s), pair in zip(far_chunks, far_parts):
            if f <= first < f + s:
                far_pair, far_start = pair, f
        return (*own_pair, *far_pair), (own_start, own_start, far_start, far_start)

    bounds = sorted({f for f, _ in own_chunks} | {f for f, _ in far_chunks} | {tiles})
    for first, last in zip(bounds[:-1], bounds[1:]):
        parts, starts = parts_at(first)
        gt = grad_tokens_of(gt, gate_w, up_w, gk, uk, parts, starts, first, last - first, tile)
        grads = weight_grads(grads, xt_all, og_all, gk, uk, dk, parts, starts, first, last - first, tile, units)

    gt = gt.astype(BF)
    far = gt[own:].reshape(2, n_row - 1, half, feats)
    total = gt[:own].astype(F32)
    if n_row <= 8:
        for d in range(1, n_row):
            piece = far[:, d - 1].reshape(own, feats)
            total = total + lax.ppermute(piece, "row", [(i, (i - d) % n_row) for i in range(n_row)]).astype(F32)
        total = total.astype(BF)
    else:
        order = jnp.concatenate([gt[:own].reshape(2, 1, half, feats), far], axis=1)
        order = jnp.swapaxes(order, 0, 1).reshape(n_row, own, feats)
        wanted = [lax.rem(rank_row - b + n_row, n_row) for b in range(n_row)]
        by_row = jnp.concatenate([lax.dynamic_slice_in_dim(order, w, 1, 0) for w in wanted], axis=0)
        total = lax.psum_scatter(by_row.reshape(n_row * own, feats), "row", scatter_dimension=0, tiled=True)
    total = mine_first(total)
    return (total, *grads)


def solution(mesh):
    in_specs = (
        P(("groups", "row"), "col"),
        P(("groups", "row"), "col"),
        P(("groups", "col"), "row"),
        P(("groups", "col"), "row"),
        P(("groups", "row"), "col"),
        P("groups", None),
        P("groups", None),
        P("groups", None),
    )
    out_specs = (
        P(("groups", "row"), "col"),
        P(("groups", "col"), "row"),
        P(("groups", "col"), "row"),
        P(("groups", "row"), "col"),
    )
    step = functools.partial(local, mesh.shape["row"], mesh.shape["col"])
    return jax.shard_map(step, mesh=mesh, in_specs=in_specs, out_specs=out_specs, check_vma=False)
```

time: 210 us -> 118 us (0.56)
  matrix products: 70.2 us -> 3.39 us
  blocking collectives: 58.8 us -> 0 us
  Pallas kernels: 0 us -> 47 us
  starting transfers between devices: 0.08 us -> 24 us
  waiting for transfers between devices: 48.5 us -> 30.9 us
  between operations: 14.2 us -> 1.25 us
  other arithmetic: 15 us -> 4.01 us
  local copies, waits for them, and re-layouts: 2.77 us -> 6.66 us
    dot_general x11 -> x3, matrix products: 70.2 us -> 3.39 us  [pick(): return jnp.dot(part, cols, preferred_element_type=F32).astype(BF)]
    all_gather x5 -> x0, blocking collectives: 58.8 us -> none  [the longest x1 15.8 us: local(): lax.all_gather(tokens, 'row', axis=0, tiled=True)]
    reduce_scatter x2 -> x0, waiting for transfers between devices: 48.5 us -> none  [the longest x1 36.5 us: local(): lax.psum_scatter(jnp.concatenate([jnp.dot(tokens_all, gate_live, preferre...]
    pallas_call x0 -> x14, Pallas kernels: none -> 47 us  [the longest x6 23.1 us: forward(): pl.pallas_call(forward_kernel, out_shape=(out, out), grid=(tiles,), in_sp...]
    ppermute x0 -> x27, waiting for transfers between devices: none -> 30.9 us  [the longest x6 26.5 us: swap_chips(): lax.ppermute(value, 'col', [(i, (i + 2 * d) % n_col) for i in range(n_col)])]
    ppermute x0 -> x27, starting transfers between devices: none -> 24 us  [the longest x6 10.2 us: shifted(): lax.ppermute(value, 'row', [(i, (i + d) % n_row) for i in range(n_row)])]
    concatenate x1 -> x8, other arithmetic: 13.6 us -> 0.74 us  [the longest x5 0.7 us: mine_first(): return jnp.concatenate([first, last], axis=0).reshape(value.shape)]
    unnamed x19 -> x6, local copies, waits for them, and re-layouts: 2.77 us -> 6.21 us
  transfers between devices with their start and end apart: 2 -> 27, of which waited for: 2 -> 7; matrix products, arithmetic and copies ran while one was open for 4% -> 6% of each run, Pallas kernels for 0% -> 38%
where the time goes in v1:
time: 118 us; the launch traced here: 117 us
  Pallas kernels  47 us (40%)
  waiting for transfers between devices  30.9 us (26%)
  starting transfers between devices  24 us (20%)
  local copies, waits for them, and re-layouts  6.66 us (6%)
  other arithmetic  4.01 us (3%)
  matrix products  3.39 us (3%)
  between operations  1.25 us (1%)
    ppermute x6, waiting for transfers between devices, swap_chips(): lax.ppermute(value, 'col', [(i, (i + 2 * d) % n_col) for i in range(n_col)])  26.5 us
    pallas_call x6, Pallas kernels, forward(): pl.pallas_call(forward_kernel, out_shape=(out, out), grid=(tiles,), in_sp...  23.1 us
    pallas_call x4, Pallas kernels, weight_grads(): pl.pallas_call(functools.partial(weight_grads_kernel, len(parts), n_prev)...  12.7 us
    pallas_call x4, Pallas kernels, grad_tokens_of(): pl.pallas_call(functools.partial(grad_tokens_kernel, len(parts)), out_sha...  11.3 us
    ppermute x6, starting transfers between devices, shifted(): lax.ppermute(value, 'row', [(i, (i + d) % n_row) for i in range(n_row)])  10.2 us
    ppermute x6, starting transfers between devices, swap_chips(): lax.ppermute(value, 'col', [(i, (i + 2 * d) % n_col) for i in range(n_col)])  7.37 us
    unnamed x6, local copies, waits for them, and re-layouts  6.21 us
    ppermute x6, waiting for transfers between devices, shifted(): lax.ppermute(value, 'row', [(i, (i + d) % n_row) for i in range(n_row)])  4.42 us
  transfers between devices with their start and end apart: 27, of which 7 were waited for; matrix products, arithmetic and copies ran while one was open for 6% of the time, Pallas kernels for 38%

profile of v1, /device:TPU:0, one launch (start us, length us, event | category | flops | bytes accessed | tf_op | source)
XLA Modules:
  0.0 117.3 jit_solution(10941287146412643283)
XLA Ops:
  0.6 3.1 %collective-permute-start.3 = (bf16[32,1024]{1,0:T(8,128)(2,1)}, bf16[32,1024]{1,0:T(8,128)(2,1)S(1)}, u32[]{:S(2)}, u32[]{:S(2)}) collective-permute-start(bf16[32,1024]{1,0:T(8,128)(2,1)} %param.8), channel_id=1, source_target_pairs={{0,4},{4,8},{8,12},{12,0},{1,5},{5,9},{9,13},{13,1},{2,6},{6,10},{... | collective-permute-start | bytes 196616 | tf_op jit(solution)/shard_map/ppermute | solution.py:240
  3.7 2.1 %collective-permute-start.5 = (bf16[32,1024]{1,0:T(8,128)(2,1)}, bf16[32,1024]{1,0:T(8,128)(2,1)S(1)}, u32[]{:S(2)}, u32[]{:S(2)}) collective-permute-start(bf16[32,1024]{1,0:T(8,128)(2,1)} %param.8), channel_id=1, source_target_pairs={{0,12},{4,0},{8,4},{12,8},{1,13},{5,1},{9,5},{13,9},{2,14},{6,2},{... | collective-permute-start | bytes 196616 | tf_op jit(solution)/shard_map/ppermute | solution.py:240
  5.8 0.9 collective-permute-start.4
  6.7 1.6 %collective-permute-start.6 = (bf16[32,1024]{1,0:T(8,128)(2,1)}, bf16[32,1024]{1,0:T(8,128)(2,1)S(1)}, u32[]{:S(2)}, u32[]{:S(2)}) collective-permute-start(bf16[32,1024]{1,0:T(8,128)(2,1)} %param.9), channel_id=1, source_target_pairs={{0,4},{4,8},{8,12},{12,0},{1,5},{5,9},{9,13},{13,1},{2,6},{6,10},{... | collective-permute-start | bytes 196616 | tf_op jit(solution)/shard_map/ppermute | solution.py:240
  8.3 2.2 %collective-permute-start.8 = (bf16[32,1024]{1,0:T(8,128)(2,1)}, bf16[32,1024]{1,0:T(8,128)(2,1)S(1)}, u32[]{:S(2)}, u32[]{:S(2)}) collective-permute-start(bf16[32,1024]{1,0:T(8,128)(2,1)} %param.9), channel_id=1, source_target_pairs={{0,12},{4,0},{8,4},{12,8},{1,13},{5,1},{9,5},{13,9},{2,14},{6,2},{... | collective-permute-start | bytes 196616 | tf_op jit(solution)/shard_map/ppermute | solution.py:240
  10.7 1.2 %convolution_convert_fusion.uk_ref = bf16[8,3584]{1,0:T(8,128)(2,1)S(1)} fusion(s32[3584]{0:T(1024)S(1)} %add_select_fusion, s32[32,112]{1,0:T(8,128)} %param.14, s32[8]{0:T(128)S(1)} %and_select_fusion.1), kind=kOutput, calls=%fused_computation | convolution fusion | flops 6914688 | bytes 86048 | tf_op jit(solution)/shard_map/dot_general | solution.py:35
  11.8 1.2 %convolution_convert_fusion.1.gk_ref = bf16[8,3584]{1,0:T(8,128)(2,1)S(1)} fusion(s32[3584]{0:T(1024)S(1)} %add_select_fusion, s32[32,112]{1,0:T(8,128)} %param.13, s32[8]{0:T(128)S(1)} %and_select_fusion.1), kind=kOutput, calls=%fused_computation.1 | convolution fusion | flops 6914688 | bytes 86048 | tf_op jit(solution)/shard_map/dot_general | solution.py:35
  13.0 1.0 convolution_convert_fusion.2
  14.1 0.8 select_bitcast_fusion.5
  14.9 0.8 select_bitcast_fusion.7
  15.7 0.2 copy.41
  15.9 3.1 %copy-done = bf16[1024,3584]{1,0:T(8,128)(2,1)S(1)} copy-done((bf16[1024,3584]{1,0:T(8,128)(2,1)S(1)}, bf16[1024,3584]{1,0:T(8,128)(2,1)}, u32[]{:S(2)}) %copy-start) | copy-done | bytes 7340056
  19.0 3.3 %forward.6 = (bf16[3,16,1024]{2,1,0:T(8,128)(2,1)S(1)}, bf16[3,16,1024]{2,1,0:T(8,128)(2,1)S(1)}) custom-call(bf16[32,1024]{1,0:T(8,128)(2,1)S(1)} %bitcast.71, bf16[32,1024]{1,0:T(8,128)(2,1)S(1)} %bitcast.73, bf16[1024,3584]{1,0:T(8,128)(2,1)S(1)} %copy-done, bf16[1024,3584]{1,0:T(8,128)(2,1)} %up_ref.19, bf16[3584,1024]{1,0:T(8,128)(2,1)} %down_ref.11, ...), custom_call_target="tpu_custom_call" | custom-call | flops 201326592 | bytes 6422528 | tf_op jit(solution)/shard_map/forward/pallas_call | solution.py:69
  22.3 7.4 %forward.8 = (bf16[3,16,2560]{2,1,0:T(8,128)(2,1)S(1)}, bf16[3,16,2560]{2,1,0:T(8,128)(2,1)S(1)}) custom-call(bf16[32,1024]{1,0:T(8,128)(2,1)S(1)} %bitcast.72, bf16[32,1024]{1,0:T(8,128)(2,1)S(1)} %bitcast.74, bf16[1024,3584]{1,0:T(8,128)(2,1)S(1)} %copy-done, bf16[1024,3584]{1,0:T(8,128)(2,1)} %up_ref.19, bf16[3584,1024]{1,0:T(8,128)(2,1)} %down_ref.11, ...), custom_call_target="tpu_custom_call" | custom-call | flops 503316480 | bytes 15859712 | tf_op jit(solution)/shard_map/forward/pallas_call | solution.py:69
  29.7 0.2 collective-permute-start.7
  30.0 0.5 collective-permute-start.12
  30.5 4.4 %collective-permute-done.7 = bf16[32,1024]{1,0:T(8,128)(2,1)S(1)} collective-permute-done((bf16[32,1024]{1,0:T(8,128)(2,1)S(1)}, bf16[32,1024]{1,0:T(8,128)(2,1)S(1)}, u32[]{:S(2)}, u32[]{:S(2)}) %collective-permute-start.7) | collective-permute-done | bytes 65568 | tf_op jit(solution)/shard_map/ppermute | solution.py:240
  35.0 0.2 copy.42
  35.2 3.1 %copy-done.1 = bf16[1024,3584]{1,0:T(8,128)(2,1)S(1)} copy-done((bf16[1024,3584]{1,0:T(8,128)(2,1)S(1)}, bf16[1024,3584]{1,0:T(8,128)(2,1)}, u32[]{:S(2)}) %copy-start.1) | copy-done | bytes 7340056
  38.3 2.4 %forward.11 = (bf16[3,48,512]{2,1,0:T(8,128)(2,1)S(1)}, bf16[3,48,512]{2,1,0:T(8,128)(2,1)S(1)}) custom-call(bf16[96,1024]{1,0:T(8,128)(2,1)S(1)} %bitcast.66, bf16[96,1024]{1,0:T(8,128)(2,1)S(1)} %bitcast.60, bf16[1024,3584]{1,0:T(8,128)(2,1)S(1)} %copy-done.1, bf16[1024,3584]{1,0:T(8,128)(2,1)} %up_ref.19, bf16[3584,1024]{1,0:T(8,128)(2,1)} %down_ref.11, ...), custom_call_target="tpu_custom_call" | custom-call | flops 301989888 | bytes 3538944 | tf_op jit(solution)/shard_map/forward/pallas_call | solution.py:69
  40.7 3.3 %forward.10 = (bf16[3,48,1024]{2,1,0:T(8,128)(2,1)S(1)}, bf16[3,48,1024]{2,1,0:T(8,128)(2,1)S(1)}) custom-call(bf16[96,1024]{1,0:T(8,128)(2,1)S(1)} %bitcast.67, bf16[96,1024]{1,0:T(8,128)(2,1)S(1)} %bitcast.61, bf16[1024,3584]{1,0:T(8,128)(2,1)S(1)} %copy-done.1, bf16[1024,3584]{1,0:T(8,128)(2,1)} %up_ref.19, bf16[3584,1024]{1,0:T(8,128)(2,1)} %down_ref.11, ...), custom_call_target="tpu_custom_call" | custom-call | flops 603979776 | bytes 6684672 | tf_op jit(solution)/shard_map/forward/pallas_call | solution.py:69
  44.1 3.3 %forward.9 = (bf16[3,48,1024]{2,1,0:T(8,128)(2,1)S(1)}, bf16[3,48,1024]{2,1,0:T(8,128)(2,1)S(1)}) custom-call(bf16[96,1024]{1,0:T(8,128)(2,1)S(1)} %bitcast.68, bf16[96,1024]{1,0:T(8,128)(2,1)S(1)} %bitcast.62, bf16[1024,3584]{1,0:T(8,128)(2,1)S(1)} %copy-done.1, bf16[1024,3584]{1,0:T(8,128)(2,1)} %up_ref.19, bf16[3584,1024]{1,0:T(8,128)(2,1)} %down_ref.11, ...), custom_call_target="tpu_custom_call" | custom-call | flops 603979776 | bytes 6684672 | tf_op jit(solution)/shard_map/forward/pallas_call | solution.py:69
  47.4 3.3 %forward.7 = (bf16[3,48,1024]{2,1,0:T(8,128)(2,1)S(1)}, bf16[3,48,1024]{2,1,0:T(8,128)(2,1)S(1)}) custom-call(bf16[96,1024]{1,0:T(8,128)(2,1)S(1)} %bitcast.69, bf16[96,1024]{1,0:T(8,128)(2,1)S(1)} %bitcast.63, bf16[1024,3584]{1,0:T(8,128)(2,1)S(1)} %copy-done.1, bf16[1024,3584]{1,0:T(8,128)(2,1)} %up_ref.19, bf16[3584,1024]{1,0:T(8,128)(2,1)} %down_ref.11, ...), custom_call_target="tpu_custom_call" | custom-call | flops 603979776 | bytes 6684672 | tf_op jit(solution)/shard_map/forward/pallas_call | solution.py:69
  50.8 0.5 collective-permute-start.18
  51.5 1.6 %collective-permute-start.1 = (bf16[3,16,1024]{2,1,0:T(8,128)(2,1)S(1)}, bf16[3,16,1024]{2,1,0:T(8,128)(2,1)S(1)}, u32[]{:S(2)}, u32[]{:S(2)}) collective-permute-start(bf16[3,16,1024]{2,1,0:T(8,128)(2,1)S(1)} %add_convert_fusion.5), channel_id=1, source_target_pairs={{0,2},{1,3},{2,0},{3,1},{4,6},{5,7},{6,4},{7,5},{8,10},{9,11},{10,... | collective-permute-start | bytes 294920 | tf_op jit(solution)/shard_map/ppermute | solution.py:229
  53.2 3.5 %collective-permute-done.1 = bf16[3,16,1024]{2,1,0:T(8,128)(2,1)S(1)} collective-permute-done((bf16[3,16,1024]{2,1,0:T(8,128)(2,1)S(1)}, bf16[3,16,1024]{2,1,0:T(8,128)(2,1)S(1)}, u32[]{:S(2)}, u32[]{:S(2)}) %collective-permute-start.1) | collective-permute-done | bytes 98336 | tf_op jit(solution)/shard_map/ppermute | solution.py:229
  56.8 0.6 collective-permute-start.2
  57.4 1.6 %collective-permute-start.22 = (bf16[3,48,512]{2,1,0:T(8,128)(2,1)S(1)}, bf16[3,48,512]{2,1,0:T(8,128)(2,1)S(1)}, u32[]{:S(2)}, u32[]{:S(2)}) collective-permute-start(bf16[3,48,512]{2,1,0:T(8,128)(2,1)S(1)} %add_convert_fusion.4), channel_id=1, source_target_pairs={{0,2},{1,3},{2,0},{3,1},{4,6},{5,7},{6,4},{7,5},{8,10},{9,11},{10,... | collective-permute-start | bytes 442376 | tf_op jit(solution)/shard_map/ppermute | solution.py:229
  59.1 0.6 collective-permute-start.13
  59.8 1.6 %collective-permute-start.19 = (bf16[3,48,1024]{2,1,0:T(8,128)(2,1)S(1)}, bf16[3,48,1024]{2,1,0:T(8,128)(2,1)S(1)}, u32[]{:S(2)}, u32[]{:S(2)}) collective-permute-start(bf16[3,48,1024]{2,1,0:T(8,128)(2,1)S(1)} %add_convert_fusion), channel_id=1, source_target_pairs={{0,2},{1,3},{2,0},{3,1},{4,6},{5,7},{6,4},{7,5},{8,10},{9,11},{10,... | collective-permute-start | bytes 884744 | tf_op jit(solution)/shard_map/ppermute | solution.py:229
  61.4 0.6 collective-permute-start.10
  62.1 2.1 %collective-permute-done.22 = bf16[3,48,512]{2,1,0:T(8,128)(2,1)S(1)} collective-permute-done((bf16[3,48,512]{2,1,0:T(8,128)(2,1)S(1)}, bf16[3,48,512]{2,1,0:T(8,128)(2,1)S(1)}, u32[]{:S(2)}, u32[]{:S(2)}) %collective-permute-start.22) | collective-permute-done | bytes 147488 | tf_op jit(solution)/shard_map/ppermute | solution.py:229
  64.2 1.5 %collective-permute-start.16 = (bf16[3,48,1024]{2,1,0:T(8,128)(2,1)S(1)}, bf16[3,48,1024]{2,1,0:T(8,128)(2,1)S(1)}, u32[]{:S(2)}, u32[]{:S(2)}) collective-permute-start(bf16[3,48,1024]{2,1,0:T(8,128)(2,1)S(1)} %add_convert_fusion.1), channel_id=1, source_target_pairs={{0,2},{1,3},{2,0},{3,1},{4,6},{5,7},{6,4},{7,5},{8,10},{9,11},{10,... | collective-permute-start | bytes 884744 | tf_op jit(solution)/shard_map/ppermute | solution.py:229
  65.8 3.7 %collective-permute-done.13 = bf16[3,16,2560]{2,1,0:T(8,128)(2,1)S(1)} collective-permute-done((bf16[3,16,2560]{2,1,0:T(8,128)(2,1)S(1)}, bf16[3,16,2560]{2,1,0:T(8,128)(2,1)S(1)}, u32[]{:S(2)}, u32[]{:S(2)}) %collective-permute-start.13) | collective-permute-done | bytes 245792 | tf_op jit(solution)/shard_map/ppermute | solution.py:229
  69.8 6.0 %collective-permute-done.19 = bf16[3,48,1024]{2,1,0:T(8,128)(2,1)S(1)} collective-permute-done((bf16[3,48,1024]{2,1,0:T(8,128)(2,1)S(1)}, bf16[3,48,1024]{2,1,0:T(8,128)(2,1)S(1)}, u32[]{:S(2)}, u32[]{:S(2)}) %collective-permute-start.19) | collective-permute-done | bytes 294944 | tf_op jit(solution)/shard_map/ppermute | solution.py:229
  76.1 6.0 %collective-permute-done.10 = bf16[3,48,1024]{2,1,0:T(8,128)(2,1)S(1)} collective-permute-done((bf16[3,48,1024]{2,1,0:T(8,128)(2,1)S(1)}, bf16[3,48,1024]{2,1,0:T(8,128)(2,1)S(1)}, u32[]{:S(2)}, u32[]{:S(2)}) %collective-permute-start.10) | collective-permute-done | bytes 294944 | tf_op jit(solution)/shard_map/ppermute | solution.py:229
  82.4 5.1 %collective-permute-done.16 = bf16[3,48,1024]{2,1,0:T(8,128)(2,1)S(1)} collective-permute-done((bf16[3,48,1024]{2,1,0:T(8,128)(2,1)S(1)}, bf16[3,48,1024]{2,1,0:T(8,128)(2,1)S(1)}, u32[]{:S(2)}, u32[]{:S(2)}) %collective-permute-start.16) | collective-permute-done | bytes 294944 | tf_op jit(solution)/shard_map/ppermute | solution.py:229
  87.9 0.6 collective-permute-start.23
  88.5 3.0 %grad_tokens.4.prev_ref = f32[128,1024]{1,0:T(8,128)S(1)} custom-call(f32[128,1024]{1,0:T(8,128)S(1)} %broadcast_in_dim.2.prev_ref, bf16[1024,3584]{1,0:T(8,128)(2,1)S(1)} %copy-done.1, bf16[1024,3584]{1,0:T(8,128)(2,1)} %up_ref.19, bf16[8,3584]{1,0:T(8,128)(2,1)S(1)} %convolution_convert_fusion.1.gk_ref, ...), custom_call_target="tpu_custom_call" | custom-call | flops 536870912 | bytes 5242880 | tf_op jit(solution)/shard_map/grad_tokens/pallas_call | solution.py:109
  91.6 3.1 %grad_tokens.5.prev_ref = f32[128,1024]{1,0:T(8,128)S(1)} custom-call(f32[128,1024]{1,0:T(8,128)S(1)} %grad_tokens.4.prev_ref, bf16[1024,3584]{1,0:T(8,128)(2,1)S(1)} %copy-done.1, bf16[1024,3584]{1,0:T(8,128)(2,1)} %up_ref.19, bf16[8,3584]{1,0:T(8,128)(2,1)S(1)} %convolution_convert_fusion.1.gk_ref, bf16[8,3584]{1,0:T(8,128)(2,1)S(1)} %convolution_convert_fusion.uk_ref, ...), custom_call_target="tpu_custom_call" | custom-call | flops 536870912 | bytes 5242880 | tf_op jit(solution)/shard_map/grad_tokens/pallas_call | solution.py:109
  94.7 3.1 %grad_tokens.6.prev_ref = f32[128,1024]{1,0:T(8,128)S(1)} custom-call(f32[128,1024]{1,0:T(8,128)S(1)} %grad_tokens.5.prev_ref, bf16[1024,3584]{1,0:T(8,128)(2,1)S(1)} %copy-done.1, bf16[1024,3584]{1,0:T(8,128)(2,1)} %up_ref.19, bf16[8,3584]{1,0:T(8,128)(2,1)S(1)} %convolution_convert_fusion.1.gk_ref, bf16[8,3584]{1,0:T(8,128)(2,1)S(1)} %convolution_convert_fusion.uk_ref, ...), custom_call_target="tpu_custom_call" | custom-call | flops 536870912 | bytes 5242880 | tf_op jit(solution)/shard_map/grad_tokens/pallas_call | solution.py:109
  97.8 2.1 %grad_tokens.7 = f32[128,1024]{1,0:T(8,128)S(1)} custom-call(f32[128,1024]{1,0:T(8,128)S(1)} %grad_tokens.6.prev_ref, bf16[1024,3584]{1,0:T(8,128)(2,1)S(1)} %copy-done.1, bf16[1024,3584]{1,0:T(8,128)(2,1)} %up_ref.19, bf16[8,3584]{1,0:T(8,128)(2,1)S(1)} %convolution_convert_fusion.1.gk_ref, bf16[8,3584]{1,0:T(8,128)(2,1)S(1)} %convolution_convert_fusion.uk_ref, ...), custom_call_target="tpu_custom_call" | custom-call | flops 268435456 | bytes 3145728 | tf_op jit(solution)/shard_map/grad_tokens/pallas_call | solution.py:109
  100.1 3.8 %collective-permute-start.24 = (bf16[32,1024]{1,0:T(8,128)(2,1)S(1)}, bf16[32,1024]{1,0:T(8,128)(2,1)S(1)}, u32[]{:S(2)}, u32[]{:S(2)}) collective-permute-start(bf16[32,1024]{1,0:T(8,128)(2,1)S(1)} %bitcast.85), channel_id=1, source_target_pairs={{0,12},{4,0},{8,4},{12,8},{1,13},{5,1},{9,5},{13,9},{2,14},{6,2},{... | collective-permute-start | bytes 196616 | tf_op jit(solution)/shard_map/ppermute | solution.py:303
  103.9 3.6 %weight_grads.4 = (bf16[1024,3584]{1,0:T(8,128)(2,1)}, bf16[1024,3584]{1,0:T(8,128)(2,1)}, bf16[3584,1024]{1,0:T(8,128)(2,1)}) custom-call(bf16[1024,128]{1,0:T(8,128)(2,1)S(1)} %maximum_bitcast_fusion.xt_ref, bf16[128,1024]{1,0:T(8,128)(2,1)S(1)} %pad_maximum_fusion.3.og_ref, bf16[8,3584]{1,0:T(8,128)(2,1)S(1)} %convolution_convert_fusion.1.gk_ref, ...), custom_call_target="tpu_custom_call" | custom-call | flops 805306368 | bytes 6815744 | tf_op jit(solution)/shard_map/weight_grads/pallas_call | solution.py:153
  107.5 3.5 %weight_grads.5 = (bf16[1024,3584]{1,0:T(8,128)(2,1)}, bf16[1024,3584]{1,0:T(8,128)(2,1)}, bf16[3584,1024]{1,0:T(8,128)(2,1)}) custom-call(bf16[1024,128]{1,0:T(8,128)(2,1)S(1)} %maximum_bitcast_fusion.xt_ref, bf16[128,1024]{1,0:T(8,128)(2,1)S(1)} %pad_maximum_fusion.3.og_ref, ...), custom_call_target="tpu_custom_call", output_to_operand_aliasing={{0}: (9, {}), {1}: (10, {}), {2}: (11, {})} | custom-call | flops 805306368 | bytes 6815744 | tf_op jit(solution)/shard_map/weight_grads/pallas_call | solution.py:153
  110.9 3.5 %weight_grads.6 = (bf16[1024,3584]{1,0:T(8,128)(2,1)}, bf16[1024,3584]{1,0:T(8,128)(2,1)}, bf16[3584,1024]{1,0:T(8,128)(2,1)}) custom-call(bf16[1024,128]{1,0:T(8,128)(2,1)S(1)} %maximum_bitcast_fusion.xt_ref, bf16[128,1024]{1,0:T(8,128)(2,1)S(1)} %pad_maximum_fusion.3.og_ref, ...), custom_call_target="tpu_custom_call", output_to_operand_aliasing={{0}: (9, {}), {1}: (10, {}), {2}: (11, {})} | custom-call | flops 805306368 | bytes 6815744 | tf_op jit(solution)/shard_map/weight_grads/pallas_call | solution.py:153
  114.4 2.1 %weight_grads.7 = (bf16[1024,3584]{1,0:T(8,128)(2,1)}, bf16[1024,3584]{1,0:T(8,128)(2,1)}, bf16[3584,1024]{1,0:T(8,128)(2,1)}) custom-call(bf16[1024,128]{1,0:T(8,128)(2,1)S(1)} %maximum_bitcast_fusion.xt_ref, bf16[128,1024]{1,0:T(8,128)(2,1)S(1)} %pad_maximum_fusion.3.og_ref, ...), custom_call_target="tpu_custom_call", output_to_operand_aliasing={{0}: (9, {}), {1}: (10, {}), {2}: (11, {})} | custom-call | flops 402653184 | bytes 3670016 | tf_op jit(solution)/shard_map/weight_grads/pallas_call | solution.py:153
  116.6 0.6 pad_maximum_fusion.13
  (79 shorter events, 2.5 us)
Async XLA Ops:
  0.6 29.1 %collective-permute-start.3 = (bf16[32,1024]{1,0:T(8,128)(2,1)}, bf16[32,1024]{1,0:T(8,128)(2,1)S(1)}, u32[]{:S(2)}, u32[]{:S(2)}) collective-permute-start(bf16[32,1024]{1,0:T(8,128)(2,1)} %param.8), channel_id=1, source_target_pairs={{0,4},{4,8},{8,12},{12,0},{1,5},{5,9},{9,13},{13,1},{2,6},{6,10},{... | collective-permute-start | bytes 196616 | tf_op jit(solution)/shard_map/ppermute | solution.py:240
  3.7 26.2 %collective-permute-start.5 = (bf16[32,1024]{1,0:T(8,128)(2,1)}, bf16[32,1024]{1,0:T(8,128)(2,1)S(1)}, u32[]{:S(2)}, u32[]{:S(2)}) collective-permute-start(bf16[32,1024]{1,0:T(8,128)(2,1)} %param.8), channel_id=1, source_target_pairs={{0,12},{4,0},{8,4},{12,8},{1,13},{5,1},{9,5},{13,9},{2,14},{6,2},{... | collective-permute-start | bytes 196616 | tf_op jit(solution)/shard_map/ppermute | solution.py:240
  5.8 24.2 %collective-permute-start.4 = (bf16[32,1024]{1,0:T(8,128)(2,1)}, bf16[32,1024]{1,0:T(8,128)(2,1)S(1)}, u32[]{:S(2)}, u32[]{:S(2)}) collective-permute-start(bf16[32,1024]{1,0:T(8,128)(2,1)} %param.8), channel_id=1, source_target_pairs={{0,8},{4,12},{8,0},{12,4},{1,9},{5,13},{9,1},{13,5},{2,10},{6,14},... | collective-permute-start | bytes 196616 | tf_op jit(solution)/shard_map/ppermute | solution.py:240
  6.7 23.8 %collective-permute-start.6 = (bf16[32,1024]{1,0:T(8,128)(2,1)}, bf16[32,1024]{1,0:T(8,128)(2,1)S(1)}, u32[]{:S(2)}, u32[]{:S(2)}) collective-permute-start(bf16[32,1024]{1,0:T(8,128)(2,1)} %param.9), channel_id=1, source_target_pairs={{0,4},{4,8},{8,12},{12,0},{1,5},{5,9},{9,13},{13,1},{2,6},{6,10},{... | collective-permute-start | bytes 196616 | tf_op jit(solution)/shard_map/ppermute | solution.py:240
  8.3 22.2 %collective-permute-start.8 = (bf16[32,1024]{1,0:T(8,128)(2,1)}, bf16[32,1024]{1,0:T(8,128)(2,1)S(1)}, u32[]{:S(2)}, u32[]{:S(2)}) collective-permute-start(bf16[32,1024]{1,0:T(8,128)(2,1)} %param.9), channel_id=1, source_target_pairs={{0,12},{4,0},{8,4},{12,8},{1,13},{5,1},{9,5},{13,9},{2,14},{6,2},{... | collective-permute-start | bytes 196616 | tf_op jit(solution)/shard_map/ppermute | solution.py:240
  15.9 3.1 %copy-start = (bf16[1024,3584]{1,0:T(8,128)(2,1)S(1)}, bf16[1024,3584]{1,0:T(8,128)(2,1)}, u32[]{:S(2)}) copy-start(bf16[1024,3584]{1,0:T(8,128)(2,1)} %gate_ref.19) | copy-start | bytes 22020100
  22.3 7.4 %copy-start.2 = (bf16[32,1024]{1,0:T(8,128)(2,1)S(1)}, bf16[32,1024]{1,0:T(8,128)(2,1)}, u32[]{:S(2)}) copy-start(bf16[32,1024]{1,0:T(8,128)(2,1)} %param.9) | copy-start | bytes 196612
  29.7 5.2 %collective-permute-start.7 = (bf16[32,1024]{1,0:T(8,128)(2,1)S(1)}, bf16[32,1024]{1,0:T(8,128)(2,1)S(1)}, u32[]{:S(2)}, u32[]{:S(2)}) collective-permute-start(bf16[32,1024]{1,0:T(8,128)(2,1)S(1)} %copy-done.2), channel_id=1, source_target_pairs={{0,8},{4,12},{8,0},{12,4},{1,9},{5,13},{9,1},{13,5},{2,10},{6,14},... | collective-permute-start | bytes 196616 | tf_op jit(solution)/shard_map/ppermute | solution.py:240
  30.0 21.5 %collective-permute-start = (bf16[3,16,1024]{2,1,0:T(8,128)(2,1)S(1)}, bf16[3,16,1024]{2,1,0:T(8,128)(2,1)S(1)}, u32[]{:S(2)}, u32[]{:S(2)}) collective-permute-start(bf16[3,16,1024]{2,1,0:T(8,128)(2,1)S(1)} %get-tuple-element.29), channel_id=1, source_target_pairs={{0,1},{1,0},{2,3},{3,2},{4,5},{5,4},{6,7},{7,6},{8,9},{9,8},{10,11... | collective-permute-start | bytes 294920 | tf_op jit(solution)/shard_map/ppermute | solution.py:224
  30.0 27.5 %collective-permute-start.12 = (bf16[3,16,2560]{2,1,0:T(8,128)(2,1)S(1)}, bf16[3,16,2560]{2,1,0:T(8,128)(2,1)S(1)}, u32[]{:S(2)}, u32[]{:S(2)}) collective-permute-start(bf16[3,16,2560]{2,1,0:T(8,128)(2,1)S(1)} %get-tuple-element.33), channel_id=1, source_target_pairs={{0,1},{1,0},{2,3},{3,2},{4,5},{5,4},{6,7},{7,6},{8,9},{9,8},{10,11... | collective-permute-start | bytes 737288 | tf_op jit(solution)/shard_map/ppermute | solution.py:224
  35.2 3.1 %copy-start.1 = (bf16[1024,3584]{1,0:T(8,128)(2,1)S(1)}, bf16[1024,3584]{1,0:T(8,128)(2,1)}, u32[]{:S(2)}) copy-start(bf16[1024,3584]{1,0:T(8,128)(2,1)} %gate_ref.19) | copy-start | bytes 22020100
  50.8 6.0 %collective-permute-start.21 = (bf16[3,48,512]{2,1,0:T(8,128)(2,1)S(1)}, bf16[3,48,512]{2,1,0:T(8,128)(2,1)S(1)}, u32[]{:S(2)}, u32[]{:S(2)}) collective-permute-start(bf16[3,48,512]{2,1,0:T(8,128)(2,1)S(1)} %get-tuple-element.39), channel_id=1, source_target_pairs={{0,1},{1,0},{2,3},{3,2},{4,5},{5,4},{6,7},{7,6},{8,9},{9,8},{10,11... | collective-permute-start | bytes 442376 | tf_op jit(solution)/shard_map/ppermute | solution.py:224
  50.8 8.2 %collective-permute-start.18 = (bf16[3,48,1024]{2,1,0:T(8,128)(2,1)S(1)}, bf16[3,48,1024]{2,1,0:T(8,128)(2,1)S(1)}, u32[]{:S(2)}, u32[]{:S(2)}) collective-permute-start(bf16[3,48,1024]{2,1,0:T(8,128)(2,1)S(1)} %get-tuple-element.37), channel_id=1, source_target_pairs={{0,1},{1,0},{2,3},{3,2},{4,5},{5,4},{6,7},{7,6},{8,9},{9,8},{10,11... | collective-permute-start | bytes 884744 | tf_op jit(solution)/shard_map/ppermute | solution.py:224
  51.3 8.4 %collective-permute-start.9 = (bf16[3,48,1024]{2,1,0:T(8,128)(2,1)S(1)}, bf16[3,48,1024]{2,1,0:T(8,128)(2,1)S(1)}, u32[]{:S(2)}, u32[]{:S(2)}) collective-permute-start(bf16[3,48,1024]{2,1,0:T(8,128)(2,1)S(1)} %get-tuple-element.31), channel_id=1, source_target_pairs={{0,1},{1,0},{2,3},{3,2},{4,5},{5,4},{6,7},{7,6},{8,9},{9,8},{10,11... | collective-permute-start | bytes 884744 | tf_op jit(solution)/shard_map/ppermute | solution.py:224
  51.5 5.2 %collective-permute-start.1 = (bf16[3,16,1024]{2,1,0:T(8,128)(2,1)S(1)}, bf16[3,16,1024]{2,1,0:T(8,128)(2,1)S(1)}, u32[]{:S(2)}, u32[]{:S(2)}) collective-permute-start(bf16[3,16,1024]{2,1,0:T(8,128)(2,1)S(1)} %add_convert_fusion.5), channel_id=1, source_target_pairs={{0,2},{1,3},{2,0},{3,1},{4,6},{5,7},{6,4},{7,5},{8,10},{9,11},{10,... | collective-permute-start | bytes 294920 | tf_op jit(solution)/shard_map/ppermute | solution.py:229
  56.7 4.7 %collective-permute-start.15 = (bf16[3,48,1024]{2,1,0:T(8,128)(2,1)S(1)}, bf16[3,48,1024]{2,1,0:T(8,128)(2,1)S(1)}, u32[]{:S(2)}, u32[]{:S(2)}) collective-permute-start(bf16[3,48,1024]{2,1,0:T(8,128)(2,1)S(1)} %get-tuple-element.35), channel_id=1, source_target_pairs={{0,1},{1,0},{2,3},{3,2},{4,5},{5,4},{6,7},{7,6},{8,9},{9,8},{10,11... | collective-permute-start | bytes 884744 | tf_op jit(solution)/shard_map/ppermute | solution.py:224
  56.8 31.1 %collective-permute-start.2 = (bf16[3,16,1024]{2,1,0:T(8,128)(2,1)S(1)}, bf16[3,16,1024]{2,1,0:T(8,128)(2,1)S(1)}, u32[]{:S(2)}, u32[]{:S(2)}) collective-permute-start(bf16[3,16,1024]{2,1,0:T(8,128)(2,1)S(1)} %pad_maximum_fusion.10.rest_0_), channel_id=1, source_target_pairs={{0,1},{1,0},{2,3},{3,2},{4,5},{5,4},{6,7},{7,6},{8,9},{9,8},{10,11... | collective-permute-start | bytes 294920 | tf_op jit(solution)/shard_map/ppermute | solution.py:224
  57.4 6.8 %collective-permute-start.22 = (bf16[3,48,512]{2,1,0:T(8,128)(2,1)S(1)}, bf16[3,48,512]{2,1,0:T(8,128)(2,1)S(1)}, u32[]{:S(2)}, u32[]{:S(2)}) collective-permute-start(bf16[3,48,512]{2,1,0:T(8,128)(2,1)S(1)} %add_convert_fusion.4), channel_id=1, source_target_pairs={{0,2},{1,3},{2,0},{3,1},{4,6},{5,7},{6,4},{7,5},{8,10},{9,11},{10,... | collective-permute-start | bytes 442376 | tf_op jit(solution)/shard_map/ppermute | solution.py:229
  59.1 10.4 %collective-permute-start.13 = (bf16[3,16,2560]{2,1,0:T(8,128)(2,1)S(1)}, bf16[3,16,2560]{2,1,0:T(8,128)(2,1)S(1)}, u32[]{:S(2)}, u32[]{:S(2)}) collective-permute-start(bf16[3,16,2560]{2,1,0:T(8,128)(2,1)S(1)} %add_convert_fusion.3), channel_id=1, source_target_pairs={{0,2},{1,3},{2,0},{3,1},{4,6},{5,7},{6,4},{7,5},{8,10},{9,11},{10,... | collective-permute-start | bytes 737288 | tf_op jit(solution)/shard_map/ppermute | solution.py:229
  59.8 16.0 %collective-permute-start.19 = (bf16[3,48,1024]{2,1,0:T(8,128)(2,1)S(1)}, bf16[3,48,1024]{2,1,0:T(8,128)(2,1)S(1)}, u32[]{:S(2)}, u32[]{:S(2)}) collective-permute-start(bf16[3,48,1024]{2,1,0:T(8,128)(2,1)S(1)} %add_convert_fusion), channel_id=1, source_target_pairs={{0,2},{1,3},{2,0},{3,1},{4,6},{5,7},{6,4},{7,5},{8,10},{9,11},{10,... | collective-permute-start | bytes 884744 | tf_op jit(solution)/shard_map/ppermute | solution.py:229
  61.4 20.7 %collective-permute-start.10 = (bf16[3,48,1024]{2,1,0:T(8,128)(2,1)S(1)}, bf16[3,48,1024]{2,1,0:T(8,128)(2,1)S(1)}, u32[]{:S(2)}, u32[]{:S(2)}) collective-permute-start(bf16[3,48,1024]{2,1,0:T(8,128)(2,1)S(1)} %add_convert_fusion.2), channel_id=1, source_target_pairs={{0,2},{1,3},{2,0},{3,1},{4,6},{5,7},{6,4},{7,5},{8,10},{9,11},{10,... | collective-permute-start | bytes 884744 | tf_op jit(solution)/shard_map/ppermute | solution.py:229
  64.2 23.3 %collective-permute-start.16 = (bf16[3,48,1024]{2,1,0:T(8,128)(2,1)S(1)}, bf16[3,48,1024]{2,1,0:T(8,128)(2,1)S(1)}, u32[]{:S(2)}, u32[]{:S(2)}) collective-permute-start(bf16[3,48,1024]{2,1,0:T(8,128)(2,1)S(1)} %add_convert_fusion.1), channel_id=1, source_target_pairs={{0,2},{1,3},{2,0},{3,1},{4,6},{5,7},{6,4},{7,5},{8,10},{9,11},{10,... | collective-permute-start | bytes 884744 | tf_op jit(solution)/shard_map/ppermute | solution.py:229
  69.7 21.9 %collective-permute-start.14 = (bf16[3,16,2560]{2,1,0:T(8,128)(2,1)S(1)}, bf16[3,16,2560]{2,1,0:T(8,128)(2,1)S(1)}, u32[]{:S(2)}, u32[]{:S(2)}) collective-permute-start(bf16[3,16,2560]{2,1,0:T(8,128)(2,1)S(1)} %pad_maximum_fusion.4.rest_0_), channel_id=1, source_target_pairs={{0,1},{1,0},{2,3},{3,2},{4,5},{5,4},{6,7},{7,6},{8,9},{9,8},{10,11... | collective-permute-start | bytes 737288 | tf_op jit(solution)/shard_map/ppermute | solution.py:224
  76.0 18.6 %collective-permute-start.20 = (bf16[3,48,1024]{2,1,0:T(8,128)(2,1)S(1)}, bf16[3,48,1024]{2,1,0:T(8,128)(2,1)S(1)}, u32[]{:S(2)}, u32[]{:S(2)}) collective-permute-start(bf16[3,48,1024]{2,1,0:T(8,128)(2,1)S(1)} %pad_maximum_fusion.2.rest_2_), channel_id=1, source_target_pairs={{0,1},{1,0},{2,3},{3,2},{4,5},{5,4},{6,7},{7,6},{8,9},{9,8},{10,11... | collective-permute-start | bytes 884744 | tf_op jit(solution)/shard_map/ppermute | solution.py:224
  82.4 6.1 %collective-permute-start.11 = (bf16[3,48,1024]{2,1,0:T(8,128)(2,1)S(1)}, bf16[3,48,1024]{2,1,0:T(8,128)(2,1)S(1)}, u32[]{:S(2)}, u32[]{:S(2)}) collective-permute-start(bf16[3,48,1024]{2,1,0:T(8,128)(2,1)S(1)} %pad_maximum_fusion.rest_2_), channel_id=1, source_target_pairs={{0,1},{1,0},{2,3},{3,2},{4,5},{5,4},{6,7},{7,6},{8,9},{9,8},{10,11... | collective-permute-start | bytes 884744 | tf_op jit(solution)/shard_map/ppermute | solution.py:224
  87.7 3.9 %collective-permute-start.17 = (bf16[3,48,1024]{2,1,0:T(8,128)(2,1)S(1)}, bf16[3,48,1024]{2,1,0:T(8,128)(2,1)S(1)}, u32[]{:S(2)}, u32[]{:S(2)}) collective-permute-start(bf16[3,48,1024]{2,1,0:T(8,128)(2,1)S(1)} %pad_maximum_fusion.1.rest_2_), channel_id=1, source_target_pairs={{0,1},{1,0},{2,3},{3,2},{4,5},{5,4},{6,7},{7,6},{8,9},{9,8},{10,11... | collective-permute-start | bytes 884744 | tf_op jit(solution)/shard_map/ppermute | solution.py:224
  87.9 9.9 %collective-permute-start.23 = (bf16[3,48,512]{2,1,0:T(8,128)(2,1)S(1)}, bf16[3,48,512]{2,1,0:T(8,128)(2,1)S(1)}, u32[]{:S(2)}, u32[]{:S(2)}) collective-permute-start(bf16[3,48,512]{2,1,0:T(8,128)(2,1)S(1)} %pad_maximum_fusion.9.rest_2_), channel_id=1, source_target_pairs={{0,1},{1,0},{2,3},{3,2},{4,5},{5,4},{6,7},{7,6},{8,9},{9,8},{10,11... | collective-permute-start | bytes 442376 | tf_op jit(solution)/shard_map/ppermute | solution.py:224
  100.0 16.5 %collective-permute-start.26 = (bf16[32,1024]{1,0:T(8,128)(2,1)S(1)}, bf16[32,1024]{1,0:T(8,128)(2,1)S(1)}, u32[]{:S(2)}, u32[]{:S(2)}) collective-permute-start(bf16[32,1024]{1,0:T(8,128)(2,1)S(1)} %bitcast.86), channel_id=1, source_target_pairs={{0,4},{4,8},{8,12},{12,0},{1,5},{5,9},{9,13},{13,1},{2,6},{6,10},{... | collective-permute-start | bytes 196616 | tf_op jit(solution)/shard_map/ppermute | solution.py:303
  100.1 16.5 %collective-permute-start.24 = (bf16[32,1024]{1,0:T(8,128)(2,1)S(1)}, bf16[32,1024]{1,0:T(8,128)(2,1)S(1)}, u32[]{:S(2)}, u32[]{:S(2)}) collective-permute-start(bf16[32,1024]{1,0:T(8,128)(2,1)S(1)} %bitcast.85), channel_id=1, source_target_pairs={{0,12},{4,0},{8,4},{12,8},{1,13},{5,1},{9,5},{13,9},{2,14},{6,2},{... | collective-permute-start | bytes 196616 | tf_op jit(solution)/shard_map/ppermute | solution.py:303
  103.9 12.7 %collective-permute-start.25 = (bf16[32,1024]{1,0:T(8,128)(2,1)S(1)}, bf16[32,1024]{1,0:T(8,128)(2,1)S(1)}, u32[]{:S(2)}, u32[]{:S(2)}) collective-permute-start(bf16[32,1024]{1,0:T(8,128)(2,1)S(1)} %bitcast.84), channel_id=1, source_target_pairs={{0,8},{4,12},{8,0},{12,4},{1,9},{5,13},{9,1},{13,5},{2,10},{6,14},... | collective-permute-start | bytes 196616 | tf_op jit(solution)/shard_map/ppermute | solution.py:303

commit v2 on v0

v2 whole, which is shorter than its diff:
```python
import functools

import jax
import jax.numpy as jnp
from jax import lax
from jax.experimental import pallas as pl
from jax.experimental.pallas import tpu as pltpu
from jax.sharding import PartitionSpec as P

BLK = 128
TILE = 512
COST_SCALE = 1000000000
OWN_CHUNKS = (7,)
FAR_CHUNKS = (2, 2, 2, 1)
BF = jnp.bfloat16
F32 = jnp.float32
ANY = pl.BlockSpec(memory_space=pl.ANY)
VMEM = pl.BlockSpec(memory_space=pltpu.VMEM)
SMEM = pl.BlockSpec(memory_space=pltpu.SMEM)


def params(mib=8):
    return pltpu.CompilerParams(vmem_limit_bytes=mib * 1024 * 1024)


def cost(flops, nbytes):
    return pl.CostEstimate(flops=int(flops) // COST_SCALE, bytes_accessed=int(nbytes) // COST_SCALE, transcendentals=0)


def gcd_of(a, b):
    while b:
        a, b = b, a % b
    return a


def in_vmem(value):
    return pltpu.with_memory_space_constraint(value, pltpu.VMEM)


def in_hbm(value):
    return pltpu.with_memory_space_constraint(value, pltpu.HBM)


def mask_rows(weight, keep, rows):
    return jnp.concatenate(
        [weight[i * rows : (i + 1) * rows, :] * keep[i : i + 1, :] for i in range(keep.shape[0])], axis=0
    )


def dot_nt(left, right):
    return lax.dot_general(left, right, (((1,), (1,)), ((), ())), preferred_element_type=F32)


def dot_tn(left, right):
    return lax.dot_general(left, right, (((0,), (0,)), ((), ())), preferred_element_type=F32)


def both_halves(blocks, half, second):
    low = [b[:half] for b in blocks]
    high = [b[half:] for b in blocks]
    mine = [jnp.where(second, h, l) for l, h in zip(low, high)]
    theirs = [jnp.where(second, l, h) for l, h in zip(low, high)]
    return jnp.concatenate(mine + theirs, axis=0)


def far_blocks(refs, k, own):
    return [r[k, b * own : (b + 1) * own, :] for r in refs for b in range(r.shape[1] // own)]


def one_hot(shape, match):
    return jnp.where(match, jnp.ones(shape, F32), jnp.zeros(shape, F32)).astype(BF)


def live(mask_ref):
    return jnp.where(mask_ref[...] > 0, 1.0, 0.0).astype(BF)


def open_kernel(n_deps, first, tiles, tile, place, x_ref, og_ref, gate_ref, up_ref, down_ref, gm_ref, um_ref, dm_ref, *rest):
    keep_ref, *send_refs, wg_ref, wu_ref, wd_ref, gk_ref, uk_ref, dk_ref, tok_ref, sems = rest[n_deps:]
    half = keep_ref.shape[1]
    feats = x_ref.shape[1]
    blocks = feats // BLK
    granules = dk_ref.shape[1]
    granule = tile // granules
    span = tiles * tile
    feat_block, unit_first, second = place[0], place[1] + first * tile, place[2] > 0

    def copies(t):
        if tiles == 1:
            here, there = pl.ds(first * tile, tile), pl.ds(0, tile)
        else:
            here = pl.ds(pl.multiple_of((first + t) * tile, tile), tile)
            there = pl.ds(pl.multiple_of(t * tile, tile), tile)
        return (
            pltpu.make_async_copy(gate_ref.at[:, here], wg_ref.at[:, there], sems.at[0, t]),
            pltpu.make_async_copy(up_ref.at[:, here], wu_ref.at[:, there], sems.at[1, t]),
            pltpu.make_async_copy(down_ref.at[here, :], wd_ref.at[there, :], sems.at[2, t]),
        )

    for t in range(tiles):
        for copy in copies(t):
            copy.start()

    tok_ref[...] = jnp.zeros_like(tok_ref)
    n_feat, n_unit = gm_ref.shape
    iota = lax.broadcasted_iota
    rows = one_hot((blocks, n_feat), iota(jnp.int32, (blocks, n_feat), 1) == feat_block + iota(jnp.int32, (blocks, n_feat), 0))
    lanes = one_hot((n_unit, span), iota(jnp.int32, (n_unit, span), 0) == (unit_first + iota(jnp.int32, (n_unit, span), 1)) // BLK)
    for m_ref, r_ref in ((gm_ref, gk_ref), (um_ref, uk_ref)):
        picked = jnp.dot(rows, live(m_ref), preferred_element_type=F32).astype(BF)
        r_ref[...] = jnp.dot(picked, lanes, preferred_element_type=F32).astype(BF)
    count = tiles * granules
    rows = one_hot((count, n_unit), iota(jnp.int32, (count, n_unit), 1) == (unit_first + iota(jnp.int32, (count, n_unit), 0) * granule) // BLK)
    lanes = one_hot((n_feat, feats), iota(jnp.int32, (n_feat, feats), 0) == feat_block + iota(jnp.int32, (n_feat, feats), 1) // BLK)
    picked = dot_nt(rows, live(dm_ref)).astype(BF)
    down_keep = jnp.dot(picked, lanes, preferred_element_type=F32).astype(BF)
    for t in range(tiles):
        dk_ref[t] = down_keep[t * granules : (t + 1) * granules]

    x = both_halves([x_ref[...]], half, second)
    og = both_halves([og_ref[...]], half, second)

    for t in range(tiles):
        here = pl.ds(t * tile, tile)
        arrivals = copies(t)
        for k, (w_ref, r_ref) in enumerate(((wg_ref, gk_ref), (wu_ref, uk_ref))):
            arrivals[k].wait()
            weight = mask_rows(w_ref[:, here], r_ref[:, here], BLK)
            w_ref[:, here] = weight
            part = jnp.dot(x, weight, preferred_element_type=F32).astype(BF)
            keep_ref[k, :, here] = part[:half]
            send_refs[k][:, here] = part[half:]
        arrivals[2].wait()
        weight = mask_rows(wd_ref[here, :], dk_ref[t], granule)
        wd_ref[here, :] = weight
        part = dot_nt(og, weight).astype(BF)
        keep_ref[2, :, here] = part[:half]
        send_refs[2][:, here] = part[half:]


TOKEN = jax.ShapeDtypeStruct((8, 128), F32)


def open_weights(place, x, og, gate_w, up_w, down_w, gm, um, dm, first, tiles, tile, granule, deps):
    rows, feats = x.shape
    half = rows // 2
    span = tiles * tile
    out = jax.ShapeDtypeStruct((3, half, span), BF)
    send = jax.ShapeDtypeStruct((half, span), BF)
    return pl.pallas_call(
        functools.partial(open_kernel, len(deps), first, tiles, tile),
        out_shape=(
            out,
            send,
            send,
            send,
            pltpu.VMEM((feats, span), BF),
            pltpu.VMEM((feats, span), BF),
            pltpu.VMEM((span, feats), BF),
            jax.ShapeDtypeStruct((feats // BLK, span), BF),
            jax.ShapeDtypeStruct((feats // BLK, span), BF),
            jax.ShapeDtypeStruct((tiles, tile // granule, feats), BF),
            TOKEN,
        ),
        in_specs=[SMEM, VMEM, VMEM, ANY, ANY, ANY, VMEM, VMEM, VMEM] + [ANY] * len(deps),
        out_specs=[VMEM] * 11,
        scratch_shapes=[pltpu.SemaphoreType.DMA((3, tiles))],
        compiler_params=params(),
        cost_estimate=cost(6 * rows * feats * span, 6 * feats * span),
        name="open_weights",
    )(place, x, og, in_hbm(gate_w), in_hbm(up_w), in_hbm(down_w), gm, um, dm, *deps)


def forward_kernel(n_far, own, offset, span, place, wg_ref, wu_ref, wd_ref, *rest):
    refs = rest[:n_far]
    keep_ref, *send_refs, tok_ref = rest[-5:]
    half = keep_ref.shape[1]
    second = place[2] > 0
    tok_ref[...] = jnp.zeros_like(tok_ref)
    x = both_halves(far_blocks(refs, 0, own), own // 2, second)
    here = pl.ds(offset, span)

    def put(k, value):
        value = value.astype(BF)
        keep_ref[k] = value[:half]
        send_refs[k][...] = value[half:]

    put(0, jnp.dot(x, wg_ref[:, here], preferred_element_type=F32))
    put(1, jnp.dot(x, wu_ref[:, here], preferred_element_type=F32))
    og = both_halves(far_blocks(refs, 1, own), own // 2, second)
    put(2, dot_nt(og, wd_ref[here, :]))


def forward(place, far, own, wg, wu, wd, offset, span, deps):
    rows, feats = sum(f.shape[1] for f in far), wg.shape[0]
    out = jax.ShapeDtypeStruct((3, rows // 2, span), BF)
    send = jax.ShapeDtypeStruct((rows // 2, span), BF)
    return pl.pallas_call(
        functools.partial(forward_kernel, len(far), own, offset, span),
        out_shape=(out, send, send, send, TOKEN),
        in_specs=[SMEM] + [VMEM] * (3 + len(far)) + [ANY] * len(deps),
        out_specs=[VMEM] * 5,
        compiler_params=params(),
        cost_estimate=cost(6 * rows * feats * span, 6 * feats * span),
        name="forward",
    )(place, in_vmem(wg), in_vmem(wu), in_vmem(wd), *far, *deps)


def tokens_kernel(n_far, own, place, x_ref, og_ref, *rest):
    refs = rest[:n_far]
    xt_ref, all_ref, tok_ref = rest[-3:]
    second = place[2] > 0
    tok_ref[...] = jnp.zeros_like(tok_ref)
    half = own // 2
    for k, mine in ((0, x_ref), (1, og_ref)):
        whole = jnp.concatenate(
            [both_halves([mine[...]], half, second), both_halves(far_blocks(refs, k, own), half, second)], axis=0
        )
        if k == 0:
            xt_ref[...] = whole.T
        else:
            all_ref[...] = whole


def all_tokens(place, x, og, far, deps):
    own, feats = x.shape
    rows = own + sum(f.shape[1] for f in far)
    return pl.pallas_call(
        functools.partial(tokens_kernel, len(far), own),
        out_shape=(jax.ShapeDtypeStruct((feats, rows), BF), jax.ShapeDtypeStruct((rows, feats), BF), TOKEN),
        in_specs=[SMEM] + [VMEM] * (2 + len(far)) + [ANY] * len(deps),
        out_specs=[VMEM] * 3,
        compiler_params=params(),
        cost_estimate=cost(rows * feats, 8 * rows * feats),
        name="all_tokens",
    )(place, x, og, *far, *deps)


def sum_kernel(keep_ref, *rest):
    others, out_ref = rest[:3], rest[3]
    for k, other in enumerate(others):
        out_ref[k] = (keep_ref[k].astype(F32) + other[...].astype(F32)).astype(BF)


def sum_of(keep, others):
    return pl.pallas_call(
        sum_kernel,
        out_shape=jax.ShapeDtypeStruct(keep.shape, BF),
        in_specs=[VMEM] * 4,
        out_specs=VMEM,
        compiler_params=params(),
        cost_estimate=cost(keep.size, 6 * keep.size),
        name="sum_cores",
    )(keep, *others)


def pointwise_kernel(n_other, sum_ref, *rest):
    others, (hidden_ref, gate_ref, up_ref, tok_ref) = rest[:n_other], rest[-4:]
    rows = hidden_ref.shape[0]
    tok_ref[...] = jnp.zeros_like(tok_ref)

    def step(here):
        total = [sum_ref[k, here, :].astype(F32) for k in range(3)]
        for other in others:
            total = [total[k] + other[k, here, :].astype(F32) for k in range(3)]
        gate_pre, up_pre, hidden_grad = total
        sigmoid_gate = jax.nn.sigmoid(gate_pre)
        active = gate_pre * sigmoid_gate
        hidden_ref[here, :] = (active * up_pre).astype(BF)
        gate_ref[here, :] = (
            hidden_grad * up_pre * sigmoid_gate * (1.0 + gate_pre * (1.0 - sigmoid_gate))
        ).astype(BF)
        up_ref[here, :] = (hidden_grad * active).astype(BF)

    if rows == 16:
        step(pl.ds(0, rows))
    else:

        @pl.loop(0, rows // 16)
        def _(i):
            step(pl.ds(pl.multiple_of(i * 16, 16), 16))


def pointwise(chip_sum, others, deps):
    return pl.pallas_call(
        functools.partial(pointwise_kernel, len(others)),
        out_shape=(*[jax.ShapeDtypeStruct(chip_sum.shape[1:], BF)] * 3, TOKEN),
        in_specs=[VMEM] * (1 + len(others)) + [ANY] * len(deps),
        out_specs=[VMEM] * 4,
        compiler_params=params(),
        cost_estimate=cost(20 * chip_sum.size, 6 * chip_sum.size),
        name="pointwise",
    )(chip_sum, *others, *deps)


def grad_tokens_kernel(offsets, weight_offset, span, prev_ref, wg_ref, wu_ref, *rest):
    n = len(offsets)
    gates, ups, (out_ref, tok_ref) = rest[:n], rest[n : 2 * n], rest[-2:]
    tok_ref[...] = jnp.zeros_like(tok_ref)
    here = pl.ds(weight_offset, span)
    gate_act = jnp.concatenate([p[:, s : s + span] for p, s in zip(gates, offsets)], axis=0)
    up_act = jnp.concatenate([p[:, s : s + span] for p, s in zip(ups, offsets)], axis=0)
    add = dot_nt(gate_act, wg_ref[:, here]) + dot_nt(up_act, wu_ref[:, here])
    if prev_ref is None:
        out_ref[...] = add
    else:
        out_ref[...] = prev_ref[...] + add


def grad_tokens_of(prev, wg, wu, weight_offset, parts, offsets, span, deps):
    rows = sum(p[1].shape[0] for p in parts)
    feats = wg.shape[0]
    kernel = functools.partial(grad_tokens_kernel, offsets, weight_offset, span)
    prevs = (prev,)
    if prev is None:
        kernel, prevs = functools.partial(kernel, None), ()
    return pl.pallas_call(
        kernel,
        out_shape=(jax.ShapeDtypeStruct((rows, feats), F32), TOKEN),
        in_specs=[VMEM] * (len(prevs) + 2 + 2 * len(parts)) + [ANY] * len(deps),
        out_specs=[VMEM] * 2,
        compiler_params=params(),
        cost_estimate=cost(4 * rows * feats * span, 4 * feats * span),
        name="grad_tokens",
    )(*prevs, in_vmem(wg), in_vmem(wu), *[p[1] for p in parts], *[p[2] for p in parts], *deps)


def weight_grads_kernel(n_parts, xt_ref, og_ref, gk_ref, uk_ref, dk_ref, *rest):
    n = n_parts
    hidden, gate_act, up_act = [
        jnp.concatenate([p[...] for p in rest[k * n : (k + 1) * n]], axis=0) for k in range(3)
    ]
    gate_ref, up_ref, down_ref, tok_ref = rest[-4:]
    tok_ref[...] = jnp.zeros_like(tok_ref)
    granule = down_ref.shape[0] // dk_ref.shape[1]
    xt = xt_ref[...]
    gate_ref[...] = mask_rows(
        jnp.dot(xt, gate_act, preferred_element_type=F32).astype(BF), gk_ref[...], BLK
    )
    up_ref[...] = mask_rows(jnp.dot(xt, up_act, preferred_element_type=F32).astype(BF), uk_ref[...], BLK)
    down_ref[...] = mask_rows(dot_tn(hidden, og_ref[...]).astype(BF), dk_ref[0], granule)


def weight_grads(prev, xt, og, gk, uk, dk, weight_start, parts, starts, first, tiles, tile, units, deps):
    feats, rows = xt.shape
    span = tiles * tile
    n_prev = 0 if prev is None else 3
    base = 5 + 3 * len(parts)

    def moved(s, i):
        return (0, s + i)

    return pl.pallas_call(
        functools.partial(weight_grads_kernel, len(parts)),
        out_shape=(
            pltpu.HBM((feats, units), BF),
            pltpu.HBM((feats, units), BF),
            pltpu.HBM((units, feats), BF),
            TOKEN,
        ),
        grid=(tiles,),
        in_specs=[
            pl.BlockSpec((feats, rows), lambda i: (0, 0)),
            pl.BlockSpec((rows, feats), lambda i: (0, 0)),
            pl.BlockSpec((gk.shape[0], tile), lambda i: (0, weight_start + i)),
            pl.BlockSpec((uk.shape[0], tile), lambda i: (0, weight_start + i)),
            pl.BlockSpec((1,) + dk.shape[1:], lambda i: (weight_start + i, 0, 0)),
        ]
        + [pl.BlockSpec((p[0].shape[0], tile), functools.partial(moved, s)) for p, s in zip(parts, starts)] * 3
        + [ANY] * (n_prev + len(deps)),
        out_specs=[
            pl.BlockSpec((feats, tile), lambda i: (0, first + i)),
            pl.BlockSpec((feats, tile), lambda i: (0, first + i)),
            pl.BlockSpec((tile, feats), lambda i: (first + i, 0)),
            pl.BlockSpec((8, 128), lambda i: (0, 0)),
        ],
        input_output_aliases={base + k: k for k in range(n_prev)},
        compiler_params=params(16),
        cost_estimate=cost(6 * rows * feats * span, 6 * feats * span),
        name="weight_grads",
    )(xt, og, gk, uk, dk, *[p[k] for k in range(3) for p in parts], *(() if prev is None else map(in_hbm, prev)), *deps)


def chunks_of(tiles, sizes):
    out, first = [], 0
    for size in sizes:
        size = min(size, tiles - first)
        if size > 0:
            out.append((first, size))
            first += size
    if first < tiles:
        out.append((first, tiles - first))
    return out


def local(n_row, n_col, tokens, out_grad, gate_w, up_w, down_w, gate_mask, up_mask, down_mask):
    rank_row, rank_col = lax.axis_index("row"), lax.axis_index("col")
    own, feats = tokens.shape
    units = gate_w.shape[1]
    half = own // 2
    n_chip = n_col // 2
    second_core = rank_col % 2 == 1
    tile = TILE if units % TILE == 0 else units
    tiles = units // tile
    granule = gcd_of(units, BLK)
    core_swap = [(i, i ^ 1) for i in range(n_col)]

    def swap_cores(values):
        return [lax.ppermute(value, "col", core_swap) for value in values]

    def from_chips(value):
        return [
            lax.ppermute(value, "col", [(i, (i + 2 * d) % n_col) for i in range(n_col)])
            for d in range(1, n_chip)
        ]

    both = jnp.stack([tokens, out_grad])
    if n_row <= 8:
        far = [lax.ppermute(both, "row", [(i, (i + d) % n_row) for i in range(n_row)]) for d in range(1, n_row)]
    else:
        whole = lax.all_gather(both, "row", axis=1, tiled=True)
        wanted = [lax.rem(rank_row - d + n_row, n_row) for d in range(1, n_row)]
        far = [jnp.concatenate([lax.dynamic_slice_in_dim(whole, w * own, own, 1) for w in wanted], axis=1)]

    place = jnp.stack([rank_col * (feats // BLK), rank_row * units, rank_col % 2]).astype(jnp.int32)
    masks = (gate_mask, up_mask, down_mask.T)

    own_chunks = chunks_of(tiles, OWN_CHUNKS)
    far_chunks = chunks_of(tiles, FAR_CHUNKS)

    def group_of(first):
        for g, (f, s) in enumerate(own_chunks):
            if f <= first < f + s:
                return g, first - f

    groups, own_sums, own_others, deps = [], [], [], ()
    for first, size in own_chunks:
        keep, *send, tok = open_weights(
            place, tokens, out_grad, gate_w, up_w, down_w, *masks, first, size, tile, granule, deps
        )
        send, group = send[:3], send[3:]
        groups.append(group)
        own_sums.append(sum_of(keep, swap_cores(send)))
        own_others.append(from_chips(own_sums[-1]))
        deps = (own_sums[-1],)

    far_sums, far_others, waiting = [], [], None
    for first, size in far_chunks:
        g, offset = group_of(first)
        keep, *send, tok = forward(place, far, own, *groups[g][:3], offset * tile, size * tile, deps)
        deps = (tok,)
        if waiting is not None:
            far_sums.append(sum_of(*waiting))
            far_others.append(from_chips(far_sums[-1]))
            deps += (far_sums[-1],)
        waiting = (keep, swap_cores(send))
    far_sums.append(sum_of(*waiting))
    far_others.append(from_chips(far_sums[-1]))

    xt_all, og_all, tok = all_tokens(place, tokens, out_grad, far, deps)
    deps = (tok, far_sums[-1])
    own_parts = []
    for chip_sum, other in zip(own_sums, own_others):
        *mine, tok = pointwise(chip_sum, other, deps)
        own_parts.append((mine, swap_cores(mine)))
        deps = (tok,)

    grads, gt, pending = None, None, []

    def flush(grads, work, deps):
        first, size, g, offset, parts, starts = work
        *grads, tok = weight_grads(
            grads, xt_all, og_all, *groups[g][3:], offset, parts, starts, first, size, tile, units, deps
        )
        return grads, (tok,)

    for c, (first, size) in enumerate(far_chunks):
        g, offset = group_of(first)
        *mine, tok = pointwise(far_sums[c], far_others[c], deps)
        deps = (tok,)
        parts = (*own_parts[g], mine, swap_cores(mine))
        if pending and c < len(far_chunks) - 1:
            grads, deps = flush(grads, pending.pop(0), deps)
        gt, tok = grad_tokens_of(
            gt, *groups[g][:2], offset * tile, parts, (offset * tile, offset * tile, 0, 0), size * tile, deps
        )
        deps = (tok,)
        pending.append((first, size, g, offset, parts, (offset, offset, 0, 0)))
    for work in pending:
        grads, deps = flush(grads, work, deps)

    gt = gt.astype(BF)
    far = gt[own:].reshape(2, n_row - 1, half, feats)
    total = gt[:own].astype(F32)
    if n_row <= 8:
        for d in range(1, n_row):
            piece = far[:, d - 1].reshape(own, feats)
            total = total + lax.ppermute(piece, "row", [(i, (i - d) % n_row) for i in range(n_row)]).astype(F32)
        total = total.astype(BF)
    else:
        order = jnp.concatenate([gt[:own].reshape(2, 1, half, feats), far], axis=1)
        order = jnp.swapaxes(order, 0, 1).reshape(n_row, own, feats)
        wanted = [lax.rem(rank_row - b + n_row, n_row) for b in range(n_row)]
        by_row = jnp.concatenate([lax.dynamic_slice_in_dim(order, w, 1, 0) for w in wanted], axis=0)
        total = lax.psum_scatter(by_row.reshape(n_row * own, feats), "row", scatter_dimension=0, tiled=True)
    low, high = total[:half], total[half:]
    total = jnp.concatenate([jnp.where(second_core, high, low), jnp.where(second_core, low, high)], axis=0)
    return (total, *grads)


def solution(mesh):
    in_specs = (
        P(("groups", "row"), "col"),
        P(("groups", "row"), "col"),
        P(("groups", "col"), "row"),
        P(("groups", "col"), "row"),
        P(("groups", "row"), "col"),
        P("groups", None),
        P("groups", None),
        P("groups", None),
    )
    out_specs = (
        P(("groups", "row"), "col"),
        P(("groups", "col"), "row"),
        P(("groups", "col"), "row"),
        P(("groups", "row"), "col"),
    )
    step = functools.partial(local, mesh.shape["row"], mesh.shape["col"])
    return jax.shard_map(step, mesh=mesh, in_specs=in_specs, out_specs=out_specs, check_vma=False)
```

time: 210 us -> 84.7 us (0.40)
  matrix products: 70.2 us -> 0 us
  blocking collectives: 58.8 us -> 0 us
  Pallas kernels: 0 us -> 37.9 us
  waiting for transfers between devices: 48.5 us -> 16.6 us
  starting transfers between devices: 0.08 us -> 24 us
  other arithmetic: 15 us -> 0.8 us
  between operations: 14.2 us -> 0.96 us
    dot_general x11 -> x0, matrix products: 70.2 us -> none  [the longest x3 24.2 us: block_keep(): jnp.dot(jnp.dot(pick_rows, block_table.astype(jnp.float32)), pick_cols)]
    all_gather x5 -> x0, blocking collectives: 58.8 us -> none  [the longest x1 15.8 us: local(): lax.all_gather(tokens, 'row', axis=0, tiled=True)]
    reduce_scatter x2 -> x0, waiting for transfers between devices: 48.5 us -> none  [the longest x1 36.5 us: local(): lax.psum_scatter(jnp.concatenate([jnp.dot(tokens_all, gate_live, preferre...]
    pallas_call x0 -> x24, Pallas kernels: none -> 37.9 us  [the longest x4 13.2 us: weight_grads(): pl.pallas_call(functools.partial(weight_grads_kernel, len(parts)), out_sh...]
    ppermute x0 -> x41, starting transfers between devices: none -> 24 us  [the longest x30 7.22 us: swap_cores(): return [lax.ppermute(value, 'col', core_swap) for value in values]]
    ppermute x0 -> x41, waiting for transfers between devices: none -> 16.6 us  [the longest x5 6.65 us: from_chips(): lax.ppermute(value, 'col', [(i, (i + 2 * d) % n_col) for i in range(n_col)])]
    concatenate x1, other arithmetic: 13.6 us -> 0.64 us  [local(): jnp.concatenate([jnp.where(second_core, high, low), jnp.where(second_core...]
  transfers between devices with their start and end apart: 2 -> 41, of which waited for: 2 -> 13; matrix products, arithmetic and copies ran while one was open for 4% -> 0% of each run, Pallas kernels for 0% -> 30%
where the time goes in v2:
time: 84.7 us; the launch traced here: 84 us
  Pallas kernels  37.9 us (45%)
  starting transfers between devices  24 us (28%)
  waiting for transfers between devices  16.6 us (20%)
  local copies, waits for them, and re-layouts  3.87 us (5%)
  between operations  0.96 us (1%)
    pallas_call x4, Pallas kernels, weight_grads(): pl.pallas_call(functools.partial(weight_grads_kernel, len(parts)), out_sh...  13.2 us
    pallas_call x1, Pallas kernels, open_weights(): pl.pallas_call(functools.partial(open_kernel, len(deps), first, tiles, ti...  10.4 us
    pallas_call x4, Pallas kernels, forward(): pl.pallas_call(functools.partial(forward_kernel, len(far), own, offset, s...  7.25 us
    ppermute x30, starting transfers between devices, swap_cores(): return [lax.ppermute(value, 'col', core_swap) for value in values]  7.22 us
    ppermute x5, waiting for transfers between devices, from_chips(): lax.ppermute(value, 'col', [(i, (i + 2 * d) % n_col) for i in range(n_col)])  6.65 us
    ppermute x3, starting transfers between devices, local(): lax.ppermute(both, 'row', [(i, (i + d) % n_row) for i in range(n_row)])  6.59 us
    ppermute x3, waiting for transfers between devices, local(): lax.ppermute(both, 'row', [(i, (i + d) % n_row) for i in range(n_row)])  6.34 us
    pallas_call x4, Pallas kernels, grad_tokens_of(): pl.pallas_call(kernel, out_shape=(jax.ShapeDtypeStruct((rows, feats), F32...  5.21 us
  transfers between devices with their start and end apart: 41, of which 13 were waited for; matrix products, arithmetic and copies ran while one was open for 0% of the time, Pallas kernels for 30%

profile of v2, /device:TPU:0, one launch (start us, length us, event | category | flops | bytes accessed | tf_op | source)
XLA Modules:
  0.0 84.0 jit_solution(5558332591439432337)
XLA Ops:
  0.7 0.8 copy-done
  1.6 0.8 copy-done.2
  2.4 0.7 copy-done.4
  3.1 0.7 copy-done.5
  3.8 0.7 copy-done.6
  4.6 10.4 %open_weights.1 = (bf16[3,16,3584]{2,1,0:T(8,128)(2,1)S(1)}, bf16[16,3584]{1,0:T(8,128)(2,1)S(1)}, bf16[16,3584]{1,0:T(8,128)(2,1)S(1)}, bf16[16,3584]{1,0:T(8,1...) custom-call(s32[3]{0:T(128)S(1)} %pad_add_fusion.place, ...), custom_call_target="tpu_custom_call" | custom-call | tf_op jit(solution)/shard_map/open_weights/pallas_call | solution.py:150
  15.0 0.5 collective-permute-start
  15.5 2.7 %collective-permute-start.4 = (bf16[2,32,1024]{2,1,0:T(8,128)(2,1)S(1)}, bf16[2,32,1024]{2,1,0:T(8,128)(2,1)S(1)}, u32[]{:S(2)}, u32[]{:S(2)}) collective-permute-start(bf16[2,32,1024]{2,1,0:T(8,128)(2,1)S(1)} %pad_maximum_fusion), channel_id=1, source_target_pairs={{0,4},{4,8},{8,12},{12,0},{1,5},{5,9},{9,13},{13,1},{2,6},{6,10},{... | collective-permute-start | bytes 393224 | tf_op jit(solution)/shard_map/ppermute | solution.py:419
  18.2 2.6 %collective-permute-start.5 = (bf16[2,32,1024]{2,1,0:T(8,128)(2,1)S(1)}, bf16[2,32,1024]{2,1,0:T(8,128)(2,1)S(1)}, u32[]{:S(2)}, u32[]{:S(2)}) collective-permute-start(bf16[2,32,1024]{2,1,0:T(8,128)(2,1)S(1)} %pad_maximum_fusion), channel_id=1, source_target_pairs={{0,8},{4,12},{8,0},{12,4},{1,9},{5,13},{9,1},{13,5},{2,10},{6,14},... | collective-permute-start | bytes 393224 | tf_op jit(solution)/shard_map/ppermute | solution.py:419
  20.8 1.3 %collective-permute-start.6 = (bf16[2,32,1024]{2,1,0:T(8,128)(2,1)S(1)}, bf16[2,32,1024]{2,1,0:T(8,128)(2,1)S(1)}, u32[]{:S(2)}, u32[]{:S(2)}) collective-permute-start(bf16[2,32,1024]{2,1,0:T(8,128)(2,1)S(1)} %pad_maximum_fusion), channel_id=1, source_target_pairs={{0,12},{4,0},{8,4},{12,8},{1,13},{5,1},{9,5},{13,9},{2,14},{6,2},{... | collective-permute-start | bytes 393224 | tf_op jit(solution)/shard_map/ppermute | solution.py:419
  22.1 0.5 collective-permute-start.2
  22.6 0.8 collective-permute-done.1.rest_1_
  23.7 1.0 %collective-permute-done.4.rest_0_ = bf16[2,32,1024]{2,1,0:T(8,128)(2,1)S(1)} collective-permute-done((bf16[2,32,1024]{2,1,0:T(8,128)(2,1)S(1)}, bf16[2,32,1024]{2,1,0:T(8,128)(2,1)S(1)}, u32[]{:S(2)}, u32[]{:S(2)}) %collective-permute-start.4) | collective-permute-done | bytes 131104 | tf_op jit(solution)/shard_map/ppermute | solution.py:419
  24.6 5.4 %collective-permute-done.5.rest_1_ = bf16[2,32,1024]{2,1,0:T(8,128)(2,1)S(1)} collective-permute-done((bf16[2,32,1024]{2,1,0:T(8,128)(2,1)S(1)}, bf16[2,32,1024]{2,1,0:T(8,128)(2,1)S(1)}, u32[]{:S(2)}, u32[]{:S(2)}) %collective-permute-start.5) | collective-permute-done | bytes 131104 | tf_op jit(solution)/shard_map/ppermute | solution.py:419
  30.0 2.0 %forward.4 = (bf16[3,48,1024]{2,1,0:T(8,128)(2,1)S(1)}, bf16[48,1024]{1,0:T(8,128)(2,1)S(1)}, bf16[48,1024]{1,0:T(8,128)(2,1)S(1)}, bf16[48,1024]{1,0:T(8,128)(2,1)S(1)}, f32[8,128]{1,0:T(8,128)S(1)}) custom-call(s32[3]{0:T(128)S(1)} %pad_add_fusion.place, bf16[1024,3584]{1,0:T(8,128)(2,1)S(1)} %get-tuple-element.80.wg_ref, ...), custom_call_target="tpu_custom_call" | custom-call | tf_op jit(solution)/shard_map/forward/pallas_call | solution.py:198
  32.1 0.5 collective-permute-start.8
  32.6 1.5 %collective-permute-start.3 = (bf16[3,16,3584]{2,1,0:T(8,128)(2,1)S(1)}, bf16[3,16,3584]{2,1,0:T(8,128)(2,1)S(1)}, u32[]{:S(2)}, u32[]{:S(2)}) collective-permute-start(bf16[3,16,3584]{2,1,0:T(8,128)(2,1)S(1)} %sum_cores.5.rest_3_.sum_ref), channel_id=1, source_target_pairs={{0,2},{1,3},{2,0},{3,1},{4,6},{5,7},{6,4},{7,5},{8,10},{9,11},{10,... | collective-permute-start | bytes 1032200 | tf_op jit(solution)/shard_map/ppermute | solution.py:413
  34.1 2.0 %forward.5 = (bf16[3,48,1024]{2,1,0:T(8,128)(2,1)S(1)}, bf16[48,1024]{1,0:T(8,128)(2,1)S(1)}, bf16[48,1024]{1,0:T(8,128)(2,1)S(1)}, bf16[48,1024]{1,0:T(8,128)(2,1)S(1)}, f32[8,128]{1,0:T(8,128)S(1)}) custom-call(s32[3]{0:T(128)S(1)} %pad_add_fusion.place, bf16[1024,3584]{1,0:T(8,128)(2,1)S(1)} %get-tuple-element.80.wg_ref, ...), custom_call_target="tpu_custom_call" | custom-call | tf_op jit(solution)/shard_map/forward/pallas_call | solution.py:198
  36.1 0.6 collective-permute-start.10
  36.7 0.4 collective-permute-start.12
  37.2 2.0 %forward.6 = (bf16[3,48,1024]{2,1,0:T(8,128)(2,1)S(1)}, bf16[48,1024]{1,0:T(8,128)(2,1)S(1)}, bf16[48,1024]{1,0:T(8,128)(2,1)S(1)}, bf16[48,1024]{1,0:T(8,128)(2,1)S(1)}, f32[8,128]{1,0:T(8,128)S(1)}) custom-call(s32[3]{0:T(128)S(1)} %pad_add_fusion.place, bf16[1024,3584]{1,0:T(8,128)(2,1)S(1)} %get-tuple-element.80.wg_ref, ...), custom_call_target="tpu_custom_call" | custom-call | tf_op jit(solution)/shard_map/forward/pallas_call | solution.py:198
  39.3 1.3 %forward.7 = (bf16[3,48,512]{2,1,0:T(8,128)(2,1)S(1)}, bf16[48,512]{1,0:T(8,128)(2,1)S(1)}, bf16[48,512]{1,0:T(8,128)(2,1)S(1)}, bf16[48,512]{1,0:T(8,128)(2,1)S(1)}, f32[8,128]{1,0:T(8,128)S(1)}) custom-call(s32[3]{0:T(128)S(1)} %pad_add_fusion.place, bf16[1024,3584]{1,0:T(8,128)(2,1)S(1)} %get-tuple-element.80.wg_ref, ...), custom_call_target="tpu_custom_call" | custom-call | tf_op jit(solution)/shard_map/forward/pallas_call | solution.py:198
  40.8 0.5 collective-permute-start.20
  42.1 0.6 collective-permute-done.17.rest_1_
  43.4 1.4 %collective-permute-start.24 = (bf16[3,48,1024]{2,1,0:T(8,128)(2,1)S(1)}, bf16[3,48,1024]{2,1,0:T(8,128)(2,1)S(1)}, u32[]{:S(2)}, u32[]{:S(2)}) collective-permute-start(bf16[3,48,1024]{2,1,0:T(8,128)(2,1)S(1)} %sum_cores.7.rest_4_.sum_ref), channel_id=1, source_target_pairs={{0,2},{1,3},{2,0},{3,1},{4,6},{5,7},{6,4},{7,5},{8,10},{9,11},{10,... | collective-permute-start | bytes 884744 | tf_op jit(solution)/shard_map/ppermute | solution.py:413
  44.9 0.7 all_tokens.1
  45.9 1.2 %collective-permute-start.29 = (bf16[3,48,1024]{2,1,0:T(8,128)(2,1)S(1)}, bf16[3,48,1024]{2,1,0:T(8,128)(2,1)S(1)}, u32[]{:S(2)}, u32[]{:S(2)}) collective-permute-start(bf16[3,48,1024]{2,1,0:T(8,128)(2,1)S(1)} %sum_cores.8.rest_4_.sum_ref), channel_id=1, source_target_pairs={{0,2},{1,3},{2,0},{3,1},{4,6},{5,7},{6,4},{7,5},{8,10},{9,11},{10,... | collective-permute-start | bytes 884744 | tf_op jit(solution)/shard_map/ppermute | solution.py:413
  47.2 3.5 %collective-permute-done.20.rest_0_ = bf16[3,48,1024]{2,1,0:T(8,128)(2,1)S(1)} collective-permute-done((bf16[3,48,1024]{2,1,0:T(8,128)(2,1)S(1)}, bf16[3,48,1024]{2,1,0:T(8,128)(2,1)S(1)}, u32[]{:S(2)}, u32[]{:S(2)}) %collective-permute-start.20) | collective-permute-done | bytes 294944 | tf_op jit(solution)/shard_map/ppermute | solution.py:413
  50.9 0.5 collective-permute-start.23
  51.5 0.7 collective-permute-done.21.rest_3_.rest_7_
  52.3 1.5 %grad_tokens.4 = (f32[128,1024]{1,0:T(8,128)S(1)}, f32[8,128]{1,0:T(8,128)S(1)}) custom-call(bf16[1024,3584]{1,0:T(8,128)(2,1)S(1)} %get-tuple-element.80.wg_ref, bf16[1024,3584]{1,0:T(8,128)(2,1)S(1)} %get-tuple-element.81.wu_ref, bf16[16,3584]{1,0:T(8,128)(2,1)S(1)} %get-tuple-element.108.rest_0_.rest_4_, ...), custom_call_target="tpu_custom_call" | custom-call | tf_op jit(solution)/shard_map/grad_tokens/pallas_call | solution.py:317
  53.8 3.2 %collective-permute-done.24.rest_0_ = bf16[3,48,1024]{2,1,0:T(8,128)(2,1)S(1)} collective-permute-done((bf16[3,48,1024]{2,1,0:T(8,128)(2,1)S(1)}, bf16[3,48,1024]{2,1,0:T(8,128)(2,1)S(1)}, u32[]{:S(2)}, u32[]{:S(2)}) %collective-permute-start.24) | collective-permute-done | bytes 294944 | tf_op jit(solution)/shard_map/ppermute | solution.py:413
  57.2 0.5 collective-permute-start.26
  57.7 0.5 collective-permute-start.33
  58.3 3.7 %weight_grads.4 = (bf16[1024,3584]{1,0:T(8,128)(2,1)}, bf16[1024,3584]{1,0:T(8,128)(2,1)}, bf16[3584,1024]{1,0:T(8,128)(2,1)}, f32[8,128]{1,0:T(8,128)S(1)}) custom-call(bf16[1024,128]{1,0:T(8,128)(2,1)S(1)} %get-tuple-element.118.xt_ref, bf16[128,1024]{1,0:T(8,128)(2,1)S(1)} %get-tuple-element.119.og_ref, bf16[8,3584]{1,0:T(8,128)(2,1)S(1)} %get-tuple-element.120.gk_ref, ...), custom_call_target="tpu_custom_call" | custom-call | tf_op jit(solution)/shard_map/weight_grads/pallas_call | solution.py:353
  61.9 1.5 %grad_tokens.5 = (f32[128,1024]{1,0:T(8,128)S(1)}, f32[8,128]{1,0:T(8,128)S(1)}) custom-call(f32[128,1024]{1,0:T(8,128)S(1)} %get-tuple-element.114.prev_ref, bf16[1024,3584]{1,0:T(8,128)(2,1)S(1)} %get-tuple-element.80.wg_ref, bf16[1024,3584]{1,0:T(8,128)(2,1)S(1)} %get-tuple-element.81.wu_ref, bf16[16,3584]{1,0:T(8,128)(2,1)S(1)} %get-tuple-element.108.rest_0_.rest_4_, ...), custom_call_target="tpu_custom_call" | custom-call | tf_op jit(solution)/shard_map/grad_tokens/pallas_call | solution.py:317
  63.6 0.6 collective-permute-start.30
  64.2 3.7 %weight_grads.5 = (bf16[1024,3584]{1,0:T(8,128)(2,1)}, bf16[1024,3584]{1,0:T(8,128)(2,1)}, bf16[3584,1024]{1,0:T(8,128)(2,1)}, f32[8,128]{1,0:T(8,128)S(1)}) custom-call(bf16[1024,128]{1,0:T(8,128)(2,1)S(1)} %get-tuple-element.118.xt_ref, ...), custom_call_target="tpu_custom_call", output_to_operand_aliasing={{0}: (17, {}), {1}: (18, {}), {2}: (19, {})} | custom-call | tf_op jit(solution)/shard_map/weight_grads/pallas_call | solution.py:353
  67.9 1.5 %grad_tokens.6 = (f32[128,1024]{1,0:T(8,128)S(1)}, f32[8,128]{1,0:T(8,128)S(1)}) custom-call(f32[128,1024]{1,0:T(8,128)S(1)} %get-tuple-element.127.prev_ref, bf16[1024,3584]{1,0:T(8,128)(2,1)S(1)} %get-tuple-element.80.wg_ref, bf16[1024,3584]{1,0:T(8,128)(2,1)S(1)} %get-tuple-element.81.wu_ref, bf16[16,3584]{1,0:T(8,128)(2,1)S(1)} %get-tuple-element.108.rest_0_.rest_4_, ...), custom_call_target="tpu_custom_call" | custom-call | tf_op jit(solution)/shard_map/grad_tokens/pallas_call | solution.py:317
  69.5 0.5 collective-permute-start.34
  70.0 0.4 collective-permute-start.40
  70.5 0.4 collective-permute-done.34.rest_3_.rest_7_
  71.2 0.8 grad_tokens.7
  72.1 4.4 %collective-permute-start.36 = (bf16[32,1024]{1,0:T(8,128)(2,1)S(1)}, bf16[32,1024]{1,0:T(8,128)(2,1)S(1)}, u32[]{:S(2)}, u32[]{:S(2)}) collective-permute-start(bf16[32,1024]{1,0:T(8,128)(2,1)S(1)} %bitcast.16), channel_id=1, source_target_pairs={{0,12},{4,0},{8,4},{12,8},{1,13},{5,1},{9,5},{13,9},{2,14},{6,2},{... | collective-permute-start | bytes 196616 | tf_op jit(solution)/shard_map/ppermute | solution.py:498
  76.5 0.4 collective-permute-start.37
  77.1 3.7 %weight_grads.6 = (bf16[1024,3584]{1,0:T(8,128)(2,1)}, bf16[1024,3584]{1,0:T(8,128)(2,1)}, bf16[3584,1024]{1,0:T(8,128)(2,1)}, f32[8,128]{1,0:T(8,128)S(1)}) custom-call(bf16[1024,128]{1,0:T(8,128)(2,1)S(1)} %get-tuple-element.118.xt_ref, ...), custom_call_target="tpu_custom_call", output_to_operand_aliasing={{0}: (17, {}), {1}: (18, {}), {2}: (19, {})} | custom-call | tf_op jit(solution)/shard_map/weight_grads/pallas_call | solution.py:353
  80.8 2.2 %weight_grads.7 = (bf16[1024,3584]{1,0:T(8,128)(2,1)}, bf16[1024,3584]{1,0:T(8,128)(2,1)}, bf16[3584,1024]{1,0:T(8,128)(2,1)}, f32[8,128]{1,0:T(8,128)}) custom-call(bf16[1024,128]{1,0:T(8,128)(2,1)S(1)} %get-tuple-element.118.xt_ref, bf16[128,1024]{1,0:T(8,128)(2,1)S(1)} %get-tuple-element.119.og_ref, ...), custom_call_target="tpu_custom_call", output_to_operand_aliasing={{0}: (17, {}), {1}: (18, {}), {2}: (19, {})} | custom-call | tf_op jit(solution)/shard_map/weight_grads/pallas_call | solution.py:353
  83.4 0.6 pad_maximum_fusion.1
  (80 shorter events, 4.9 us)
Async XLA Ops:
  0.7 0.8 %copy-start = (bf16[32,1024]{1,0:T(8,128)(2,1)S(1)}, bf16[32,1024]{1,0:T(8,128)(2,1)}, u32[]{:S(2)}) copy-start(bf16[32,1024]{1,0:T(8,128)(2,1)} %x_ref.3) | copy-start | bytes 196612
  1.6 0.8 copy-start.2
  2.4 0.7 copy-start.4
  3.1 0.7 copy-start.5
  3.8 0.7 copy-start.6
  4.6 10.9 %copy-start.1 = (bf16[32,1024]{1,0:T(8,128)(2,1)S(1)}, bf16[32,1024]{1,0:T(8,128)(2,1)}, u32[]{:S(2)}) copy-start(bf16[32,1024]{1,0:T(8,128)(2,1)} %x_ref.3) | copy-start | bytes 196612
  4.6 10.9 %copy-start.3 = (bf16[32,1024]{1,0:T(8,128)(2,1)S(1)}, bf16[32,1024]{1,0:T(8,128)(2,1)}, u32[]{:S(2)}) copy-start(bf16[32,1024]{1,0:T(8,128)(2,1)} %og_ref.3) | copy-start | bytes 196612
  15.0 7.1 %collective-permute-start = (bf16[16,3584]{1,0:T(8,128)(2,1)S(1)}, bf16[16,3584]{1,0:T(8,128)(2,1)S(1)}, u32[]{:S(2)}, u32[]{:S(2)}) collective-permute-start(bf16[16,3584]{1,0:T(8,128)(2,1)S(1)} %get-tuple-element.83), channel_id=1, source_target_pairs={{0,1},{1,0},{2,3},{3,2},{4,5},{5,4},{6,7},{7,6},{8,9},{9,8},{10,11... | collective-permute-start | bytes 344072 | tf_op jit(solution)/shard_map/ppermute | solution.py:409
  15.5 9.1 %collective-permute-start.4 = (bf16[2,32,1024]{2,1,0:T(8,128)(2,1)S(1)}, bf16[2,32,1024]{2,1,0:T(8,128)(2,1)S(1)}, u32[]{:S(2)}, u32[]{:S(2)}) collective-permute-start(bf16[2,32,1024]{2,1,0:T(8,128)(2,1)S(1)} %pad_maximum_fusion), channel_id=1, source_target_pairs={{0,4},{4,8},{8,12},{12,0},{1,5},{5,9},{9,13},{13,1},{2,6},{6,10},{... | collective-permute-start | bytes 393224 | tf_op jit(solution)/shard_map/ppermute | solution.py:419
  18.2 11.8 %collective-permute-start.5 = (bf16[2,32,1024]{2,1,0:T(8,128)(2,1)S(1)}, bf16[2,32,1024]{2,1,0:T(8,128)(2,1)S(1)}, u32[]{:S(2)}, u32[]{:S(2)}) collective-permute-start(bf16[2,32,1024]{2,1,0:T(8,128)(2,1)S(1)} %pad_maximum_fusion), channel_id=1, source_target_pairs={{0,8},{4,12},{8,0},{12,4},{1,9},{5,13},{9,1},{13,5},{2,10},{6,14},... | collective-permute-start | bytes 393224 | tf_op jit(solution)/shard_map/ppermute | solution.py:419
  20.8 9.3 %collective-permute-start.6 = (bf16[2,32,1024]{2,1,0:T(8,128)(2,1)S(1)}, bf16[2,32,1024]{2,1,0:T(8,128)(2,1)S(1)}, u32[]{:S(2)}, u32[]{:S(2)}) collective-permute-start(bf16[2,32,1024]{2,1,0:T(8,128)(2,1)S(1)} %pad_maximum_fusion), channel_id=1, source_target_pairs={{0,12},{4,0},{8,4},{12,8},{1,13},{5,1},{9,5},{13,9},{2,14},{6,2},{... | collective-permute-start | bytes 393224 | tf_op jit(solution)/shard_map/ppermute | solution.py:419
  22.1 1.3 %collective-permute-start.1 = (bf16[16,3584]{1,0:T(8,128)(2,1)S(1)}, bf16[16,3584]{1,0:T(8,128)(2,1)S(1)}, u32[]{:S(2)}, u32[]{:S(2)}) collective-permute-start(bf16[16,3584]{1,0:T(8,128)(2,1)S(1)} %get-tuple-element.84), channel_id=1, source_target_pairs={{0,1},{1,0},{2,3},{3,2},{4,5},{5,4},{6,7},{7,6},{8,9},{9,8},{10,11... | collective-permute-start | bytes 344072 | tf_op jit(solution)/shard_map/ppermute | solution.py:409
  22.1 1.5 %collective-permute-start.2 = (bf16[16,3584]{1,0:T(8,128)(2,1)S(1)}, bf16[16,3584]{1,0:T(8,128)(2,1)S(1)}, u32[]{:S(2)}, u32[]{:S(2)}) collective-permute-start(bf16[16,3584]{1,0:T(8,128)(2,1)S(1)} %get-tuple-element.85), channel_id=1, source_target_pairs={{0,1},{1,0},{2,3},{3,2},{4,5},{5,4},{6,7},{7,6},{8,9},{9,8},{10,11... | collective-permute-start | bytes 344072 | tf_op jit(solution)/shard_map/ppermute | solution.py:409
  32.0 4.6 %collective-permute-start.7 = (bf16[48,1024]{1,0:T(8,128)(2,1)S(1)}, bf16[48,1024]{1,0:T(8,128)(2,1)S(1)}, u32[]{:S(2)}, u32[]{:S(2)}) collective-permute-start(bf16[48,1024]{1,0:T(8,128)(2,1)S(1)} %get-tuple-element.90), channel_id=1, source_target_pairs={{0,1},{1,0},{2,3},{3,2},{4,5},{5,4},{6,7},{7,6},{8,9},{9,8},{10,11... | collective-permute-start | bytes 294920 | tf_op jit(solution)/shard_map/ppermute | solution.py:409
  32.1 4.6 %collective-permute-start.8 = (bf16[48,1024]{1,0:T(8,128)(2,1)S(1)}, bf16[48,1024]{1,0:T(8,128)(2,1)S(1)}, u32[]{:S(2)}, u32[]{:S(2)}) collective-permute-start(bf16[48,1024]{1,0:T(8,128)(2,1)S(1)} %get-tuple-element.91), channel_id=1, source_target_pairs={{0,1},{1,0},{2,3},{3,2},{4,5},{5,4},{6,7},{7,6},{8,9},{9,8},{10,11... | collective-permute-start | bytes 294920 | tf_op jit(solution)/shard_map/ppermute | solution.py:409
  32.6 13.0 %collective-permute-start.3 = (bf16[3,16,3584]{2,1,0:T(8,128)(2,1)S(1)}, bf16[3,16,3584]{2,1,0:T(8,128)(2,1)S(1)}, u32[]{:S(2)}, u32[]{:S(2)}) collective-permute-start(bf16[3,16,3584]{2,1,0:T(8,128)(2,1)S(1)} %sum_cores.5.rest_3_.sum_ref), channel_id=1, source_target_pairs={{0,2},{1,3},{2,0},{3,1},{4,6},{5,7},{6,4},{7,5},{8,10},{9,11},{10,... | collective-permute-start | bytes 1032200 | tf_op jit(solution)/shard_map/ppermute | solution.py:413
  34.1 3.1 %collective-permute-start.9 = (bf16[48,1024]{1,0:T(8,128)(2,1)S(1)}, bf16[48,1024]{1,0:T(8,128)(2,1)S(1)}, u32[]{:S(2)}, u32[]{:S(2)}) collective-permute-start(bf16[48,1024]{1,0:T(8,128)(2,1)S(1)} %get-tuple-element.92), channel_id=1, source_target_pairs={{0,1},{1,0},{2,3},{3,2},{4,5},{5,4},{6,7},{7,6},{8,9},{9,8},{10,11... | collective-permute-start | bytes 294920 | tf_op jit(solution)/shard_map/ppermute | solution.py:409
  36.1 3.2 %collective-permute-start.10 = (bf16[48,1024]{1,0:T(8,128)(2,1)S(1)}, bf16[48,1024]{1,0:T(8,128)(2,1)S(1)}, u32[]{:S(2)}, u32[]{:S(2)}) collective-permute-start(bf16[48,1024]{1,0:T(8,128)(2,1)S(1)} %get-tuple-element.95), channel_id=1, source_target_pairs={{0,1},{1,0},{2,3},{3,2},{4,5},{5,4},{6,7},{7,6},{8,9},{9,8},{10,11... | collective-permute-start | bytes 294920 | tf_op jit(solution)/shard_map/ppermute | solution.py:409
  36.7 2.6 %collective-permute-start.11 = (bf16[48,1024]{1,0:T(8,128)(2,1)S(1)}, bf16[48,1024]{1,0:T(8,128)(2,1)S(1)}, u32[]{:S(2)}, u32[]{:S(2)}) collective-permute-start(bf16[48,1024]{1,0:T(8,128)(2,1)S(1)} %get-tuple-element.96), channel_id=1, source_target_pairs={{0,1},{1,0},{2,3},{3,2},{4,5},{5,4},{6,7},{7,6},{8,9},{9,8},{10,11... | collective-permute-start | bytes 294920 | tf_op jit(solution)/shard_map/ppermute | solution.py:409
  36.7 2.5 %collective-permute-start.12 = (bf16[48,1024]{1,0:T(8,128)(2,1)S(1)}, bf16[48,1024]{1,0:T(8,128)(2,1)S(1)}, u32[]{:S(2)}, u32[]{:S(2)}) collective-permute-start(bf16[48,1024]{1,0:T(8,128)(2,1)S(1)} %get-tuple-element.97), channel_id=1, source_target_pairs={{0,1},{1,0},{2,3},{3,2},{4,5},{5,4},{6,7},{7,6},{8,9},{9,8},{10,11... | collective-permute-start | bytes 294920 | tf_op jit(solution)/shard_map/ppermute | solution.py:409
  40.7 1.3 %collective-permute-start.16 = (bf16[48,512]{1,0:T(8,128)(2,1)S(1)}, bf16[48,512]{1,0:T(8,128)(2,1)S(1)}, u32[]{:S(2)}, u32[]{:S(2)}) collective-permute-start(bf16[48,512]{1,0:T(8,128)(2,1)S(1)} %get-tuple-element.105), channel_id=1, source_target_pairs={{0,1},{1,0},{2,3},{3,2},{4,5},{5,4},{6,7},{7,6},{8,9},{9,8},{10,11... | collective-permute-start | bytes 147464 | tf_op jit(solution)/shard_map/ppermute | solution.py:409
  40.8 9.8 %collective-permute-start.20 = (bf16[3,48,1024]{2,1,0:T(8,128)(2,1)S(1)}, bf16[3,48,1024]{2,1,0:T(8,128)(2,1)S(1)}, u32[]{:S(2)}, u32[]{:S(2)}) collective-permute-start(bf16[3,48,1024]{2,1,0:T(8,128)(2,1)S(1)} %sum_cores.6.rest_4_.sum_ref), channel_id=1, source_target_pairs={{0,2},{1,3},{2,0},{3,1},{4,6},{5,7},{6,4},{7,5},{8,10},{9,11},{10,... | collective-permute-start | bytes 884744 | tf_op jit(solution)/shard_map/ppermute | solution.py:413
  41.4 2.0 %collective-permute-start.13 = (bf16[48,1024]{1,0:T(8,128)(2,1)S(1)}, bf16[48,1024]{1,0:T(8,128)(2,1)S(1)}, u32[]{:S(2)}, u32[]{:S(2)}) collective-permute-start(bf16[48,1024]{1,0:T(8,128)(2,1)S(1)} %get-tuple-element.100), channel_id=1, source_target_pairs={{0,1},{1,0},{2,3},{3,2},{4,5},{5,4},{6,7},{7,6},{8,9},{9,8},{10,11... | collective-permute-start | bytes 294920 | tf_op jit(solution)/shard_map/ppermute | solution.py:409
  41.5 1.2 %collective-permute-start.17 = (bf16[48,512]{1,0:T(8,128)(2,1)S(1)}, bf16[48,512]{1,0:T(8,128)(2,1)S(1)}, u32[]{:S(2)}, u32[]{:S(2)}) collective-permute-start(bf16[48,512]{1,0:T(8,128)(2,1)S(1)} %get-tuple-element.106), channel_id=1, source_target_pairs={{0,1},{1,0},{2,3},{3,2},{4,5},{5,4},{6,7},{7,6},{8,9},{9,8},{10,11... | collective-permute-start | bytes 147464 | tf_op jit(solution)/shard_map/ppermute | solution.py:409
  42.0 1.2 %collective-permute-start.18 = (bf16[48,512]{1,0:T(8,128)(2,1)S(1)}, bf16[48,512]{1,0:T(8,128)(2,1)S(1)}, u32[]{:S(2)}, u32[]{:S(2)}) collective-permute-start(bf16[48,512]{1,0:T(8,128)(2,1)S(1)} %get-tuple-element.107), channel_id=1, source_target_pairs={{0,1},{1,0},{2,3},{3,2},{4,5},{5,4},{6,7},{7,6},{8,9},{9,8},{10,11... | collective-permute-start | bytes 147464 | tf_op jit(solution)/shard_map/ppermute | solution.py:409
  42.8 2.1 %collective-permute-start.14 = (bf16[48,1024]{1,0:T(8,128)(2,1)S(1)}, bf16[48,1024]{1,0:T(8,128)(2,1)S(1)}, u32[]{:S(2)}, u32[]{:S(2)}) collective-permute-start(bf16[48,1024]{1,0:T(8,128)(2,1)S(1)} %get-tuple-element.101), channel_id=1, source_target_pairs={{0,1},{1,0},{2,3},{3,2},{4,5},{5,4},{6,7},{7,6},{8,9},{9,8},{10,11... | collective-permute-start | bytes 294920 | tf_op jit(solution)/shard_map/ppermute | solution.py:409
  43.2 1.6 %collective-permute-start.15 = (bf16[48,1024]{1,0:T(8,128)(2,1)S(1)}, bf16[48,1024]{1,0:T(8,128)(2,1)S(1)}, u32[]{:S(2)}, u32[]{:S(2)}) collective-permute-start(bf16[48,1024]{1,0:T(8,128)(2,1)S(1)} %get-tuple-element.102), channel_id=1, source_target_pairs={{0,1},{1,0},{2,3},{3,2},{4,5},{5,4},{6,7},{7,6},{8,9},{9,8},{10,11... | collective-permute-start | bytes 294920 | tf_op jit(solution)/shard_map/ppermute | solution.py:409
  43.4 13.6 %collective-permute-start.24 = (bf16[3,48,1024]{2,1,0:T(8,128)(2,1)S(1)}, bf16[3,48,1024]{2,1,0:T(8,128)(2,1)S(1)}, u32[]{:S(2)}, u32[]{:S(2)}) collective-permute-start(bf16[3,48,1024]{2,1,0:T(8,128)(2,1)S(1)} %sum_cores.7.rest_4_.sum_ref), channel_id=1, source_target_pairs={{0,2},{1,3},{2,0},{3,1},{4,6},{5,7},{6,4},{7,5},{8,10},{9,11},{10,... | collective-permute-start | bytes 884744 | tf_op jit(solution)/shard_map/ppermute | solution.py:413
  45.8 5.1 %collective-permute-start.19 = (bf16[16,3584]{1,0:T(8,128)(2,1)S(1)}, bf16[16,3584]{1,0:T(8,128)(2,1)S(1)}, u32[]{:S(2)}, u32[]{:S(2)}) collective-permute-start(bf16[16,3584]{1,0:T(8,128)(2,1)S(1)} %get-tuple-element.108.rest_0_.rest_4_), channel_id=1, source_target_pairs={{0,1},{1,0},{2,3},{3,2},{4,5},{5,4},{6,7},{7,6},{8,9},{9,8},{10,11... | collective-permute-start | bytes 344072 | tf_op jit(solution)/shard_map/ppermute | solution.py:409
  45.9 17.5 %collective-permute-start.29 = (bf16[3,48,1024]{2,1,0:T(8,128)(2,1)S(1)}, bf16[3,48,1024]{2,1,0:T(8,128)(2,1)S(1)}, u32[]{:S(2)}, u32[]{:S(2)}) collective-permute-start(bf16[3,48,1024]{2,1,0:T(8,128)(2,1)S(1)} %sum_cores.8.rest_4_.sum_ref), channel_id=1, source_target_pairs={{0,2},{1,3},{2,0},{3,1},{4,6},{5,7},{6,4},{7,5},{8,10},{9,11},{10,... | collective-permute-start | bytes 884744 | tf_op jit(solution)/shard_map/ppermute | solution.py:413
  47.1 4.3 %collective-permute-start.22 = (bf16[16,3584]{1,0:T(8,128)(2,1)S(1)}, bf16[16,3584]{1,0:T(8,128)(2,1)S(1)}, u32[]{:S(2)}, u32[]{:S(2)}) collective-permute-start(bf16[16,3584]{1,0:T(8,128)(2,1)S(1)} %get-tuple-element.111.rest_4_.rest_8_), channel_id=1, source_target_pairs={{0,1},{1,0},{2,3},{3,2},{4,5},{5,4},{6,7},{7,6},{8,9},{9,8},{10,11... | collective-permute-start | bytes 344072 | tf_op jit(solution)/shard_map/ppermute | solution.py:409
  50.8 1.4 %collective-permute-start.21 = (bf16[48,1024]{1,0:T(8,128)(2,1)S(1)}, bf16[48,1024]{1,0:T(8,128)(2,1)S(1)}, u32[]{:S(2)}, u32[]{:S(2)}) collective-permute-start(bf16[48,1024]{1,0:T(8,128)(2,1)S(1)} %get-tuple-element.110.rest_2_.rest_6_), channel_id=1, source_target_pairs={{0,1},{1,0},{2,3},{3,2},{4,5},{5,4},{6,7},{7,6},{8,9},{9,8},{10,11... | collective-permute-start | bytes 294920 | tf_op jit(solution)/shard_map/ppermute | solution.py:409
  50.9 1.4 %collective-permute-start.23 = (bf16[48,1024]{1,0:T(8,128)(2,1)S(1)}, bf16[48,1024]{1,0:T(8,128)(2,1)S(1)}, u32[]{:S(2)}, u32[]{:S(2)}) collective-permute-start(bf16[48,1024]{1,0:T(8,128)(2,1)S(1)} %get-tuple-element.112.rest_6_.rest_10_), channel_id=1, source_target_pairs={{0,1},{1,0},{2,3},{3,2},{4,5},{5,4},{6,7},{7,6},{8,9},{9,8},{10,11... | collective-permute-start | bytes 294920 | tf_op jit(solution)/shard_map/ppermute | solution.py:409
  51.4 6.3 %collective-permute-start.27 = (bf16[16,3584]{1,0:T(8,128)(2,1)S(1)}, bf16[16,3584]{1,0:T(8,128)(2,1)S(1)}, u32[]{:S(2)}, u32[]{:S(2)}) collective-permute-start(bf16[16,3584]{1,0:T(8,128)(2,1)S(1)} %get-tuple-element.123.rest_0_), channel_id=1, source_target_pairs={{0,1},{1,0},{2,3},{3,2},{4,5},{5,4},{6,7},{7,6},{8,9},{9,8},{10,11... | collective-permute-start | bytes 344072 | tf_op jit(solution)/shard_map/ppermute | solution.py:409
  52.2 6.1 %collective-permute-start.28 = (bf16[48,1024]{1,0:T(8,128)(2,1)S(1)}, bf16[48,1024]{1,0:T(8,128)(2,1)S(1)}, u32[]{:S(2)}, u32[]{:S(2)}) collective-permute-start(bf16[48,1024]{1,0:T(8,128)(2,1)S(1)} %get-tuple-element.124.rest_2_), channel_id=1, source_target_pairs={{0,1},{1,0},{2,3},{3,2},{4,5},{5,4},{6,7},{7,6},{8,9},{9,8},{10,11... | collective-permute-start | bytes 294920 | tf_op jit(solution)/shard_map/ppermute | solution.py:409
  57.1 4.8 %collective-permute-start.25 = (bf16[48,1024]{1,0:T(8,128)(2,1)S(1)}, bf16[48,1024]{1,0:T(8,128)(2,1)S(1)}, u32[]{:S(2)}, u32[]{:S(2)}) collective-permute-start(bf16[48,1024]{1,0:T(8,128)(2,1)S(1)} %get-tuple-element.116.rest_2_.rest_6_), channel_id=1, source_target_pairs={{0,1},{1,0},{2,3},{3,2},{4,5},{5,4},{6,7},{7,6},{8,9},{9,8},{10,11... | collective-permute-start | bytes 294920 | tf_op jit(solution)/shard_map/ppermute | solution.py:409
  57.2 4.7 %collective-permute-start.26 = (bf16[48,1024]{1,0:T(8,128)(2,1)S(1)}, bf16[48,1024]{1,0:T(8,128)(2,1)S(1)}, u32[]{:S(2)}, u32[]{:S(2)}) collective-permute-start(bf16[48,1024]{1,0:T(8,128)(2,1)S(1)} %get-tuple-element.117.rest_6_.rest_10_), channel_id=1, source_target_pairs={{0,1},{1,0},{2,3},{3,2},{4,5},{5,4},{6,7},{7,6},{8,9},{9,8},{10,11... | collective-permute-start | bytes 294920 | tf_op jit(solution)/shard_map/ppermute | solution.py:409
  57.7 11.7 %collective-permute-start.33 = (bf16[3,48,512]{2,1,0:T(8,128)(2,1)S(1)}, bf16[3,48,512]{2,1,0:T(8,128)(2,1)S(1)}, u32[]{:S(2)}, u32[]{:S(2)}) collective-permute-start(bf16[3,48,512]{2,1,0:T(8,128)(2,1)S(1)} %sum_cores.9.rest_2_.sum_ref), channel_id=1, source_target_pairs={{0,2},{1,3},{2,0},{3,1},{4,6},{5,7},{6,4},{7,5},{8,10},{9,11},{10,... | collective-permute-start | bytes 442376 | tf_op jit(solution)/shard_map/ppermute | solution.py:413
  58.2 6.0 %collective-permute-start.32 = (bf16[48,1024]{1,0:T(8,128)(2,1)S(1)}, bf16[48,1024]{1,0:T(8,128)(2,1)S(1)}, u32[]{:S(2)}, u32[]{:S(2)}) collective-permute-start(bf16[48,1024]{1,0:T(8,128)(2,1)S(1)} %get-tuple-element.131.rest_2_), channel_id=1, source_target_pairs={{0,1},{1,0},{2,3},{3,2},{4,5},{5,4},{6,7},{7,6},{8,9},{9,8},{10,11... | collective-permute-start | bytes 294920 | tf_op jit(solution)/shard_map/ppermute | solution.py:409
  63.6 4.3 %collective-permute-start.30 = (bf16[48,1024]{1,0:T(8,128)(2,1)S(1)}, bf16[48,1024]{1,0:T(8,128)(2,1)S(1)}, u32[]{:S(2)}, u32[]{:S(2)}) collective-permute-start(bf16[48,1024]{1,0:T(8,128)(2,1)S(1)} %get-tuple-element.129.rest_2_.rest_6_), channel_id=1, source_target_pairs={{0,1},{1,0},{2,3},{3,2},{4,5},{5,4},{6,7},{7,6},{8,9},{9,8},{10,11... | collective-permute-start | bytes 294920 | tf_op jit(solution)/shard_map/ppermute | solution.py:409
  64.1 3.7 %collective-permute-start.31 = (bf16[48,1024]{1,0:T(8,128)(2,1)S(1)}, bf16[48,1024]{1,0:T(8,128)(2,1)S(1)}, u32[]{:S(2)}, u32[]{:S(2)}) collective-permute-start(bf16[48,1024]{1,0:T(8,128)(2,1)S(1)} %get-tuple-element.130.rest_6_.rest_10_), channel_id=1, source_target_pairs={{0,1},{1,0},{2,3},{3,2},{4,5},{5,4},{6,7},{7,6},{8,9},{9,8},{10,11... | collective-permute-start | bytes 294920 | tf_op jit(solution)/shard_map/ppermute | solution.py:409
  69.5 1.4 %collective-permute-start.34 = (bf16[48,512]{1,0:T(8,128)(2,1)S(1)}, bf16[48,512]{1,0:T(8,128)(2,1)S(1)}, u32[]{:S(2)}, u32[]{:S(2)}) collective-permute-start(bf16[48,512]{1,0:T(8,128)(2,1)S(1)} %get-tuple-element.139.rest_2_.rest_6_), channel_id=1, source_target_pairs={{0,1},{1,0},{2,3},{3,2},{4,5},{5,4},{6,7},{7,6},{8,9},{9,8},{10,11... | collective-permute-start | bytes 147464 | tf_op jit(solution)/shard_map/ppermute | solution.py:409
  70.0 1.2 %collective-permute-start.35 = (bf16[48,512]{1,0:T(8,128)(2,1)S(1)}, bf16[48,512]{1,0:T(8,128)(2,1)S(1)}, u32[]{:S(2)}, u32[]{:S(2)}) collective-permute-start(bf16[48,512]{1,0:T(8,128)(2,1)S(1)} %get-tuple-element.140.rest_6_.rest_10_), channel_id=1, source_target_pairs={{0,1},{1,0},{2,3},{3,2},{4,5},{5,4},{6,7},{7,6},{8,9},{9,8},{10,11... | collective-permute-start | bytes 147464 | tf_op jit(solution)/shard_map/ppermute | solution.py:409
  70.0 7.1 %collective-permute-start.40 = (bf16[48,1024]{1,0:T(8,128)(2,1)S(1)}, bf16[48,1024]{1,0:T(8,128)(2,1)S(1)}, u32[]{:S(2)}, u32[]{:S(2)}) collective-permute-start(bf16[48,1024]{1,0:T(8,128)(2,1)S(1)} %get-tuple-element.144.rest_2_), channel_id=1, source_target_pairs={{0,1},{1,0},{2,3},{3,2},{4,5},{5,4},{6,7},{7,6},{8,9},{9,8},{10,11... | collective-permute-start | bytes 294920 | tf_op jit(solution)/shard_map/ppermute | solution.py:409
  72.1 11.0 %collective-permute-start.36 = (bf16[32,1024]{1,0:T(8,128)(2,1)S(1)}, bf16[32,1024]{1,0:T(8,128)(2,1)S(1)}, u32[]{:S(2)}, u32[]{:S(2)}) collective-permute-start(bf16[32,1024]{1,0:T(8,128)(2,1)S(1)} %bitcast.16), channel_id=1, source_target_pairs={{0,12},{4,0},{8,4},{12,8},{1,13},{5,1},{9,5},{13,9},{2,14},{6,2},{... | collective-permute-start | bytes 196616 | tf_op jit(solution)/shard_map/ppermute | solution.py:498
  76.5 6.8 %collective-permute-start.37 = (bf16[32,1024]{1,0:T(8,128)(2,1)S(1)}, bf16[32,1024]{1,0:T(8,128)(2,1)S(1)}, u32[]{:S(2)}, u32[]{:S(2)}) collective-permute-start(bf16[32,1024]{1,0:T(8,128)(2,1)S(1)} %bitcast.15), channel_id=1, source_target_pairs={{0,8},{4,12},{8,0},{12,4},{1,9},{5,13},{9,1},{13,5},{2,10},{6,14},... | collective-permute-start | bytes 196616 | tf_op jit(solution)/shard_map/ppermute | solution.py:498
  76.9 6.5 %collective-permute-start.38 = (bf16[32,1024]{1,0:T(8,128)(2,1)S(1)}, bf16[32,1024]{1,0:T(8,128)(2,1)S(1)}, u32[]{:S(2)}, u32[]{:S(2)}) collective-permute-start(bf16[32,1024]{1,0:T(8,128)(2,1)S(1)} %bitcast.14), channel_id=1, source_target_pairs={{0,4},{4,8},{8,12},{12,0},{1,5},{5,9},{9,13},{13,1},{2,6},{6,10},{... | collective-permute-start | bytes 196616 | tf_op jit(solution)/shard_map/ppermute | solution.py:498
  77.1 3.7 %collective-permute-start.39 = (bf16[48,512]{1,0:T(8,128)(2,1)S(1)}, bf16[48,512]{1,0:T(8,128)(2,1)S(1)}, u32[]{:S(2)}, u32[]{:S(2)}) collective-permute-start(bf16[48,512]{1,0:T(8,128)(2,1)S(1)} %get-tuple-element.143.rest_2_), channel_id=1, source_target_pairs={{0,1},{1,0},{2,3},{3,2},{4,5},{5,4},{6,7},{7,6},{8,9},{9,8},{10,11... | collective-permute-start | bytes 147464 | tf_op jit(solution)/shard_map/ppermute | solution.py:409

commit v3 on v2

v3 whole, which is shorter than its diff:
```python
import functools

import jax
import jax.numpy as jnp
from jax import lax
from jax.experimental import pallas as pl
from jax.experimental.pallas import tpu as pltpu
from jax.sharding import PartitionSpec as P

BLK = 128
TILE = 512
LANE = 16
AHEAD = 2
COST_SCALE = 1000000000
OWN_CHUNKS = (4, 3)
OWN_PIECES = (((0,), (1,), (2,)), ((0, 1), (2,)))
OWN_AFTER = (0, 2)
FAR_PIECES = ((0,), (1,), (2,))
FAR_CHUNKS = (2, 2, 2, 1)
BF = jnp.bfloat16
F32 = jnp.float32
ANY = pl.BlockSpec(memory_space=pl.ANY)
VMEM = pl.BlockSpec(memory_space=pltpu.VMEM)
SMEM = pl.BlockSpec(memory_space=pltpu.SMEM)


def params(mib=8):
    return pltpu.CompilerParams(vmem_limit_bytes=mib * 1024 * 1024)


def cost(flops, nbytes):
    return pl.CostEstimate(flops=int(flops) // COST_SCALE, bytes_accessed=int(nbytes) // COST_SCALE, transcendentals=0)


def gcd_of(a, b):
    while b:
        a, b = b, a % b
    return a


def in_vmem(value):
    return pltpu.with_memory_space_constraint(value, pltpu.VMEM)


def in_hbm(value):
    return pltpu.with_memory_space_constraint(value, pltpu.HBM)


def mask_rows(weight, keep, rows):
    pieces = []
    for i in range(weight.shape[0] // rows):
        mask = keep[LANE * i : LANE * (i + 1), :]
        pieces += [weight[i * rows + g : i * rows + g + LANE, :] * mask for g in range(0, rows, LANE)]
    return jnp.concatenate(pieces, axis=0)


def dot_nt(left, right):
    return lax.dot_general(left, right, (((1,), (1,)), ((), ())), preferred_element_type=F32)


def dot_tn(left, right):
    return lax.dot_general(left, right, (((0,), (0,)), ((), ())), preferred_element_type=F32)


def both_halves(blocks, half, second):
    low = [b[:half] for b in blocks]
    high = [b[half:] for b in blocks]
    mine = [jnp.where(second, h, l) for l, h in zip(low, high)]
    theirs = [jnp.where(second, l, h) for l, h in zip(low, high)]
    return jnp.concatenate(mine + theirs, axis=0)


def far_blocks(refs, k, own):
    return [r[k, b * own : (b + 1) * own, :] for r in refs for b in range(r.shape[1] // own)]


def one_hot(shape, match):
    return jnp.where(match, jnp.ones(shape, F32), jnp.zeros(shape, F32)).astype(BF)


def live(mask_ref):
    return jnp.where(mask_ref[...] > 0, 1.0, 0.0).astype(BF)


def open_kernel(n_deps, pieces, opener, first, tiles, tile, granule, place, both_ref, gate_ref, up_ref, down_ref, *rest):
    keeps, rest = rest[:3], rest[3 + n_deps :]
    keep_ref, *sends = rest[: 1 + len(pieces)]
    rest = rest[1 + len(pieces) :]
    wg_ref, wu_ref, wd_ref, tok_ref = rest[:4]
    sems, rest = rest[-1], rest[4:-1]
    half, feats = keep_ref.shape[1], wg_ref.shape[0]
    granules = tile // granule

    def copies(t):
        here, there = pl.ds((first + t) * tile, tile), pl.ds(t * tile, tile)
        return (
            pltpu.make_async_copy(gate_ref.at[:, here], wg_ref.at[:, there], sems.at[0, t]),
            pltpu.make_async_copy(up_ref.at[:, here], wu_ref.at[:, there], sems.at[1, t]),
            pltpu.make_async_copy(down_ref.at[here, :], wd_ref.at[there, :], sems.at[2, t]),
        )

    if opener:
        gk_ref, uk_ref, dk_ref, gm_ref, um_ref, dm_ref, mask_sems = rest
        fetches = [pltpu.make_async_copy(a, b, mask_sems.at[i]) for i, (a, b) in enumerate(zip(keeps, (gm_ref, um_ref, dm_ref)))]
        for fetch in fetches:
            fetch.start()
    else:
        gk_ref, uk_ref, dk_ref = keeps
    for t in range(min(AHEAD, tiles)):
        for copy in copies(t):
            copy.start()
    tok_ref[...] = jnp.zeros_like(tok_ref)
    if opener:
        for fetch in fetches:
            fetch.wait()
        keep_rows(place, gm_ref, um_ref, dm_ref, gk_ref, uk_ref, dk_ref, granule)

    second = place[2] > 0
    x = both_halves([both_ref[0]], half, second)
    og = both_halves([both_ref[1]], half, second)

    def put(k, t, part):
        here = pl.ds(t * tile, tile)
        keep_ref[k, :, here] = part[:half]
        for ks, ref in zip(pieces, sends):
            if k in ks:
                ref[ks.index(k), :, here] = part[half:]

    for t in range(tiles):
        here, lanes = pl.ds(t * tile, tile), pl.ds((first + t) * tile, tile)
        arrivals = copies(t)
        for k, (w_ref, r_ref) in enumerate(((wg_ref, gk_ref), (wu_ref, uk_ref))):
            arrivals[k].wait()
            if t + AHEAD < tiles:
                copies(t + AHEAD)[k].start()
            weight = mask_rows(w_ref[:, here], r_ref[:, lanes], BLK)
            w_ref[:, here] = weight
            put(k, t, jnp.dot(x, weight, preferred_element_type=F32).astype(BF))
        arrivals[2].wait()
        if t + AHEAD < tiles:
            copies(t + AHEAD)[2].start()
        masks = pl.ds((first + t) * granules * LANE, granules * LANE)
        weight = mask_rows(wd_ref[here, :], dk_ref[masks, :], granule)
        wd_ref[here, :] = weight
        put(2, t, dot_nt(og, weight).astype(BF))


def keep_rows(place, gm_ref, um_ref, dm_ref, gk_ref, uk_ref, dk_ref, granule):
    feat_block, unit_first = place[0], place[1]
    n_feat, n_unit = gm_ref.shape
    units, feats = gk_ref.shape[1], dk_ref.shape[1]
    iota = lax.broadcasted_iota
    rows = (feats // BLK * LANE, n_feat)
    rows = one_hot(rows, iota(jnp.int32, rows, 1) == feat_block + iota(jnp.int32, rows, 0) // LANE)
    lanes = (n_unit, units)
    lanes = one_hot(lanes, iota(jnp.int32, lanes, 0) == (unit_first + iota(jnp.int32, lanes, 1)) // BLK)
    for m_ref, r_ref in ((gm_ref, gk_ref), (um_ref, uk_ref)):
        picked = jnp.dot(rows, live(m_ref), preferred_element_type=F32).astype(BF)
        r_ref[...] = jnp.dot(picked, lanes, preferred_element_type=F32).astype(BF)
    rows = (units // granule * LANE, n_unit)
    rows = one_hot(rows, iota(jnp.int32, rows, 1) == (unit_first + iota(jnp.int32, rows, 0) // LANE * granule) // BLK)
    lanes = (n_feat, feats)
    lanes = one_hot(lanes, iota(jnp.int32, lanes, 0) == feat_block + iota(jnp.int32, lanes, 1) // BLK)
    picked = dot_nt(rows, live(dm_ref)).astype(BF)
    dk_ref[...] = jnp.dot(picked, lanes, preferred_element_type=F32).astype(BF)


TOKEN = jax.ShapeDtypeStruct((8, 128), F32)


def open_weights(place, both, gate_w, up_w, down_w, masks, keeps, first, tiles, tile, granule, pieces, deps):
    _, rows, feats = both.shape
    units = gate_w.shape[1]
    half = rows // 2
    span = tiles * tile
    opener = keeps is None
    made = [
        jax.ShapeDtypeStruct((feats // BLK * LANE, units), BF),
        jax.ShapeDtypeStruct((feats // BLK * LANE, units), BF),
        jax.ShapeDtypeStruct((units // granule * LANE, feats), BF),
    ]
    scratch = [pltpu.VMEM(m.shape, m.dtype) for m in masks] + [pltpu.SemaphoreType.DMA((3,))]
    keep, *rest = pl.pallas_call(
        functools.partial(open_kernel, len(deps), pieces, opener, first, tiles, tile, granule),
        out_shape=(
            jax.ShapeDtypeStruct((3, half, span), BF),
            *[jax.ShapeDtypeStruct((len(ks), half, span), BF) for ks in pieces],
            pltpu.VMEM((feats, span), BF),
            pltpu.VMEM((feats, span), BF),
            pltpu.VMEM((span, feats), BF),
            TOKEN,
            *(made if opener else ()),
        ),
        in_specs=[SMEM, VMEM, ANY, ANY, ANY] + [ANY if opener else VMEM] * 3 + [ANY] * len(deps),
        out_specs=[VMEM] * (5 + len(pieces) + (3 if opener else 0)),
        scratch_shapes=(scratch if opener else []) + [pltpu.SemaphoreType.DMA((3, tiles))],
        compiler_params=params(),
        cost_estimate=cost(6 * rows * feats * span, 6 * feats * span),
        name="open_weights",
    )(place, both, *map(in_hbm, (gate_w, up_w, down_w)), *(map(in_hbm, masks) if opener else keeps), *deps)
    n = len(pieces)
    return keep, rest[:n], rest[n : n + 3], rest[n + 4 :] if opener else keeps


def forward_kernel(pieces, own, offset, span, x_ref, og_ref, wg_ref, wu_ref, wd_ref, *rest):
    keep_ref, *sends, tok_ref = rest[-2 - len(pieces) :]
    half = keep_ref.shape[1]
    tok_ref[...] = jnp.zeros_like(tok_ref)
    x = x_ref[own:, :]
    here = pl.ds(offset, span)

    def put(k, value):
        value = value.astype(BF)
        keep_ref[k] = value[:half]
        for ks, ref in zip(pieces, sends):
            if k in ks:
                ref[ks.index(k)] = value[half:]

    put(0, jnp.dot(x, wg_ref[:, here], preferred_element_type=F32))
    put(1, jnp.dot(x, wu_ref[:, here], preferred_element_type=F32))
    put(2, dot_nt(og_ref[own:, :], wd_ref[here, :]))


def forward(x_all, og_all, own, wg, wu, wd, offset, span, pieces, deps):
    rows, feats = x_all.shape[0] - own, x_all.shape[1]
    keep, *sends, tok = pl.pallas_call(
        functools.partial(forward_kernel, pieces, own, offset, span),
        out_shape=(
            jax.ShapeDtypeStruct((3, rows // 2, span), BF),
            *[jax.ShapeDtypeStruct((len(ks), rows // 2, span), BF) for ks in pieces],
            TOKEN,
        ),
        in_specs=[VMEM] * 5 + [ANY] * len(deps),
        out_specs=[VMEM] * (2 + len(pieces)),
        compiler_params=params(),
        cost_estimate=cost(6 * rows * feats * span, 6 * feats * span),
        name="forward",
    )(x_all, og_all, in_vmem(wg), in_vmem(wu), in_vmem(wd), *deps)
    return keep, sends, tok


def tokens_kernel(n_far, own, place, both_ref, *rest):
    refs = rest[:n_far]
    x_ref, xt_ref, og_ref, tok_ref = rest[-4:]
    second = place[2] > 0
    tok_ref[...] = jnp.zeros_like(tok_ref)
    half = own // 2
    for k, out_ref in ((0, x_ref), (1, og_ref)):
        whole = jnp.concatenate(
            [both_halves([both_ref[k]], half, second), both_halves(far_blocks(refs, k, own), half, second)], axis=0
        )
        out_ref[...] = whole
        if k == 0:
            xt_ref[...] = whole.T


def all_tokens(place, both, far, deps):
    _, own, feats = both.shape
    rows = own + sum(f.shape[1] for f in far)
    return pl.pallas_call(
        functools.partial(tokens_kernel, len(far), own),
        out_shape=(
            jax.ShapeDtypeStruct((rows, feats), BF),
            jax.ShapeDtypeStruct((feats, rows), BF),
            jax.ShapeDtypeStruct((rows, feats), BF),
            TOKEN,
        ),
        in_specs=[SMEM] + [VMEM] * (1 + len(far)) + [ANY] * len(deps),
        out_specs=[VMEM] * 4,
        compiler_params=params(),
        cost_estimate=cost(rows * feats, 8 * rows * feats),
        name="all_tokens",
    )(place, both, *far, *deps)


def sum_kernel(pieces, keep_ref, *rest):
    others, out_ref = rest[: len(pieces)], rest[-1]
    for ks, other in zip(pieces, others):
        for i, k in enumerate(ks):
            out_ref[k] = (keep_ref[k].astype(F32) + other[i].astype(F32)).astype(BF)


def sum_of(keep, others, pieces, deps):
    return pl.pallas_call(
        functools.partial(sum_kernel, pieces),
        out_shape=jax.ShapeDtypeStruct(keep.shape, BF),
        in_specs=[VMEM] * (1 + len(others)) + [ANY] * len(deps),
        out_specs=VMEM,
        compiler_params=params(),
        cost_estimate=cost(keep.size, 6 * keep.size),
        name="sum_cores",
    )(keep, *others, *deps)


def pointwise_kernel(n_other, sum_ref, *rest):
    others, (hidden_ref, gate_ref, up_ref, tok_ref) = rest[:n_other], rest[-4:]
    rows = hidden_ref.shape[0]
    tok_ref[...] = jnp.zeros_like(tok_ref)

    def step(here):
        total = [sum_ref[k, here, :].astype(F32) for k in range(3)]
        for other in others:
            total = [total[k] + other[k, here, :].astype(F32) for k in range(3)]
        gate_pre, up_pre, hidden_grad = total
        sigmoid_gate = jax.nn.sigmoid(gate_pre)
        active = gate_pre * sigmoid_gate
        hidden_ref[here, :] = (active * up_pre).astype(BF)
        gate_ref[here, :] = (
            hidden_grad * up_pre * sigmoid_gate * (1.0 + gate_pre * (1.0 - sigmoid_gate))
        ).astype(BF)
        up_ref[here, :] = (hidden_grad * active).astype(BF)

    if rows == 16:
        step(pl.ds(0, rows))
    else:

        @pl.loop(0, rows // 16)
        def _(i):
            step(pl.ds(pl.multiple_of(i * 16, 16), 16))


def pointwise(chip_sum, others, deps):
    return pl.pallas_call(
        functools.partial(pointwise_kernel, len(others)),
        out_shape=(*[jax.ShapeDtypeStruct(chip_sum.shape[1:], BF)] * 3, TOKEN),
        in_specs=[VMEM] * (1 + len(others)) + [ANY] * len(deps),
        out_specs=[VMEM] * 4,
        compiler_params=params(),
        cost_estimate=cost(20 * chip_sum.size, 6 * chip_sum.size),
        name="pointwise",
    )(chip_sum, *others, *deps)


def grad_tokens_kernel(offsets, weight_offset, span, own, n_out, prev_ref, wg_ref, wu_ref, *rest):
    n = len(offsets)
    gates, ups, (*outs, tok_ref) = rest[:n], rest[n : 2 * n], rest[-1 - n_out :]
    tok_ref[...] = jnp.zeros_like(tok_ref)
    here = pl.ds(weight_offset, span)
    gate_act = jnp.concatenate([p[:, s : s + span] for p, s in zip(gates, offsets)], axis=0)
    up_act = jnp.concatenate([p[:, s : s + span] for p, s in zip(ups, offsets)], axis=0)
    add = dot_nt(gate_act, wg_ref[:, here]) + dot_nt(up_act, wu_ref[:, here])
    if prev_ref is not None:
        add += prev_ref[...]
    if not own:
        outs[0][...] = add
        return
    half = own // 2
    blocks = outs[0].shape[0] // own
    outs[1][...] = add[:own]
    add = add.astype(BF)
    for b in range(blocks):
        for h in range(2):
            start = own + (h * blocks + b) * half
            outs[0][pl.ds(b * own + h * half, half), :] = add[start : start + half]


def grad_tokens_of(prev, wg, wu, weight_offset, parts, offsets, span, own, deps):
    rows = sum(p[1].shape[0] for p in parts)
    feats = wg.shape[0]
    outs = [jax.ShapeDtypeStruct((rows, feats), F32)]
    if own:
        outs = [jax.ShapeDtypeStruct((rows - own, feats), BF), jax.ShapeDtypeStruct((own, feats), F32)]
    kernel = functools.partial(grad_tokens_kernel, offsets, weight_offset, span, own, len(outs))
    prevs = (prev,)
    if prev is None:
        kernel, prevs = functools.partial(kernel, None), ()
    return pl.pallas_call(
        kernel,
        out_shape=(*outs, TOKEN),
        in_specs=[VMEM] * (len(prevs) + 2 + 2 * len(parts)) + [ANY] * len(deps),
        out_specs=[VMEM] * (1 + len(outs)),
        compiler_params=params(),
        cost_estimate=cost(4 * rows * feats * span, 4 * feats * span),
        name="grad_tokens",
    )(*prevs, in_vmem(wg), in_vmem(wu), *[p[1] for p in parts], *[p[2] for p in parts], *deps)


def weight_grads_kernel(n, granule, xt_ref, og_ref, gk_ref, uk_ref, dk_ref, *rest):
    gate_ref, up_ref, down_ref, tok_ref = rest[-4:]
    tok_ref[...] = jnp.zeros_like(tok_ref)
    hidden, gate_act, up_act = [
        jnp.concatenate([p[...] for p in rest[k * n : (k + 1) * n]], axis=0) for k in range(3)
    ]
    for act, keep, out_ref in ((gate_act, gk_ref, gate_ref), (up_act, uk_ref, up_ref)):
        value = jnp.dot(xt_ref[...], act, preferred_element_type=F32).astype(BF)
        out_ref[...] = mask_rows(value, keep[...], BLK)
    down_ref[...] = mask_rows(dot_tn(hidden, og_ref[...]).astype(BF), dk_ref[...], granule)


def weight_grads(prev, xt, og, gk, uk, dk, weight_start, parts, starts, first, tiles, tile, units, granule, deps):
    feats, rows = xt.shape
    span = tiles * tile
    n_prev = 0 if prev is None else 3
    base = 5 + 3 * len(parts)

    def moved(s, i):
        return (0, s + i)

    return pl.pallas_call(
        functools.partial(weight_grads_kernel, len(parts), granule),
        out_shape=(
            pltpu.HBM((feats, units), BF),
            pltpu.HBM((feats, units), BF),
            pltpu.HBM((units, feats), BF),
            TOKEN,
        ),
        grid=(tiles,),
        in_specs=[
            pl.BlockSpec((feats, rows), lambda i: (0, 0)),
            pl.BlockSpec((rows, feats), lambda i: (0, 0)),
            pl.BlockSpec((gk.shape[0], tile), lambda i: (0, weight_start + i)),
            pl.BlockSpec((uk.shape[0], tile), lambda i: (0, weight_start + i)),
            pl.BlockSpec((tile // granule * LANE, feats), lambda i: (weight_start + i, 0)),
        ]
        + [pl.BlockSpec((p[0].shape[0], tile), functools.partial(moved, s)) for p, s in zip(parts, starts)] * 3
        + [ANY] * (n_prev + len(deps)),
        out_specs=[
            pl.BlockSpec((feats, tile), lambda i: (0, first + i)),
            pl.BlockSpec((feats, tile), lambda i: (0, first + i)),
            pl.BlockSpec((tile, feats), lambda i: (first + i, 0)),
            pl.BlockSpec((8, 128), lambda i: (0, 0)),
        ],
        input_output_aliases={base + k: k for k in range(n_prev)},
        compiler_params=params(16),
        cost_estimate=cost(6 * rows * feats * span, 6 * feats * span),
        name="weight_grads",
    )(xt, og, gk, uk, dk, *[p[k] for k in range(3) for p in parts], *(() if prev is None else map(in_hbm, prev)), *deps)


def finish_kernel(place, own_ref, *rest):
    arrived, out_ref = rest[:-1], rest[-1]
    total = own_ref[...]
    for piece in arrived:
        total += piece[...].astype(F32)
    out_ref[...] = both_halves([total.astype(BF)], total.shape[0] // 2, place[2] > 0)


def finish(place, own, arrived):
    return pl.pallas_call(
        finish_kernel,
        out_shape=jax.ShapeDtypeStruct(own.shape, BF),
        in_specs=[SMEM] + [VMEM] * (1 + len(arrived)),
        out_specs=VMEM,
        compiler_params=params(),
        cost_estimate=cost(4 * own.size, 8 * own.size),
        name="finish",
    )(place, own, *arrived)


def chunks_of(tiles, sizes):
    out, first = [], 0
    for size in sizes:
        size = min(size, tiles - first)
        if size > 0:
            out.append((first, size))
            first += size
    if first < tiles:
        out.append((first, tiles - first))
    return out


def local(n_row, n_col, tokens, out_grad, gate_w, up_w, down_w, gate_mask, up_mask, down_mask):
    rank_row, rank_col = lax.axis_index("row"), lax.axis_index("col")
    own, feats = tokens.shape
    units = gate_w.shape[1]
    half = own // 2
    n_chip = n_col // 2
    tile = TILE if units % TILE == 0 else units
    tiles = units // tile
    granule = gcd_of(units, BLK)
    core_swap = [(i, i ^ 1) for i in range(n_col)]

    def swap_cores(values):
        return [lax.ppermute(value, "col", core_swap) for value in values]

    def flipped(value, d):
        return lax.ppermute(value, "row", [(i, i ^ d) for i in range(n_row)])

    def from_chips(value):
        return [
            lax.ppermute(value, "col", [(i, (i + 2 * d) % n_col) for i in range(n_col)])
            for d in range(1, n_chip)
        ]

    both = jnp.stack([tokens, out_grad])
    if n_row == 4:
        two = flipped(both, 2)
        far = [flipped(both, 1), two, flipped(two, 1)]
    else:
        whole = lax.all_gather(both, "row", axis=1, tiled=True)
        wanted = [rank_row ^ d for d in range(1, n_row)]
        far = [jnp.concatenate([lax.dynamic_slice_in_dim(whole, w * own, own, 1) for w in wanted], axis=1)]

    place = jnp.stack([rank_col * (feats // BLK), rank_row * units, rank_col % 2]).astype(jnp.int32)
    masks = (gate_mask, up_mask, down_mask.T)

    own_chunks = chunks_of(tiles, OWN_CHUNKS)
    far_chunks = chunks_of(tiles, FAR_CHUNKS)

    def group_of(first):
        for g, (f, s) in enumerate(own_chunks):
            if f <= first < f + s:
                return g, first - f

    groups, own_sums, own_others, keeps, deps = [], [], [], None, ()
    for c, (first, size) in enumerate(own_chunks):
        pieces = OWN_PIECES[min(c, len(OWN_PIECES) - 1)]
        keep, send, group, keeps = open_weights(
            place, both, gate_w, up_w, down_w, masks, keeps, first, size, tile, granule, pieces, deps
        )
        groups.append(group)
        own_sums.append(sum_of(keep, swap_cores(send), pieces, ()))
        own_others.append(from_chips(own_sums[-1]))
        deps = (own_sums[-1],)

    x_all, xt_all, og_all, tok = all_tokens(place, both, far, deps)
    deps = (tok,)
    far_sums, far_others, own_parts, waiting = [], [], [], None

    def open_own(c, deps):
        *mine, tok = pointwise(own_sums[c], own_others[c], deps)
        own_parts.append((mine, swap_cores(mine)))
        return (tok,)

    for first, size in far_chunks:
        g, offset = group_of(first)
        keep, send, tok = forward(x_all, og_all, own, *groups[g], offset * tile, size * tile, FAR_PIECES, deps)
        deps = (tok,)
        if waiting is not None:
            far_sums.append(sum_of(*waiting, FAR_PIECES, far_sums[-1:]))
            far_others.append(from_chips(far_sums[-1]))
            deps += (far_sums[-1],)
        waiting = (keep, swap_cores(send))
        if len(own_parts) < len(own_chunks) and len(far_sums) >= OWN_AFTER[len(own_parts)]:
            deps = open_own(len(own_parts), deps)
    far_sums.append(sum_of(*waiting, FAR_PIECES, far_sums[-1:]))
    far_others.append(from_chips(far_sums[-1]))

    deps = (far_sums[-1],)
    while len(own_parts) < len(own_chunks):
        deps = open_own(len(own_parts), deps)

    grads, gt, pending = None, None, []

    def flush(grads, work, deps):
        first, size, g, offset, parts, starts = work
        *grads, tok = weight_grads(
            grads, xt_all, og_all, *keeps, first, parts, starts, first, size, tile, units, granule, deps
        )
        return grads, (tok,)

    for c, (first, size) in enumerate(far_chunks):
        g, offset = group_of(first)
        *mine, tok = pointwise(far_sums[c], far_others[c], deps)
        deps = (tok,)
        parts = (*own_parts[g], mine, swap_cores(mine))
        last = c == len(far_chunks) - 1
        if pending:
            grads, deps = flush(grads, pending.pop(0), deps)
        offsets = (offset * tile, offset * tile, 0, 0)
        gt, *rest, tok = grad_tokens_of(
            gt, *groups[g][:2], offset * tile, parts, offsets, size * tile, own if last else 0, deps
        )
        deps = (tok,)
        pending.append((first, size, g, offset, parts, (offset, offset, 0, 0)))
    for work in pending:
        grads, deps = flush(grads, work, deps)

    if n_row == 4:
        arrived = [flipped(gt[(d - 1) * own : d * own], d) for d in range(1, n_row)]
    else:
        blocks = jnp.concatenate([rest[0].astype(BF), gt], axis=0).reshape(n_row, own, feats)
        wanted = [rank_row ^ b for b in range(n_row)]
        by_row = jnp.concatenate([lax.dynamic_slice_in_dim(blocks, w, 1, 0) for w in wanted], axis=0)
        arrived = [lax.psum_scatter(by_row.reshape(n_row * own, feats), "row", scatter_dimension=0, tiled=True)]
        rest = [jnp.zeros_like(rest[0])]
    return (finish(place, rest[0], arrived), *grads)


def solution(mesh):
    in_specs = (
        P(("groups", "row"), "col"),
        P(("groups", "row"), "col"),
        P(("groups", "col"), "row"),
        P(("groups", "col"), "row"),
        P(("groups", "row"), "col"),
        P("groups", None),
        P("groups", None),
        P("groups", None),
    )
    out_specs = (
        P(("groups", "row"), "col"),
        P(("groups", "col"), "row"),
        P(("groups", "col"), "row"),
        P(("groups", "row"), "col"),
    )
    step = functools.partial(local, mesh.shape["row"], mesh.shape["col"])
    return jax.shard_map(step, mesh=mesh, in_specs=in_specs, out_specs=out_specs, check_vma=False)
```

time: 84.7 us -> 79 us (0.933)
  waiting for transfers between devices: 16.6 us -> 8.68 us
  Pallas kernels: 37.9 us -> 41.8 us
  local copies, waits for them, and re-layouts: 3.87 us -> 0.02 us
  starting transfers between devices: 24 us -> 26.4 us
    ppermute x6, waiting for transfers between devices: 6.63 us -> 1.6 us  [flipped(): return lax.ppermute(value, 'row', [(i, i ^ d) for i in range(n_row)])]
    pallas_call x18 -> x21, Pallas kernels: 36.4 us -> 40.3 us  [the longest x2 15 us: open_weights(): pl.pallas_call(functools.partial(open_kernel, len(deps), pieces, opener,...]
    unnamed x14 -> x0, local copies, waits for them, and re-layouts: 3.84 us -> none
    ppermute x5 -> x6, waiting for transfers between devices: 6.65 us -> 3.19 us  [from_chips(): lax.ppermute(value, 'col', [(i, (i + 2 * d) % n_col) for i in range(n_col)])]
    ppermute x5 -> x6, starting transfers between devices: 5.12 us -> 7.3 us  [from_chips(): lax.ppermute(value, 'col', [(i, (i + 2 * d) % n_col) for i in range(n_col)])]
    ppermute x30 -> x35, starting transfers between devices: 7.22 us -> 8.53 us  [swap_cores(): return [lax.ppermute(value, 'col', core_swap) for value in values]]
    ppermute x6, starting transfers between devices: 11.7 us -> 10.6 us  [flipped(): return lax.ppermute(value, 'row', [(i, i ^ d) for i in range(n_row)])]
    another operation x1, other arithmetic: 0.01 us -> 0.89 us  [local(): both = jnp.stack([tokens, out_grad])]
  transfers between devices with their start and end apart: 41 -> 47, of which waited for: 13 -> 7; matrix products, arithmetic and copies ran while one was open for 0% -> 0% of each run, Pallas kernels for 30% -> 51%
where the time goes in v3:
time: 79 us; the launch traced here: 78.7 us
  Pallas kernels  41.8 us (53%)
  starting transfers between devices  26.4 us (33%)
  waiting for transfers between devices  8.68 us (11%)
  other arithmetic  0.96 us (1%)
  between operations  0.89 us (1%)
    pallas_call x2, Pallas kernels, open_weights(): pl.pallas_call(functools.partial(open_kernel, len(deps), pieces, opener,...  15 us
    pallas_call x4, Pallas kernels, weight_grads(): pl.pallas_call(functools.partial(weight_grads_kernel, len(parts), granule...  13 us
    ppermute x6, starting transfers between devices, flipped(): return lax.ppermute(value, 'row', [(i, i ^ d) for i in range(n_row)])  10.6 us
    ppermute x35, starting transfers between devices, swap_cores(): return [lax.ppermute(value, 'col', core_swap) for value in values]  8.53 us
    ppermute x6, starting transfers between devices, from_chips(): lax.ppermute(value, 'col', [(i, (i + 2 * d) % n_col) for i in range(n_col)])  7.3 us
    pallas_call x4, Pallas kernels, forward(): pl.pallas_call(functools.partial(forward_kernel, pieces, own, offset, spa...  5.53 us
    pallas_call x4, Pallas kernels, grad_tokens_of(): pl.pallas_call(kernel, out_shape=(*outs, TOKEN), in_specs=[VMEM] * (len(p...  5.28 us
    ppermute x35, waiting for transfers between devices, swap_cores(): return [lax.ppermute(value, 'col', core_swap) for value in values]  3.89 us
  transfers between devices with their start and end apart: 47, of which 7 were waited for; matrix products, arithmetic and copies ran while one was open for 0% of the time, Pallas kernels for 51%

profile of v3, /device:TPU:0, one launch (start us, length us, event | category | flops | bytes accessed | tf_op | source)
XLA Modules:
  0.0 78.7 jit_solution(13345647465543833340)
XLA Ops:
  0.6 0.9 %pad_maximum_fusion.both_ref = bf16[2,32,1024]{2,1,0:T(8,128)(2,1)S(1)} fusion(bf16[1,32,1024]{2,1,0:T(8,128)(2,1)} %bitcast.6, bf16[1,32,1024]{2,1,0:T(8,128)(2,1)} %bitcast.7), kind=kLoop, calls=%fused_computation | loop fusion | flops 65536 | bytes 262144 | tf_op jit(solution)/shard_map/stack | solution.py:485
  1.5 4.1 %collective-permute-start.5 = (bf16[2,32,1024]{2,1,0:T(8,128)(2,1)S(1)}, bf16[2,32,1024]{2,1,0:T(8,128)(2,1)S(1)}, u32[]{:S(2)}, u32[]{:S(2)}) collective-permute-start(bf16[2,32,1024]{2,1,0:T(8,128)(2,1)S(1)} %pad_maximum_fusion.both_ref), channel_id=1, source_target_pairs={{0,8},{4,12},{8,0},{12,4},{1,9},{5,13},{9,1},{13,5},{2,10},{6,14},... | collective-permute-start | bytes 393224 | tf_op jit(solution)/shard_map/ppermute | solution.py:477
  5.7 9.5 %open_weights.2 = (bf16[3,16,2048]{2,1,0:T(8,128)(2,1)S(1)}, bf16[1,16,2048]{2,1,0:T(8,128)(2,1)S(1)}, bf16[1,16,2048]{2,1,0:T(8,128)(2,1)S(1)}, bf16[1,16,2048]...) custom-call(s32[3]{0:T(128)S(1)} %pad_add_fusion.place, ...), custom_call_target="tpu_custom_call" | custom-call | tf_op jit(solution)/shard_map/open_weights/pallas_call | solution.py:183
  15.3 0.5 collective-permute-start.1
  15.8 1.6 %collective-permute-start.4 = (bf16[2,32,1024]{2,1,0:T(8,128)(2,1)S(1)}, bf16[2,32,1024]{2,1,0:T(8,128)(2,1)S(1)}, u32[]{:S(2)}, u32[]{:S(2)}) collective-permute-start(bf16[2,32,1024]{2,1,0:T(8,128)(2,1)S(1)} %pad_maximum_fusion.both_ref), channel_id=1, source_target_pairs={{0,4},{4,0},{8,12},{12,8},{1,5},{5,1},{9,13},{13,9},{2,6},{6,2},{1... | collective-permute-start | bytes 393224 | tf_op jit(solution)/shard_map/ppermute | solution.py:477
  17.4 0.4 collective-permute-start.6
  17.9 1.6 %collective-permute-start.3 = (bf16[3,16,2048]{2,1,0:T(8,128)(2,1)S(1)}, bf16[3,16,2048]{2,1,0:T(8,128)(2,1)S(1)}, u32[]{:S(2)}, u32[]{:S(2)}) collective-permute-start(bf16[3,16,2048]{2,1,0:T(8,128)(2,1)S(1)} %sum_cores.6.rest_3_.sum_ref), channel_id=1, source_target_pairs={{0,2},{1,3},{2,0},{3,1},{4,6},{5,7},{6,4},{7,5},{8,10},{9,11},{10,... | collective-permute-start | bytes 589832 | tf_op jit(solution)/shard_map/ppermute | solution.py:481
  19.5 5.5 %open_weights.3 = (bf16[3,16,1536]{2,1,0:T(8,128)(2,1)S(1)}, bf16[2,16,1536]{2,1,0:T(8,128)(2,1)S(1)}, bf16[1,16,1536]{2,1,0:T(8,128)(2,1)S(1)}, bf16[1024,1536]...) custom-call(s32[3]{0:T(128)S(1)} %pad_add_fusion.place, ...), custom_call_target="tpu_custom_call" | custom-call | tf_op jit(solution)/shard_map/open_weights/pallas_call | solution.py:183
  25.1 0.5 collective-permute-start.8
  25.6 0.9 %collective-permute-done.8.rest_1_ = bf16[1,16,1536]{2,1,0:T(8,128)(2,1)S(1)} collective-permute-done((bf16[1,16,1536]{2,1,0:T(8,128)(2,1)S(1)}, bf16[1,16,1536]{2,1,0:T(8,128)(2,1)S(1)}, u32[]{:S(2)}, u32[]{:S(2)}) %collective-permute-start.8) | collective-permute-done | bytes 49184 | tf_op jit(solution)/shard_map/ppermute | solution.py:474
  26.5 0.7 all_tokens.1
  27.2 1.4 %forward.4 = (bf16[3,48,1024]{2,1,0:T(8,128)(2,1)S(1)}, bf16[1,48,1024]{2,1,0:T(8,128)(2,1)S(1)}, bf16[1,48,1024]{2,1,0:T(8,128)(2,1)S(1)}, bf16[1,48,1024]{2,1,0:T(8,128)(2,1)S(1)}, f32[8,128]{1,0:T(8,128)S(1)}) custom-call(bf16[128,1024]{1,0:T(8,128)(2,1)S(1)} %get-tuple-element.103.x_ref, bf16[128,1024]{1,0:T(8,128)(2,1)S(1)} %get-tuple-element.104.og_ref, ...), custom_call_target="tpu_custom_call" | custom-call | tf_op jit(solution)/shard_map/forward/pallas_call | solution.py:226
  28.7 0.4 collective-permute-start.10
  29.2 0.3 collective-permute-start.12
  29.6 0.5 collective-permute-start.14
  30.2 1.4 %forward.5 = (bf16[3,48,1024]{2,1,0:T(8,128)(2,1)S(1)}, bf16[1,48,1024]{2,1,0:T(8,128)(2,1)S(1)}, bf16[1,48,1024]{2,1,0:T(8,128)(2,1)S(1)}, bf16[1,48,1024]{2,1,0:T(8,128)(2,1)S(1)}, f32[8,128]{1,0:T(8,128)S(1)}) custom-call(bf16[128,1024]{1,0:T(8,128)(2,1)S(1)} %get-tuple-element.103.x_ref, bf16[128,1024]{1,0:T(8,128)(2,1)S(1)} %get-tuple-element.104.og_ref, ...), custom_call_target="tpu_custom_call" | custom-call | tf_op jit(solution)/shard_map/forward/pallas_call | solution.py:226
  31.8 0.5 collective-permute-start.16
  32.3 1.6 %collective-permute-start.13 = (bf16[3,48,1024]{2,1,0:T(8,128)(2,1)S(1)}, bf16[3,48,1024]{2,1,0:T(8,128)(2,1)S(1)}, u32[]{:S(2)}, u32[]{:S(2)}) collective-permute-start(bf16[3,48,1024]{2,1,0:T(8,128)(2,1)S(1)} %sum_cores.8.rest_1_.rest_3_.sum_ref), channel_id=1, source_target_pairs={{0,2},{1,3},{2,0},{3,1},{4,6},{5,7},{6,4},{7,5},{8,10},{9,11},{10,... | collective-permute-start | bytes 884744 | tf_op jit(solution)/shard_map/ppermute | solution.py:481
  33.9 1.4 %forward.6 = (bf16[3,48,1024]{2,1,0:T(8,128)(2,1)S(1)}, bf16[1,48,1024]{2,1,0:T(8,128)(2,1)S(1)}, bf16[1,48,1024]{2,1,0:T(8,128)(2,1)S(1)}, bf16[1,48,1024]{2,1,0:T(8,128)(2,1)S(1)}, f32[8,128]{1,0:T(8,128)S(1)}) custom-call(bf16[128,1024]{1,0:T(8,128)(2,1)S(1)} %get-tuple-element.103.x_ref, bf16[128,1024]{1,0:T(8,128)(2,1)S(1)} %get-tuple-element.104.og_ref, ...), custom_call_target="tpu_custom_call" | custom-call | tf_op jit(solution)/shard_map/forward/pallas_call | solution.py:226
  35.3 0.6 collective-permute-start.21
  36.1 0.6 collective-permute-start.27
  36.9 1.2 %forward.7 = (bf16[3,48,512]{2,1,0:T(8,128)(2,1)S(1)}, bf16[1,48,512]{2,1,0:T(8,128)(2,1)S(1)}, bf16[1,48,512]{2,1,0:T(8,128)(2,1)S(1)}, bf16[1,48,512]{2,1,0:T(8,128)(2,1)S(1)}, f32[8,128]{1,0:T(8,128)}) custom-call(bf16[128,1024]{1,0:T(8,128)(2,1)S(1)} %get-tuple-element.103.x_ref, bf16[128,1024]{1,0:T(8,128)(2,1)S(1)} %get-tuple-element.104.og_ref, ...), custom_call_target="tpu_custom_call" | custom-call | tf_op jit(solution)/shard_map/forward/pallas_call | solution.py:226
  38.1 0.4 collective-permute-start.18
  38.7 1.6 %collective-permute-start.33 = (bf16[3,48,1024]{2,1,0:T(8,128)(2,1)S(1)}, bf16[3,48,1024]{2,1,0:T(8,128)(2,1)S(1)}, u32[]{:S(2)}, u32[]{:S(2)}) collective-permute-start(bf16[3,48,1024]{2,1,0:T(8,128)(2,1)S(1)} %sum_cores.10.rest_3_.sum_ref), channel_id=1, source_target_pairs={{0,2},{1,3},{2,0},{3,1},{4,6},{5,7},{6,4},{7,5},{8,10},{9,11},{10,... | collective-permute-start | bytes 884744 | tf_op jit(solution)/shard_map/ppermute | solution.py:481
  40.4 0.4 collective-permute-start.20
  40.8 0.9 %collective-permute-done.20.rest_2_ = bf16[1,48,512]{2,1,0:T(8,128)(2,1)S(1)} collective-permute-done((bf16[1,48,512]{2,1,0:T(8,128)(2,1)S(1)}, bf16[1,48,512]{2,1,0:T(8,128)(2,1)S(1)}, u32[]{:S(2)}, u32[]{:S(2)}) %collective-permute-start.20) | collective-permute-done | bytes 49184 | tf_op jit(solution)/shard_map/ppermute | solution.py:474
  41.7 0.5 collective-permute-done.13.rest_0_
  42.5 0.5 collective-permute-start.9
  43.1 0.8 %collective-permute-done.9.rest_1_.rest_5_ = bf16[16,2048]{1,0:T(8,128)(2,1)S(1)} collective-permute-done((bf16[16,2048]{1,0:T(8,128)(2,1)S(1)}, bf16[16,2048]{1,0:T(8,128)(2,1)S(1)}, u32[]{:S(2)}, u32[]{:S(2)}) %collective-permute-start.9) | collective-permute-done | bytes 65568 | tf_op jit(solution)/shard_map/ppermute | solution.py:474
  43.9 0.4 collective-permute-start.31
  44.4 1.5 %grad_tokens.4 = (f32[128,1024]{1,0:T(8,128)S(1)}, f32[8,128]{1,0:T(8,128)S(1)}) custom-call(bf16[1024,2048]{1,0:T(8,128)(2,1)S(1)} %get-tuple-element.91.wg_ref, bf16[1024,2048]{1,0:T(8,128)(2,1)S(1)} %get-tuple-element.92.wu_ref, bf16[16,2048]{1,0:T(8,128)(2,1)S(1)} %get-tuple-element.108.rest_0_.rest_4_, ...), custom_call_target="tpu_custom_call" | custom-call | tf_op jit(solution)/shard_map/grad_tokens/pallas_call | solution.py:367
  45.9 2.6 %collective-permute-done.27.rest_0_ = bf16[3,48,1024]{2,1,0:T(8,128)(2,1)S(1)} collective-permute-done((bf16[3,48,1024]{2,1,0:T(8,128)(2,1)S(1)}, bf16[3,48,1024]{2,1,0:T(8,128)(2,1)S(1)}, u32[]{:S(2)}, u32[]{:S(2)}) %collective-permute-start.27) | collective-permute-done | bytes 294944 | tf_op jit(solution)/shard_map/ppermute | solution.py:481
  48.8 0.5 collective-permute-start.29
  49.4 1.5 %collective-permute-start.38 = (bf16[3,48,512]{2,1,0:T(8,128)(2,1)S(1)}, bf16[3,48,512]{2,1,0:T(8,128)(2,1)S(1)}, u32[]{:S(2)}, u32[]{:S(2)}) collective-permute-start(bf16[3,48,512]{2,1,0:T(8,128)(2,1)S(1)} %sum_cores.11.rest_1_.sum_ref), channel_id=1, source_target_pairs={{0,2},{1,3},{2,0},{3,1},{4,6},{5,7},{6,4},{7,5},{8,10},{9,11},{10,... | collective-permute-start | bytes 442376 | tf_op jit(solution)/shard_map/ppermute | solution.py:481
  50.9 3.6 %weight_grads.4 = (bf16[1024,3584]{1,0:T(8,128)(2,1)}, bf16[1024,3584]{1,0:T(8,128)(2,1)}, bf16[3584,1024]{1,0:T(8,128)(2,1)}, f32[8,128]{1,0:T(8,128)S(1)}) custom-call(bf16[1024,128]{1,0:T(8,128)(2,1)S(1)} %get-tuple-element.140.xt_ref, bf16[128,1024]{1,0:T(8,128)(2,1)S(1)} %get-tuple-element.104.og_ref, ...), custom_call_target="tpu_custom_call" | custom-call | tf_op jit(solution)/shard_map/weight_grads/pallas_call | solution.py:399
  54.7 1.5 %grad_tokens.5 = (f32[128,1024]{1,0:T(8,128)S(1)}, f32[8,128]{1,0:T(8,128)S(1)}) custom-call(f32[128,1024]{1,0:T(8,128)S(1)} %get-tuple-element.136.prev_ref, bf16[1024,2048]{1,0:T(8,128)(2,1)S(1)} %get-tuple-element.91.wg_ref, bf16[1024,2048]{1,0:T(8,128)(2,1)S(1)} %get-tuple-element.92.wu_ref, bf16[16,2048]{1,0:T(8,128)(2,1)S(1)} %get-tuple-element.108.rest_0_.rest_4_, ...), custom_call_target="tpu_custom_call" | custom-call | tf_op jit(solution)/shard_map/grad_tokens/pallas_call | solution.py:367
  56.4 0.4 collective-permute-start.34
  57.5 3.6 %weight_grads.5 = (bf16[1024,3584]{1,0:T(8,128)(2,1)}, bf16[1024,3584]{1,0:T(8,128)(2,1)}, bf16[3584,1024]{1,0:T(8,128)(2,1)}, f32[8,128]{1,0:T(8,128)S(1)}) custom-call(bf16[1024,128]{1,0:T(8,128)(2,1)S(1)} %get-tuple-element.140.xt_ref, ...), custom_call_target="tpu_custom_call", output_to_operand_aliasing={{0}: (17, {}), {1}: (18, {}), {2}: (19, {})} | custom-call | tf_op jit(solution)/shard_map/weight_grads/pallas_call | solution.py:399
  61.1 0.3 collective-permute-start.41
  61.4 1.5 %grad_tokens.6 = (f32[128,1024]{1,0:T(8,128)S(1)}, f32[8,128]{1,0:T(8,128)S(1)}) custom-call(f32[128,1024]{1,0:T(8,128)S(1)} %get-tuple-element.145.prev_ref, bf16[1024,1536]{1,0:T(8,128)(2,1)S(1)} %get-tuple-element.113.wg_ref, bf16[1024,1536]{1,0:T(8,128)(2,1)S(1)} %get-tuple-element.114.wu_ref, bf16[16,1536]{1,0:T(8,128)(2,1)S(1)} %get-tuple-element.146.rest_0_.rest_4_, ...), custom_call_target="tpu_custom_call" | custom-call | tf_op jit(solution)/shard_map/grad_tokens/pallas_call | solution.py:367
  63.6 3.6 %weight_grads.6 = (bf16[1024,3584]{1,0:T(8,128)(2,1)}, bf16[1024,3584]{1,0:T(8,128)(2,1)}, bf16[3584,1024]{1,0:T(8,128)(2,1)}, f32[8,128]{1,0:T(8,128)S(1)}) custom-call(bf16[1024,128]{1,0:T(8,128)(2,1)S(1)} %get-tuple-element.140.xt_ref, ...), custom_call_target="tpu_custom_call", output_to_operand_aliasing={{0}: (17, {}), {1}: (18, {}), {2}: (19, {})} | custom-call | tf_op jit(solution)/shard_map/weight_grads/pallas_call | solution.py:399
  67.2 0.8 %grad_tokens.7 = (bf16[96,1024]{1,0:T(8,128)(2,1)S(1)}, f32[32,1024]{1,0:T(8,128)S(1)}, f32[8,128]{1,0:T(8,128)S(1)}) custom-call(f32[128,1024]{1,0:T(8,128)S(1)} %get-tuple-element.157.prev_ref, bf16[1024,1536]{1,0:T(8,128)(2,1)S(1)} %get-tuple-element.113.wg_ref, bf16[1024,1536]{1,0:T(8,128)(2,1)S(1)} %get-tuple-element.114.wu_ref, ...), custom_call_target="tpu_custom_call" | custom-call | tf_op jit(solution)/shard_map/grad_tokens/pallas_call | solution.py:367
  68.0 1.6 %collective-permute-start.43 = (bf16[32,1024]{1,0:T(8,128)(2,1)S(1)}, bf16[32,1024]{1,0:T(8,128)(2,1)S(1)}, u32[]{:S(2)}, u32[]{:S(2)}) collective-permute-start(bf16[32,1024]{1,0:T(8,128)(2,1)S(1)} %get-tuple-element.180), channel_id=1, source_target_pairs={{0,4},{4,0},{8,12},{12,8},{1,5},{5,1},{9,13},{13,9},{2,6},{6,2},{1... | collective-permute-start | bytes 196616 | tf_op jit(solution)/shard_map/ppermute | solution.py:477
  70.0 2.5 %collective-permute-start.45 = (bf16[32,1024]{1,0:T(8,128)(2,1)S(1)}, bf16[32,1024]{1,0:T(8,128)(2,1)S(1)}, u32[]{:S(2)}, u32[]{:S(2)}) collective-permute-start(bf16[32,1024]{1,0:T(8,128)(2,1)S(1)} %get-tuple-element.178), channel_id=1, source_target_pairs={{0,12},{4,8},{8,4},{12,0},{1,13},{5,9},{9,5},{13,1},{2,14},{6,10},... | collective-permute-start | bytes 196616 | tf_op jit(solution)/shard_map/ppermute | solution.py:477
  72.5 1.2 %collective-permute-done.46.rest_3_ = bf16[48,512]{1,0:T(8,128)(2,1)S(1)} collective-permute-done((bf16[48,512]{1,0:T(8,128)(2,1)S(1)}, bf16[48,512]{1,0:T(8,128)(2,1)S(1)}, u32[]{:S(2)}, u32[]{:S(2)}) %collective-permute-start.46) | collective-permute-done | bytes 49184 | tf_op jit(solution)/shard_map/ppermute | solution.py:474
  73.7 2.2 %weight_grads.7 = (bf16[1024,3584]{1,0:T(8,128)(2,1)}, bf16[1024,3584]{1,0:T(8,128)(2,1)}, bf16[3584,1024]{1,0:T(8,128)(2,1)}, f32[8,128]{1,0:T(8,128)}) custom-call(bf16[1024,128]{1,0:T(8,128)(2,1)S(1)} %get-tuple-element.140.xt_ref, bf16[128,1024]{1,0:T(8,128)(2,1)S(1)} %get-tuple-element.104.og_ref, ...), custom_call_target="tpu_custom_call", output_to_operand_aliasing={{0}: (17, {}), {1}: (18, {}), {2}: (19, {})} | custom-call | tf_op jit(solution)/shard_map/weight_grads/pallas_call | solution.py:399
  75.9 1.6 %collective-permute-done.44.rest_1_ = bf16[32,1024]{1,0:T(8,128)(2,1)S(1)} collective-permute-done((bf16[32,1024]{1,0:T(8,128)(2,1)S(1)}, bf16[32,1024]{1,0:T(8,128)(2,1)S(1)}, u32[]{:S(2)}, u32[]{:S(2)}) %collective-permute-start.44) | collective-permute-done | bytes 65568 | tf_op jit(solution)/shard_map/ppermute | solution.py:477
  77.5 1.2 %finish.1 = bf16[32,1024]{1,0:T(8,128)(2,1)} custom-call(s32[3]{0:T(128)S(1)} %pad_add_fusion.place, f32[32,1024]{1,0:T(8,128)S(1)} %get-tuple-element.168.own_ref, bf16[32,1024]{1,0:T(8,128)(2,1)S(1)} %collective-permute-done.43.rest_0_, bf16[32,1024]{1,0:T(8,128)(2,1)S(1)} %collective-permute-done.44.rest_1_, ...), custom_call_target="tpu_custom_call" | custom-call | tf_op jit(solution)/shard_map/finish/pallas_call | solution.py:439
  (77 shorter events, 4.4 us)
Async XLA Ops:
  1.5 15.9 %collective-permute-start.5 = (bf16[2,32,1024]{2,1,0:T(8,128)(2,1)S(1)}, bf16[2,32,1024]{2,1,0:T(8,128)(2,1)S(1)}, u32[]{:S(2)}, u32[]{:S(2)}) collective-permute-start(bf16[2,32,1024]{2,1,0:T(8,128)(2,1)S(1)} %pad_maximum_fusion.both_ref), channel_id=1, source_target_pairs={{0,8},{4,12},{8,0},{12,4},{1,9},{5,13},{9,1},{13,5},{2,10},{6,14},... | collective-permute-start | bytes 393224 | tf_op jit(solution)/shard_map/ppermute | solution.py:477
  15.2 2.7 %collective-permute-start = (bf16[1,16,2048]{2,1,0:T(8,128)(2,1)S(1)}, bf16[1,16,2048]{2,1,0:T(8,128)(2,1)S(1)}, u32[]{:S(2)}, u32[]{:S(2)}) collective-permute-start(bf16[1,16,2048]{2,1,0:T(8,128)(2,1)S(1)} %get-tuple-element.94), channel_id=1, source_target_pairs={{0,1},{1,0},{2,3},{3,2},{4,5},{5,4},{6,7},{7,6},{8,9},{9,8},{10,11... | collective-permute-start | bytes 196616 | tf_op jit(solution)/shard_map/ppermute | solution.py:474
  15.3 2.6 %collective-permute-start.1 = (bf16[1,16,2048]{2,1,0:T(8,128)(2,1)S(1)}, bf16[1,16,2048]{2,1,0:T(8,128)(2,1)S(1)}, u32[]{:S(2)}, u32[]{:S(2)}) collective-permute-start(bf16[1,16,2048]{2,1,0:T(8,128)(2,1)S(1)} %get-tuple-element.95), channel_id=1, source_target_pairs={{0,1},{1,0},{2,3},{3,2},{4,5},{5,4},{6,7},{7,6},{8,9},{9,8},{10,11... | collective-permute-start | bytes 196616 | tf_op jit(solution)/shard_map/ppermute | solution.py:474
  15.7 2.1 %collective-permute-start.2 = (bf16[1,16,2048]{2,1,0:T(8,128)(2,1)S(1)}, bf16[1,16,2048]{2,1,0:T(8,128)(2,1)S(1)}, u32[]{:S(2)}, u32[]{:S(2)}) collective-permute-start(bf16[1,16,2048]{2,1,0:T(8,128)(2,1)S(1)} %get-tuple-element.96), channel_id=1, source_target_pairs={{0,1},{1,0},{2,3},{3,2},{4,5},{5,4},{6,7},{7,6},{8,9},{9,8},{10,11... | collective-permute-start | bytes 196616 | tf_op jit(solution)/shard_map/ppermute | solution.py:474
  15.8 10.7 %collective-permute-start.4 = (bf16[2,32,1024]{2,1,0:T(8,128)(2,1)S(1)}, bf16[2,32,1024]{2,1,0:T(8,128)(2,1)S(1)}, u32[]{:S(2)}, u32[]{:S(2)}) collective-permute-start(bf16[2,32,1024]{2,1,0:T(8,128)(2,1)S(1)} %pad_maximum_fusion.both_ref), channel_id=1, source_target_pairs={{0,4},{4,0},{8,12},{12,8},{1,5},{5,1},{9,13},{13,9},{2,6},{6,2},{1... | collective-permute-start | bytes 393224 | tf_op jit(solution)/shard_map/ppermute | solution.py:477
  17.4 9.1 %collective-permute-start.6 = (bf16[2,32,1024]{2,1,0:T(8,128)(2,1)S(1)}, bf16[2,32,1024]{2,1,0:T(8,128)(2,1)S(1)}, u32[]{:S(2)}, u32[]{:S(2)}) collective-permute-start(bf16[2,32,1024]{2,1,0:T(8,128)(2,1)S(1)} %collective-permute-done.5.rest_1_), channel_id=1, source_target_pairs={{0,4},{4,0},{8,12},{12,8},{1,5},{5,1},{9,13},{13,9},{2,6},{6,2},{1... | collective-permute-start | bytes 393224 | tf_op jit(solution)/shard_map/ppermute | solution.py:477
  17.9 12.2 %collective-permute-start.3 = (bf16[3,16,2048]{2,1,0:T(8,128)(2,1)S(1)}, bf16[3,16,2048]{2,1,0:T(8,128)(2,1)S(1)}, u32[]{:S(2)}, u32[]{:S(2)}) collective-permute-start(bf16[3,16,2048]{2,1,0:T(8,128)(2,1)S(1)} %sum_cores.6.rest_3_.sum_ref), channel_id=1, source_target_pairs={{0,2},{1,3},{2,0},{3,1},{4,6},{5,7},{6,4},{7,5},{8,10},{9,11},{10,... | collective-permute-start | bytes 589832 | tf_op jit(solution)/shard_map/ppermute | solution.py:481
  25.0 1.5 %collective-permute-start.7 = (bf16[2,16,1536]{2,1,0:T(8,128)(2,1)S(1)}, bf16[2,16,1536]{2,1,0:T(8,128)(2,1)S(1)}, u32[]{:S(2)}, u32[]{:S(2)}) collective-permute-start(bf16[2,16,1536]{2,1,0:T(8,128)(2,1)S(1)} %get-tuple-element.101), channel_id=1, source_target_pairs={{0,1},{1,0},{2,3},{3,2},{4,5},{5,4},{6,7},{7,6},{8,9},{9,8},{10,11... | collective-permute-start | bytes 294920 | tf_op jit(solution)/shard_map/ppermute | solution.py:474
  25.1 1.4 %collective-permute-start.8 = (bf16[1,16,1536]{2,1,0:T(8,128)(2,1)S(1)}, bf16[1,16,1536]{2,1,0:T(8,128)(2,1)S(1)}, u32[]{:S(2)}, u32[]{:S(2)}) collective-permute-start(bf16[1,16,1536]{2,1,0:T(8,128)(2,1)S(1)} %get-tuple-element.102), channel_id=1, source_target_pairs={{0,1},{1,0},{2,3},{3,2},{4,5},{5,4},{6,7},{7,6},{8,9},{9,8},{10,11... | collective-permute-start | bytes 147464 | tf_op jit(solution)/shard_map/ppermute | solution.py:474
  28.7 3.1 %collective-permute-start.10 = (bf16[1,48,1024]{2,1,0:T(8,128)(2,1)S(1)}, bf16[1,48,1024]{2,1,0:T(8,128)(2,1)S(1)}, u32[]{:S(2)}, u32[]{:S(2)}) collective-permute-start(bf16[1,48,1024]{2,1,0:T(8,128)(2,1)S(1)} %get-tuple-element.110), channel_id=1, source_target_pairs={{0,1},{1,0},{2,3},{3,2},{4,5},{5,4},{6,7},{7,6},{8,9},{9,8},{10,11... | collective-permute-start | bytes 294920 | tf_op jit(solution)/shard_map/ppermute | solution.py:474
  29.1 3.2 %collective-permute-start.11 = (bf16[1,48,1024]{2,1,0:T(8,128)(2,1)S(1)}, bf16[1,48,1024]{2,1,0:T(8,128)(2,1)S(1)}, u32[]{:S(2)}, u32[]{:S(2)}) collective-permute-start(bf16[1,48,1024]{2,1,0:T(8,128)(2,1)S(1)} %get-tuple-element.111), channel_id=1, source_target_pairs={{0,1},{1,0},{2,3},{3,2},{4,5},{5,4},{6,7},{7,6},{8,9},{9,8},{10,11... | collective-permute-start | bytes 294920 | tf_op jit(solution)/shard_map/ppermute | solution.py:474
  29.2 3.0 %collective-permute-start.12 = (bf16[1,48,1024]{2,1,0:T(8,128)(2,1)S(1)}, bf16[1,48,1024]{2,1,0:T(8,128)(2,1)S(1)}, u32[]{:S(2)}, u32[]{:S(2)}) collective-permute-start(bf16[1,48,1024]{2,1,0:T(8,128)(2,1)S(1)} %get-tuple-element.112), channel_id=1, source_target_pairs={{0,1},{1,0},{2,3},{3,2},{4,5},{5,4},{6,7},{7,6},{8,9},{9,8},{10,11... | collective-permute-start | bytes 294920 | tf_op jit(solution)/shard_map/ppermute | solution.py:474
  29.6 7.1 %collective-permute-start.14 = (bf16[3,16,1536]{2,1,0:T(8,128)(2,1)S(1)}, bf16[3,16,1536]{2,1,0:T(8,128)(2,1)S(1)}, u32[]{:S(2)}, u32[]{:S(2)}) collective-permute-start(bf16[3,16,1536]{2,1,0:T(8,128)(2,1)S(1)} %sum_cores.7.rest_3_.sum_ref), channel_id=1, source_target_pairs={{0,2},{1,3},{2,0},{3,1},{4,6},{5,7},{6,4},{7,5},{8,10},{9,11},{10,... | collective-permute-start | bytes 442376 | tf_op jit(solution)/shard_map/ppermute | solution.py:481
  31.7 3.6 %collective-permute-start.15 = (bf16[1,48,1024]{2,1,0:T(8,128)(2,1)S(1)}, bf16[1,48,1024]{2,1,0:T(8,128)(2,1)S(1)}, u32[]{:S(2)}, u32[]{:S(2)}) collective-permute-start(bf16[1,48,1024]{2,1,0:T(8,128)(2,1)S(1)} %get-tuple-element.120), channel_id=1, source_target_pairs={{0,1},{1,0},{2,3},{3,2},{4,5},{5,4},{6,7},{7,6},{8,9},{9,8},{10,11... | collective-permute-start | bytes 294920 | tf_op jit(solution)/shard_map/ppermute | solution.py:474
  31.8 4.1 %collective-permute-start.16 = (bf16[1,48,1024]{2,1,0:T(8,128)(2,1)S(1)}, bf16[1,48,1024]{2,1,0:T(8,128)(2,1)S(1)}, u32[]{:S(2)}, u32[]{:S(2)}) collective-permute-start(bf16[1,48,1024]{2,1,0:T(8,128)(2,1)S(1)} %get-tuple-element.121), channel_id=1, source_target_pairs={{0,1},{1,0},{2,3},{3,2},{4,5},{5,4},{6,7},{7,6},{8,9},{9,8},{10,11... | collective-permute-start | bytes 294920 | tf_op jit(solution)/shard_map/ppermute | solution.py:474
  32.3 9.9 %collective-permute-start.13 = (bf16[3,48,1024]{2,1,0:T(8,128)(2,1)S(1)}, bf16[3,48,1024]{2,1,0:T(8,128)(2,1)S(1)}, u32[]{:S(2)}, u32[]{:S(2)}) collective-permute-start(bf16[3,48,1024]{2,1,0:T(8,128)(2,1)S(1)} %sum_cores.8.rest_1_.rest_3_.sum_ref), channel_id=1, source_target_pairs={{0,2},{1,3},{2,0},{3,1},{4,6},{5,7},{6,4},{7,5},{8,10},{9,11},{10,... | collective-permute-start | bytes 884744 | tf_op jit(solution)/shard_map/ppermute | solution.py:481
  33.9 2.1 %collective-permute-start.17 = (bf16[1,48,1024]{2,1,0:T(8,128)(2,1)S(1)}, bf16[1,48,1024]{2,1,0:T(8,128)(2,1)S(1)}, u32[]{:S(2)}, u32[]{:S(2)}) collective-permute-start(bf16[1,48,1024]{2,1,0:T(8,128)(2,1)S(1)} %get-tuple-element.122), channel_id=1, source_target_pairs={{0,1},{1,0},{2,3},{3,2},{4,5},{5,4},{6,7},{7,6},{8,9},{9,8},{10,11... | collective-permute-start | bytes 294920 | tf_op jit(solution)/shard_map/ppermute | solution.py:474
  35.3 2.8 %collective-permute-start.21 = (bf16[1,48,1024]{2,1,0:T(8,128)(2,1)S(1)}, bf16[1,48,1024]{2,1,0:T(8,128)(2,1)S(1)}, u32[]{:S(2)}, u32[]{:S(2)}) collective-permute-start(bf16[1,48,1024]{2,1,0:T(8,128)(2,1)S(1)} %get-tuple-element.129), channel_id=1, source_target_pairs={{0,1},{1,0},{2,3},{3,2},{4,5},{5,4},{6,7},{7,6},{8,9},{9,8},{10,11... | collective-permute-start | bytes 294920 | tf_op jit(solution)/shard_map/ppermute | solution.py:474
  35.9 2.6 %collective-permute-start.22 = (bf16[1,48,1024]{2,1,0:T(8,128)(2,1)S(1)}, bf16[1,48,1024]{2,1,0:T(8,128)(2,1)S(1)}, u32[]{:S(2)}, u32[]{:S(2)}) collective-permute-start(bf16[1,48,1024]{2,1,0:T(8,128)(2,1)S(1)} %get-tuple-element.130), channel_id=1, source_target_pairs={{0,1},{1,0},{2,3},{3,2},{4,5},{5,4},{6,7},{7,6},{8,9},{9,8},{10,11... | collective-permute-start | bytes 294920 | tf_op jit(solution)/shard_map/ppermute | solution.py:474
  36.1 12.5 %collective-permute-start.27 = (bf16[3,48,1024]{2,1,0:T(8,128)(2,1)S(1)}, bf16[3,48,1024]{2,1,0:T(8,128)(2,1)S(1)}, u32[]{:S(2)}, u32[]{:S(2)}) collective-permute-start(bf16[3,48,1024]{2,1,0:T(8,128)(2,1)S(1)} %sum_cores.9.rest_2_.rest_3_.sum_ref), channel_id=1, source_target_pairs={{0,2},{1,3},{2,0},{3,1},{4,6},{5,7},{6,4},{7,5},{8,10},{9,11},{10,... | collective-permute-start | bytes 884744 | tf_op jit(solution)/shard_map/ppermute | solution.py:481
  36.7 2.0 %collective-permute-start.23 = (bf16[1,48,1024]{2,1,0:T(8,128)(2,1)S(1)}, bf16[1,48,1024]{2,1,0:T(8,128)(2,1)S(1)}, u32[]{:S(2)}, u32[]{:S(2)}) collective-permute-start(bf16[1,48,1024]{2,1,0:T(8,128)(2,1)S(1)} %get-tuple-element.131), channel_id=1, source_target_pairs={{0,1},{1,0},{2,3},{3,2},{4,5},{5,4},{6,7},{7,6},{8,9},{9,8},{10,11... | collective-permute-start | bytes 294920 | tf_op jit(solution)/shard_map/ppermute | solution.py:474
  38.1 2.2 %collective-permute-start.18 = (bf16[1,48,512]{2,1,0:T(8,128)(2,1)S(1)}, bf16[1,48,512]{2,1,0:T(8,128)(2,1)S(1)}, u32[]{:S(2)}, u32[]{:S(2)}) collective-permute-start(bf16[1,48,512]{2,1,0:T(8,128)(2,1)S(1)} %get-tuple-element.125), channel_id=1, source_target_pairs={{0,1},{1,0},{2,3},{3,2},{4,5},{5,4},{6,7},{7,6},{8,9},{9,8},{10,11... | collective-permute-start | bytes 147464 | tf_op jit(solution)/shard_map/ppermute | solution.py:474
  38.5 1.9 %collective-permute-start.19 = (bf16[1,48,512]{2,1,0:T(8,128)(2,1)S(1)}, bf16[1,48,512]{2,1,0:T(8,128)(2,1)S(1)}, u32[]{:S(2)}, u32[]{:S(2)}) collective-permute-start(bf16[1,48,512]{2,1,0:T(8,128)(2,1)S(1)} %get-tuple-element.126), channel_id=1, source_target_pairs={{0,1},{1,0},{2,3},{3,2},{4,5},{5,4},{6,7},{7,6},{8,9},{9,8},{10,11... | collective-permute-start | bytes 147464 | tf_op jit(solution)/shard_map/ppermute | solution.py:474
  38.7 17.4 %collective-permute-start.33 = (bf16[3,48,1024]{2,1,0:T(8,128)(2,1)S(1)}, bf16[3,48,1024]{2,1,0:T(8,128)(2,1)S(1)}, u32[]{:S(2)}, u32[]{:S(2)}) collective-permute-start(bf16[3,48,1024]{2,1,0:T(8,128)(2,1)S(1)} %sum_cores.10.rest_3_.sum_ref), channel_id=1, source_target_pairs={{0,2},{1,3},{2,0},{3,1},{4,6},{5,7},{6,4},{7,5},{8,10},{9,11},{10,... | collective-permute-start | bytes 884744 | tf_op jit(solution)/shard_map/ppermute | solution.py:481
  40.3 2.7 %collective-permute-start.25 = (bf16[16,2048]{1,0:T(8,128)(2,1)S(1)}, bf16[16,2048]{1,0:T(8,128)(2,1)S(1)}, u32[]{:S(2)}, u32[]{:S(2)}) collective-permute-start(bf16[16,2048]{1,0:T(8,128)(2,1)S(1)} %get-tuple-element.133.rest_4_.rest_8_), channel_id=1, source_target_pairs={{0,1},{1,0},{2,3},{3,2},{4,5},{5,4},{6,7},{7,6},{8,9},{9,8},{10,11... | collective-permute-start | bytes 196616 | tf_op jit(solution)/shard_map/ppermute | solution.py:474
  40.4 1.3 %collective-permute-start.20 = (bf16[1,48,512]{2,1,0:T(8,128)(2,1)S(1)}, bf16[1,48,512]{2,1,0:T(8,128)(2,1)S(1)}, u32[]{:S(2)}, u32[]{:S(2)}) collective-permute-start(bf16[1,48,512]{2,1,0:T(8,128)(2,1)S(1)} %get-tuple-element.127), channel_id=1, source_target_pairs={{0,1},{1,0},{2,3},{3,2},{4,5},{5,4},{6,7},{7,6},{8,9},{9,8},{10,11... | collective-permute-start | bytes 147464 | tf_op jit(solution)/shard_map/ppermute | solution.py:474
  42.4 1.8 %collective-permute-start.24 = (bf16[48,1024]{1,0:T(8,128)(2,1)S(1)}, bf16[48,1024]{1,0:T(8,128)(2,1)S(1)}, u32[]{:S(2)}, u32[]{:S(2)}) collective-permute-start(bf16[48,1024]{1,0:T(8,128)(2,1)S(1)} %get-tuple-element.132.rest_2_.rest_6_), channel_id=1, source_target_pairs={{0,1},{1,0},{2,3},{3,2},{4,5},{5,4},{6,7},{7,6},{8,9},{9,8},{10,11... | collective-permute-start | bytes 294920 | tf_op jit(solution)/shard_map/ppermute | solution.py:474
  42.5 1.4 %collective-permute-start.9 = (bf16[16,2048]{1,0:T(8,128)(2,1)S(1)}, bf16[16,2048]{1,0:T(8,128)(2,1)S(1)}, u32[]{:S(2)}, u32[]{:S(2)}) collective-permute-start(bf16[16,2048]{1,0:T(8,128)(2,1)S(1)} %get-tuple-element.108.rest_0_.rest_4_), channel_id=1, source_target_pairs={{0,1},{1,0},{2,3},{3,2},{4,5},{5,4},{6,7},{7,6},{8,9},{9,8},{10,11... | collective-permute-start | bytes 196616 | tf_op jit(solution)/shard_map/ppermute | solution.py:474
  43.0 1.4 %collective-permute-start.26 = (bf16[48,1024]{1,0:T(8,128)(2,1)S(1)}, bf16[48,1024]{1,0:T(8,128)(2,1)S(1)}, u32[]{:S(2)}, u32[]{:S(2)}) collective-permute-start(bf16[48,1024]{1,0:T(8,128)(2,1)S(1)} %get-tuple-element.134.rest_6_.rest_10_), channel_id=1, source_target_pairs={{0,1},{1,0},{2,3},{3,2},{4,5},{5,4},{6,7},{7,6},{8,9},{9,8},{10,11... | collective-permute-start | bytes 294920 | tf_op jit(solution)/shard_map/ppermute | solution.py:474
  43.9 5.5 %collective-permute-start.31 = (bf16[48,1024]{1,0:T(8,128)(2,1)S(1)}, bf16[48,1024]{1,0:T(8,128)(2,1)S(1)}, u32[]{:S(2)}, u32[]{:S(2)}) collective-permute-start(bf16[48,1024]{1,0:T(8,128)(2,1)S(1)} %get-tuple-element.142.rest_2_), channel_id=1, source_target_pairs={{0,1},{1,0},{2,3},{3,2},{4,5},{5,4},{6,7},{7,6},{8,9},{9,8},{10,11... | collective-permute-start | bytes 294920 | tf_op jit(solution)/shard_map/ppermute | solution.py:474
  44.3 5.1 %collective-permute-start.30 = (bf16[16,2048]{1,0:T(8,128)(2,1)S(1)}, bf16[16,2048]{1,0:T(8,128)(2,1)S(1)}, u32[]{:S(2)}, u32[]{:S(2)}) collective-permute-start(bf16[16,2048]{1,0:T(8,128)(2,1)S(1)} %get-tuple-element.141.rest_0_), channel_id=1, source_target_pairs={{0,1},{1,0},{2,3},{3,2},{4,5},{5,4},{6,7},{7,6},{8,9},{9,8},{10,11... | collective-permute-start | bytes 196616 | tf_op jit(solution)/shard_map/ppermute | solution.py:474
  48.8 5.7 %collective-permute-start.28 = (bf16[48,1024]{1,0:T(8,128)(2,1)S(1)}, bf16[48,1024]{1,0:T(8,128)(2,1)S(1)}, u32[]{:S(2)}, u32[]{:S(2)}) collective-permute-start(bf16[48,1024]{1,0:T(8,128)(2,1)S(1)} %get-tuple-element.138.rest_2_.rest_6_), channel_id=1, source_target_pairs={{0,1},{1,0},{2,3},{3,2},{4,5},{5,4},{6,7},{7,6},{8,9},{9,8},{10,11... | collective-permute-start | bytes 294920 | tf_op jit(solution)/shard_map/ppermute | solution.py:474
  48.8 5.8 %collective-permute-start.29 = (bf16[48,1024]{1,0:T(8,128)(2,1)S(1)}, bf16[48,1024]{1,0:T(8,128)(2,1)S(1)}, u32[]{:S(2)}, u32[]{:S(2)}) collective-permute-start(bf16[48,1024]{1,0:T(8,128)(2,1)S(1)} %get-tuple-element.139.rest_6_.rest_10_), channel_id=1, source_target_pairs={{0,1},{1,0},{2,3},{3,2},{4,5},{5,4},{6,7},{7,6},{8,9},{9,8},{10,11... | collective-permute-start | bytes 294920 | tf_op jit(solution)/shard_map/ppermute | solution.py:474
  49.3 8.0 %collective-permute-start.37 = (bf16[48,1024]{1,0:T(8,128)(2,1)S(1)}, bf16[48,1024]{1,0:T(8,128)(2,1)S(1)}, u32[]{:S(2)}, u32[]{:S(2)}) collective-permute-start(bf16[48,1024]{1,0:T(8,128)(2,1)S(1)} %get-tuple-element.151.rest_2_), channel_id=1, source_target_pairs={{0,1},{1,0},{2,3},{3,2},{4,5},{5,4},{6,7},{7,6},{8,9},{9,8},{10,11... | collective-permute-start | bytes 294920 | tf_op jit(solution)/shard_map/ppermute | solution.py:474
  49.4 13.5 %collective-permute-start.38 = (bf16[3,48,512]{2,1,0:T(8,128)(2,1)S(1)}, bf16[3,48,512]{2,1,0:T(8,128)(2,1)S(1)}, u32[]{:S(2)}, u32[]{:S(2)}) collective-permute-start(bf16[3,48,512]{2,1,0:T(8,128)(2,1)S(1)} %sum_cores.11.rest_1_.sum_ref), channel_id=1, source_target_pairs={{0,2},{1,3},{2,0},{3,1},{4,6},{5,7},{6,4},{7,5},{8,10},{9,11},{10,... | collective-permute-start | bytes 442376 | tf_op jit(solution)/shard_map/ppermute | solution.py:481
  54.5 2.4 %collective-permute-start.32 = (bf16[16,1536]{1,0:T(8,128)(2,1)S(1)}, bf16[16,1536]{1,0:T(8,128)(2,1)S(1)}, u32[]{:S(2)}, u32[]{:S(2)}) collective-permute-start(bf16[16,1536]{1,0:T(8,128)(2,1)S(1)} %get-tuple-element.146.rest_0_.rest_4_), channel_id=1, source_target_pairs={{0,1},{1,0},{2,3},{3,2},{4,5},{5,4},{6,7},{7,6},{8,9},{9,8},{10,11... | collective-permute-start | bytes 147464 | tf_op jit(solution)/shard_map/ppermute | solution.py:474
  56.4 5.0 %collective-permute-start.34 = (bf16[48,1024]{1,0:T(8,128)(2,1)S(1)}, bf16[48,1024]{1,0:T(8,128)(2,1)S(1)}, u32[]{:S(2)}, u32[]{:S(2)}) collective-permute-start(bf16[48,1024]{1,0:T(8,128)(2,1)S(1)} %get-tuple-element.148.rest_2_.rest_6_), channel_id=1, source_target_pairs={{0,1},{1,0},{2,3},{3,2},{4,5},{5,4},{6,7},{7,6},{8,9},{9,8},{10,11... | collective-permute-start | bytes 294920 | tf_op jit(solution)/shard_map/ppermute | solution.py:474
  56.8 4.6 %collective-permute-start.36 = (bf16[48,1024]{1,0:T(8,128)(2,1)S(1)}, bf16[48,1024]{1,0:T(8,128)(2,1)S(1)}, u32[]{:S(2)}, u32[]{:S(2)}) collective-permute-start(bf16[48,1024]{1,0:T(8,128)(2,1)S(1)} %get-tuple-element.150.rest_6_.rest_10_), channel_id=1, source_target_pairs={{0,1},{1,0},{2,3},{3,2},{4,5},{5,4},{6,7},{7,6},{8,9},{9,8},{10,11... | collective-permute-start | bytes 294920 | tf_op jit(solution)/shard_map/ppermute | solution.py:474
  56.9 4.1 %collective-permute-start.35 = (bf16[16,1536]{1,0:T(8,128)(2,1)S(1)}, bf16[16,1536]{1,0:T(8,128)(2,1)S(1)}, u32[]{:S(2)}, u32[]{:S(2)}) collective-permute-start(bf16[16,1536]{1,0:T(8,128)(2,1)S(1)} %get-tuple-element.149.rest_4_.rest_8_), channel_id=1, source_target_pairs={{0,1},{1,0},{2,3},{3,2},{4,5},{5,4},{6,7},{7,6},{8,9},{9,8},{10,11... | collective-permute-start | bytes 147464 | tf_op jit(solution)/shard_map/ppermute | solution.py:474
  57.3 6.3 %collective-permute-start.42 = (bf16[48,1024]{1,0:T(8,128)(2,1)S(1)}, bf16[48,1024]{1,0:T(8,128)(2,1)S(1)}, u32[]{:S(2)}, u32[]{:S(2)}) collective-permute-start(bf16[48,1024]{1,0:T(8,128)(2,1)S(1)} %get-tuple-element.162.rest_2_), channel_id=1, source_target_pairs={{0,1},{1,0},{2,3},{3,2},{4,5},{5,4},{6,7},{7,6},{8,9},{9,8},{10,11... | collective-permute-start | bytes 294920 | tf_op jit(solution)/shard_map/ppermute | solution.py:474
  61.1 2.5 %collective-permute-start.41 = (bf16[16,1536]{1,0:T(8,128)(2,1)S(1)}, bf16[16,1536]{1,0:T(8,128)(2,1)S(1)}, u32[]{:S(2)}, u32[]{:S(2)}) collective-permute-start(bf16[16,1536]{1,0:T(8,128)(2,1)S(1)} %get-tuple-element.161.rest_0_), channel_id=1, source_target_pairs={{0,1},{1,0},{2,3},{3,2},{4,5},{5,4},{6,7},{7,6},{8,9},{9,8},{10,11... | collective-permute-start | bytes 147464 | tf_op jit(solution)/shard_map/ppermute | solution.py:474
  63.0 4.2 %collective-permute-start.39 = (bf16[48,512]{1,0:T(8,128)(2,1)S(1)}, bf16[48,512]{1,0:T(8,128)(2,1)S(1)}, u32[]{:S(2)}, u32[]{:S(2)}) collective-permute-start(bf16[48,512]{1,0:T(8,128)(2,1)S(1)} %get-tuple-element.159.rest_2_.rest_6_), channel_id=1, source_target_pairs={{0,1},{1,0},{2,3},{3,2},{4,5},{5,4},{6,7},{7,6},{8,9},{9,8},{10,11... | collective-permute-start | bytes 147464 | tf_op jit(solution)/shard_map/ppermute | solution.py:474
  63.2 3.9 %collective-permute-start.40 = (bf16[48,512]{1,0:T(8,128)(2,1)S(1)}, bf16[48,512]{1,0:T(8,128)(2,1)S(1)}, u32[]{:S(2)}, u32[]{:S(2)}) collective-permute-start(bf16[48,512]{1,0:T(8,128)(2,1)S(1)} %get-tuple-element.160.rest_6_.rest_10_), channel_id=1, source_target_pairs={{0,1},{1,0},{2,3},{3,2},{4,5},{5,4},{6,7},{7,6},{8,9},{9,8},{10,11... | collective-permute-start | bytes 147464 | tf_op jit(solution)/shard_map/ppermute | solution.py:474
  68.0 7.9 %collective-permute-start.43 = (bf16[32,1024]{1,0:T(8,128)(2,1)S(1)}, bf16[32,1024]{1,0:T(8,128)(2,1)S(1)}, u32[]{:S(2)}, u32[]{:S(2)}) collective-permute-start(bf16[32,1024]{1,0:T(8,128)(2,1)S(1)} %get-tuple-element.180), channel_id=1, source_target_pairs={{0,4},{4,0},{8,12},{12,8},{1,5},{5,1},{9,13},{13,9},{2,6},{6,2},{1... | collective-permute-start | bytes 196616 | tf_op jit(solution)/shard_map/ppermute | solution.py:477
  69.7 7.9 %collective-permute-start.44 = (bf16[32,1024]{1,0:T(8,128)(2,1)S(1)}, bf16[32,1024]{1,0:T(8,128)(2,1)S(1)}, u32[]{:S(2)}, u32[]{:S(2)}) collective-permute-start(bf16[32,1024]{1,0:T(8,128)(2,1)S(1)} %get-tuple-element.179), channel_id=1, source_target_pairs={{0,8},{4,12},{8,0},{12,4},{1,9},{5,13},{9,1},{13,5},{2,10},{6,14},... | collective-permute-start | bytes 196616 | tf_op jit(solution)/shard_map/ppermute | solution.py:477
  70.0 7.5 %collective-permute-start.45 = (bf16[32,1024]{1,0:T(8,128)(2,1)S(1)}, bf16[32,1024]{1,0:T(8,128)(2,1)S(1)}, u32[]{:S(2)}, u32[]{:S(2)}) collective-permute-start(bf16[32,1024]{1,0:T(8,128)(2,1)S(1)} %get-tuple-element.178), channel_id=1, source_target_pairs={{0,12},{4,8},{8,4},{12,0},{1,13},{5,9},{9,5},{13,1},{2,14},{6,10},... | collective-permute-start | bytes 196616 | tf_op jit(solution)/shard_map/ppermute | solution.py:477
  72.5 1.2 %collective-permute-start.46 = (bf16[48,512]{1,0:T(8,128)(2,1)S(1)}, bf16[48,512]{1,0:T(8,128)(2,1)S(1)}, u32[]{:S(2)}, u32[]{:S(2)}) collective-permute-start(bf16[48,512]{1,0:T(8,128)(2,1)S(1)} %get-tuple-element.170.rest_2_), channel_id=1, source_target_pairs={{0,1},{1,0},{2,3},{3,2},{4,5},{5,4},{6,7},{7,6},{8,9},{9,8},{10,11... | collective-permute-start | bytes 147464 | tf_op jit(solution)/shard_map/ppermute | solution.py:474

commit v4 on v3

--- a/solution.py
+++ b/solution.py
@@ -14,7 +14,8 @@
 COST_SCALE = 1000000000
 OWN_CHUNKS = (4, 3)
 OWN_PIECES = (((0,), (1,), (2,)), ((0, 1), (2,)))
-OWN_AFTER = (0, 2)
+OWN_AFTER = (1, 2)
+DEFER = True
 FAR_PIECES = ((0,), (1,), (2,))
 FAR_CHUNKS = (2, 2, 2, 1)
 BF = jnp.bfloat16
@@ -555,7 +556,7 @@
         deps = (tok,)
         parts = (*own_parts[g], mine, swap_cores(mine))
         last = c == len(far_chunks) - 1
-        if pending:
+        if pending and not (last and DEFER):
             grads, deps = flush(grads, pending.pop(0), deps)
         offsets = (offset * tile, offset * tile, 0, 0)
         gt, *rest, tok = grad_tokens_of(

time: 79 us -> 76.2 us (0.965)
  waiting for transfers between devices: 8.68 us -> 6.73 us
  starting transfers between devices: 26.4 us -> 25.5 us
    ppermute x6, waiting for transfers between devices: 1.6 us -> 0.02 us  [flipped(): return lax.ppermute(value, 'row', [(i, i ^ d) for i in range(n_row)])]
  transfers between devices with their start and end apart: 47 -> 47, of which waited for: 7 -> 7; matrix products, arithmetic and copies ran while one was open for 0% -> 0% of each run, Pallas kernels for 51% -> 53%
where the time goes in v4:
time: 76.2 us; the launch traced here: 75.9 us
  Pallas kernels  41.8 us (55%)
  starting transfers between devices  25.5 us (33%)
  waiting for transfers between devices  6.73 us (9%)
  other arithmetic  0.96 us (1%)
  between operations  0.92 us (1%)
    pallas_call x2, Pallas kernels, open_weights(): pl.pallas_call(functools.partial(open_kernel, len(deps), pieces, opener,...  15 us
    pallas_call x4, Pallas kernels, weight_grads(): pl.pallas_call(functools.partial(weight_grads_kernel, len(parts), granule...  13 us
    ppermute x6, starting transfers between devices, flipped(): return lax.ppermute(value, 'row', [(i, i ^ d) for i in range(n_row)])  10.6 us
    ppermute x35, starting transfers between devices, swap_cores(): return [lax.ppermute(value, 'col', core_swap) for value in values]  8.01 us
    ppermute x6, starting transfers between devices, from_chips(): lax.ppermute(value, 'col', [(i, (i + 2 * d) % n_col) for i in range(n_col)])  6.88 us
    pallas_call x4, Pallas kernels, forward(): pl.pallas_call(functools.partial(forward_kernel, pieces, own, offset, spa...  5.54 us
    pallas_call x4, Pallas kernels, grad_tokens_of(): pl.pallas_call(kernel, out_shape=(*outs, TOKEN), in_specs=[VMEM] * (len(p...  5.27 us
    ppermute x6, waiting for transfers between devices, from_chips(): lax.ppermute(value, 'col', [(i, (i + 2 * d) % n_col) for i in range(n_col)])  3.49 us
  transfers between devices with their start and end apart: 47, of which 7 were waited for; matrix products, arithmetic and copies ran while one was open for 0% of the time, Pallas kernels for 53%

profile of v4, /device:TPU:0, one launch (start us, length us, event | category | flops | bytes accessed | tf_op | source)
XLA Modules:
  0.0 75.9 jit_solution(5759298610034588687)
XLA Ops:
  0.6 0.9 %pad_maximum_fusion.both_ref = bf16[2,32,1024]{2,1,0:T(8,128)(2,1)S(1)} fusion(bf16[1,32,1024]{2,1,0:T(8,128)(2,1)} %bitcast.6, bf16[1,32,1024]{2,1,0:T(8,128)(2,1)} %bitcast.7), kind=kLoop, calls=%fused_computation | loop fusion | flops 65536 | bytes 262144 | tf_op jit(solution)/shard_map/stack | solution.py:486
  1.5 4.1 %collective-permute-start.5 = (bf16[2,32,1024]{2,1,0:T(8,128)(2,1)S(1)}, bf16[2,32,1024]{2,1,0:T(8,128)(2,1)S(1)}, u32[]{:S(2)}, u32[]{:S(2)}) collective-permute-start(bf16[2,32,1024]{2,1,0:T(8,128)(2,1)S(1)} %pad_maximum_fusion.both_ref), channel_id=1, source_target_pairs={{0,8},{4,12},{8,0},{12,4},{1,9},{5,13},{9,1},{13,5},{2,10},{6,14},... | collective-permute-start | bytes 393224 | tf_op jit(solution)/shard_map/ppermute | solution.py:478
  5.7 9.5 %open_weights.2 = (bf16[3,16,2048]{2,1,0:T(8,128)(2,1)S(1)}, bf16[1,16,2048]{2,1,0:T(8,128)(2,1)S(1)}, bf16[1,16,2048]{2,1,0:T(8,128)(2,1)S(1)}, bf16[1,16,2048]...) custom-call(s32[3]{0:T(128)S(1)} %pad_add_fusion.place, ...), custom_call_target="tpu_custom_call" | custom-call | tf_op jit(solution)/shard_map/open_weights/pallas_call | solution.py:184
  15.3 0.5 collective-permute-start.1
  15.8 1.6 %collective-permute-start.4 = (bf16[2,32,1024]{2,1,0:T(8,128)(2,1)S(1)}, bf16[2,32,1024]{2,1,0:T(8,128)(2,1)S(1)}, u32[]{:S(2)}, u32[]{:S(2)}) collective-permute-start(bf16[2,32,1024]{2,1,0:T(8,128)(2,1)S(1)} %pad_maximum_fusion.both_ref), channel_id=1, source_target_pairs={{0,4},{4,0},{8,12},{12,8},{1,5},{5,1},{9,13},{13,9},{2,6},{6,2},{1... | collective-permute-start | bytes 393224 | tf_op jit(solution)/shard_map/ppermute | solution.py:478
  17.4 0.4 collective-permute-start.6
  17.9 5.5 %open_weights.3 = (bf16[3,16,1536]{2,1,0:T(8,128)(2,1)S(1)}, bf16[2,16,1536]{2,1,0:T(8,128)(2,1)S(1)}, bf16[1,16,1536]{2,1,0:T(8,128)(2,1)S(1)}, bf16[1024,1536]...) custom-call(s32[3]{0:T(128)S(1)} %pad_add_fusion.place, ...), custom_call_target="tpu_custom_call" | custom-call | tf_op jit(solution)/shard_map/open_weights/pallas_call | solution.py:184
  23.5 1.6 %collective-permute-start.3 = (bf16[3,16,2048]{2,1,0:T(8,128)(2,1)S(1)}, bf16[3,16,2048]{2,1,0:T(8,128)(2,1)S(1)}, u32[]{:S(2)}, u32[]{:S(2)}) collective-permute-start(bf16[3,16,2048]{2,1,0:T(8,128)(2,1)S(1)} %sum_cores.6.rest_3_.sum_ref), channel_id=1, source_target_pairs={{0,2},{1,3},{2,0},{3,1},{4,6},{5,7},{6,4},{7,5},{8,10},{9,11},{10,... | collective-permute-start | bytes 589832 | tf_op jit(solution)/shard_map/ppermute | solution.py:482
  25.3 1.1 %collective-permute-done.8.rest_1_ = bf16[1,16,1536]{2,1,0:T(8,128)(2,1)S(1)} collective-permute-done((bf16[1,16,1536]{2,1,0:T(8,128)(2,1)S(1)}, bf16[1,16,1536]{2,1,0:T(8,128)(2,1)S(1)}, u32[]{:S(2)}, u32[]{:S(2)}) %collective-permute-start.8) | collective-permute-done | bytes 49184 | tf_op jit(solution)/shard_map/ppermute | solution.py:475
  26.4 0.7 all_tokens.1
  27.1 1.5 %forward.4 = (bf16[3,48,1024]{2,1,0:T(8,128)(2,1)S(1)}, bf16[1,48,1024]{2,1,0:T(8,128)(2,1)S(1)}, bf16[1,48,1024]{2,1,0:T(8,128)(2,1)S(1)}, bf16[1,48,1024]{2,1,0:T(8,128)(2,1)S(1)}, f32[8,128]{1,0:T(8,128)S(1)}) custom-call(bf16[128,1024]{1,0:T(8,128)(2,1)S(1)} %get-tuple-element.103.x_ref, bf16[128,1024]{1,0:T(8,128)(2,1)S(1)} %get-tuple-element.104.og_ref, ...), custom_call_target="tpu_custom_call" | custom-call | tf_op jit(solution)/shard_map/forward/pallas_call | solution.py:227
  28.7 0.3 collective-permute-start.11
  29.3 0.5 collective-permute-start.14
  29.8 1.4 %forward.5 = (bf16[3,48,1024]{2,1,0:T(8,128)(2,1)S(1)}, bf16[1,48,1024]{2,1,0:T(8,128)(2,1)S(1)}, bf16[1,48,1024]{2,1,0:T(8,128)(2,1)S(1)}, bf16[1,48,1024]{2,1,0:T(8,128)(2,1)S(1)}, f32[8,128]{1,0:T(8,128)S(1)}) custom-call(bf16[128,1024]{1,0:T(8,128)(2,1)S(1)} %get-tuple-element.103.x_ref, bf16[128,1024]{1,0:T(8,128)(2,1)S(1)} %get-tuple-element.104.og_ref, ...), custom_call_target="tpu_custom_call" | custom-call | tf_op jit(solution)/shard_map/forward/pallas_call | solution.py:227
  31.4 0.5 collective-permute-start.16
  31.9 1.5 %collective-permute-start.13 = (bf16[3,48,1024]{2,1,0:T(8,128)(2,1)S(1)}, bf16[3,48,1024]{2,1,0:T(8,128)(2,1)S(1)}, u32[]{:S(2)}, u32[]{:S(2)}) collective-permute-start(bf16[3,48,1024]{2,1,0:T(8,128)(2,1)S(1)} %sum_cores.8.rest_2_.rest_3_.sum_ref), channel_id=1, source_target_pairs={{0,2},{1,3},{2,0},{3,1},{4,6},{5,7},{6,4},{7,5},{8,10},{9,11},{10,... | collective-permute-start | bytes 884744 | tf_op jit(solution)/shard_map/ppermute | solution.py:482
  33.6 1.4 %forward.6 = (bf16[3,48,1024]{2,1,0:T(8,128)(2,1)S(1)}, bf16[1,48,1024]{2,1,0:T(8,128)(2,1)S(1)}, bf16[1,48,1024]{2,1,0:T(8,128)(2,1)S(1)}, bf16[1,48,1024]{2,1,0:T(8,128)(2,1)S(1)}, f32[8,128]{1,0:T(8,128)S(1)}) custom-call(bf16[128,1024]{1,0:T(8,128)(2,1)S(1)} %get-tuple-element.103.x_ref, bf16[128,1024]{1,0:T(8,128)(2,1)S(1)} %get-tuple-element.104.og_ref, ...), custom_call_target="tpu_custom_call" | custom-call | tf_op jit(solution)/shard_map/forward/pallas_call | solution.py:227
  35.0 0.6 collective-permute-start.21
  35.8 0.6 collective-permute-start.27
  36.6 1.2 %forward.7 = (bf16[3,48,512]{2,1,0:T(8,128)(2,1)S(1)}, bf16[1,48,512]{2,1,0:T(8,128)(2,1)S(1)}, bf16[1,48,512]{2,1,0:T(8,128)(2,1)S(1)}, bf16[1,48,512]{2,1,0:T(8,128)(2,1)S(1)}, f32[8,128]{1,0:T(8,128)}) custom-call(bf16[128,1024]{1,0:T(8,128)(2,1)S(1)} %get-tuple-element.103.x_ref, bf16[128,1024]{1,0:T(8,128)(2,1)S(1)} %get-tuple-element.104.og_ref, ...), custom_call_target="tpu_custom_call" | custom-call | tf_op jit(solution)/shard_map/forward/pallas_call | solution.py:227
  37.8 0.4 collective-permute-start.18
  38.4 1.5 %collective-permute-start.33 = (bf16[3,48,1024]{2,1,0:T(8,128)(2,1)S(1)}, bf16[3,48,1024]{2,1,0:T(8,128)(2,1)S(1)}, u32[]{:S(2)}, u32[]{:S(2)}) collective-permute-start(bf16[3,48,1024]{2,1,0:T(8,128)(2,1)S(1)} %sum_cores.10.rest_3_.sum_ref), channel_id=1, source_target_pairs={{0,2},{1,3},{2,0},{3,1},{4,6},{5,7},{6,4},{7,5},{8,10},{9,11},{10,... | collective-permute-start | bytes 884744 | tf_op jit(solution)/shard_map/ppermute | solution.py:482
  40.0 0.4 collective-permute-start.20
  40.5 0.9 %collective-permute-done.20.rest_2_ = bf16[1,48,512]{2,1,0:T(8,128)(2,1)S(1)} collective-permute-done((bf16[1,48,512]{2,1,0:T(8,128)(2,1)S(1)}, bf16[1,48,512]{2,1,0:T(8,128)(2,1)S(1)}, u32[]{:S(2)}, u32[]{:S(2)}) %collective-permute-start.20) | collective-permute-done | bytes 49184 | tf_op jit(solution)/shard_map/ppermute | solution.py:475
  41.4 0.8 %collective-permute-done.13.rest_0_ = bf16[3,48,1024]{2,1,0:T(8,128)(2,1)S(1)} collective-permute-done((bf16[3,48,1024]{2,1,0:T(8,128)(2,1)S(1)}, bf16[3,48,1024]{2,1,0:T(8,128)(2,1)S(1)}, u32[]{:S(2)}, u32[]{:S(2)}) %collective-permute-start.13) | collective-permute-done | bytes 294944 | tf_op jit(solution)/shard_map/ppermute | solution.py:482
  42.5 0.5 collective-permute-start.25
  43.1 0.8 %collective-permute-done.25.rest_5_.rest_9_ = bf16[16,2048]{1,0:T(8,128)(2,1)S(1)} collective-permute-done((bf16[16,2048]{1,0:T(8,128)(2,1)S(1)}, bf16[16,2048]{1,0:T(8,128)(2,1)S(1)}, u32[]{:S(2)}, u32[]{:S(2)}) %collective-permute-start.25) | collective-permute-done | bytes 65568 | tf_op jit(solution)/shard_map/ppermute | solution.py:475
  43.9 0.4 collective-permute-start.31
  44.4 1.5 %grad_tokens.4 = (f32[128,1024]{1,0:T(8,128)S(1)}, f32[8,128]{1,0:T(8,128)S(1)}) custom-call(bf16[1024,2048]{1,0:T(8,128)(2,1)S(1)} %get-tuple-element.91.wg_ref, bf16[1024,2048]{1,0:T(8,128)(2,1)S(1)} %get-tuple-element.92.wu_ref, bf16[16,2048]{1,0:T(8,128)(2,1)S(1)} %get-tuple-element.113.rest_0_.rest_4_, ...), custom_call_target="tpu_custom_call" | custom-call | tf_op jit(solution)/shard_map/grad_tokens/pallas_call | solution.py:368
  45.9 2.6 %collective-permute-done.27.rest_0_ = bf16[3,48,1024]{2,1,0:T(8,128)(2,1)S(1)} collective-permute-done((bf16[3,48,1024]{2,1,0:T(8,128)(2,1)S(1)}, bf16[3,48,1024]{2,1,0:T(8,128)(2,1)S(1)}, u32[]{:S(2)}, u32[]{:S(2)}) %collective-permute-start.27) | collective-permute-done | bytes 294944 | tf_op jit(solution)/shard_map/ppermute | solution.py:482
  48.8 0.5 collective-permute-start.29
  49.4 1.1 %collective-permute-start.38 = (bf16[3,48,512]{2,1,0:T(8,128)(2,1)S(1)}, bf16[3,48,512]{2,1,0:T(8,128)(2,1)S(1)}, u32[]{:S(2)}, u32[]{:S(2)}) collective-permute-start(bf16[3,48,512]{2,1,0:T(8,128)(2,1)S(1)} %sum_cores.11.rest_1_.sum_ref), channel_id=1, source_target_pairs={{0,2},{1,3},{2,0},{3,1},{4,6},{5,7},{6,4},{7,5},{8,10},{9,11},{10,... | collective-permute-start | bytes 442376 | tf_op jit(solution)/shard_map/ppermute | solution.py:482
  50.5 3.6 %weight_grads.4 = (bf16[1024,3584]{1,0:T(8,128)(2,1)}, bf16[1024,3584]{1,0:T(8,128)(2,1)}, bf16[3584,1024]{1,0:T(8,128)(2,1)}, f32[8,128]{1,0:T(8,128)S(1)}) custom-call(bf16[1024,128]{1,0:T(8,128)(2,1)S(1)} %get-tuple-element.140.xt_ref, bf16[128,1024]{1,0:T(8,128)(2,1)S(1)} %get-tuple-element.104.og_ref, ...), custom_call_target="tpu_custom_call" | custom-call | tf_op jit(solution)/shard_map/weight_grads/pallas_call | solution.py:400
  54.1 1.5 %grad_tokens.5 = (f32[128,1024]{1,0:T(8,128)S(1)}, f32[8,128]{1,0:T(8,128)S(1)}) custom-call(f32[128,1024]{1,0:T(8,128)S(1)} %get-tuple-element.136.prev_ref, bf16[1024,2048]{1,0:T(8,128)(2,1)S(1)} %get-tuple-element.91.wg_ref, bf16[1024,2048]{1,0:T(8,128)(2,1)S(1)} %get-tuple-element.92.wu_ref, bf16[16,2048]{1,0:T(8,128)(2,1)S(1)} %get-tuple-element.113.rest_0_.rest_4_, ...), custom_call_target="tpu_custom_call" | custom-call | tf_op jit(solution)/shard_map/grad_tokens/pallas_call | solution.py:368
  55.8 0.2 collective-permute-start.34
  56.0 0.3 collective-permute-start.36
  56.5 0.3 collective-permute-start.35
  56.9 3.6 %weight_grads.5 = (bf16[1024,3584]{1,0:T(8,128)(2,1)}, bf16[1024,3584]{1,0:T(8,128)(2,1)}, bf16[3584,1024]{1,0:T(8,128)(2,1)}, f32[8,128]{1,0:T(8,128)S(1)}) custom-call(bf16[1024,128]{1,0:T(8,128)(2,1)S(1)} %get-tuple-element.140.xt_ref, ...), custom_call_target="tpu_custom_call", output_to_operand_aliasing={{0}: (17, {}), {1}: (18, {}), {2}: (19, {})} | custom-call | tf_op jit(solution)/shard_map/weight_grads/pallas_call | solution.py:400
  60.5 1.5 %grad_tokens.6 = (f32[128,1024]{1,0:T(8,128)S(1)}, f32[8,128]{1,0:T(8,128)S(1)}) custom-call(f32[128,1024]{1,0:T(8,128)S(1)} %get-tuple-element.145.prev_ref, bf16[1024,1536]{1,0:T(8,128)(2,1)S(1)} %get-tuple-element.114.wg_ref, bf16[1024,1536]{1,0:T(8,128)(2,1)S(1)} %get-tuple-element.115.wu_ref, bf16[16,1536]{1,0:T(8,128)(2,1)S(1)} %get-tuple-element.146.rest_0_.rest_4_, ...), custom_call_target="tpu_custom_call" | custom-call | tf_op jit(solution)/shard_map/grad_tokens/pallas_call | solution.py:368
  62.3 0.3 collective-permute-start.40
  62.8 0.3 collective-permute-start.46
  63.5 0.8 %grad_tokens.7 = (bf16[96,1024]{1,0:T(8,128)(2,1)S(1)}, f32[32,1024]{1,0:T(8,128)S(1)}, f32[8,128]{1,0:T(8,128)S(1)}) custom-call(f32[128,1024]{1,0:T(8,128)S(1)} %get-tuple-element.157.prev_ref, bf16[1024,1536]{1,0:T(8,128)(2,1)S(1)} %get-tuple-element.114.wg_ref, bf16[1024,1536]{1,0:T(8,128)(2,1)S(1)} %get-tuple-element.115.wu_ref, ...), custom_call_target="tpu_custom_call" | custom-call | tf_op jit(solution)/shard_map/grad_tokens/pallas_call | solution.py:368
  64.4 1.6 %collective-permute-start.41 = (bf16[32,1024]{1,0:T(8,128)(2,1)S(1)}, bf16[32,1024]{1,0:T(8,128)(2,1)S(1)}, u32[]{:S(2)}, u32[]{:S(2)}) collective-permute-start(bf16[32,1024]{1,0:T(8,128)(2,1)S(1)} %get-tuple-element.180), channel_id=1, source_target_pairs={{0,4},{4,0},{8,12},{12,8},{1,5},{5,1},{9,13},{13,9},{2,6},{6,2},{1... | collective-permute-start | bytes 196616 | tf_op jit(solution)/shard_map/ppermute | solution.py:478
  66.0 0.3 collective-permute-start.42
  66.3 2.5 %collective-permute-start.43 = (bf16[32,1024]{1,0:T(8,128)(2,1)S(1)}, bf16[32,1024]{1,0:T(8,128)(2,1)S(1)}, u32[]{:S(2)}, u32[]{:S(2)}) collective-permute-start(bf16[32,1024]{1,0:T(8,128)(2,1)S(1)} %get-tuple-element.178), channel_id=1, source_target_pairs={{0,12},{4,8},{8,4},{12,0},{1,13},{5,9},{9,5},{13,1},{2,14},{6,10},... | collective-permute-start | bytes 196616 | tf_op jit(solution)/shard_map/ppermute | solution.py:478
  68.8 3.6 %weight_grads.6 = (bf16[1024,3584]{1,0:T(8,128)(2,1)}, bf16[1024,3584]{1,0:T(8,128)(2,1)}, bf16[3584,1024]{1,0:T(8,128)(2,1)}, f32[8,128]{1,0:T(8,128)S(1)}) custom-call(bf16[1024,128]{1,0:T(8,128)(2,1)S(1)} %get-tuple-element.140.xt_ref, ...), custom_call_target="tpu_custom_call", output_to_operand_aliasing={{0}: (17, {}), {1}: (18, {}), {2}: (19, {})} | custom-call | tf_op jit(solution)/shard_map/weight_grads/pallas_call | solution.py:400
  72.4 2.2 %weight_grads.7 = (bf16[1024,3584]{1,0:T(8,128)(2,1)}, bf16[1024,3584]{1,0:T(8,128)(2,1)}, bf16[3584,1024]{1,0:T(8,128)(2,1)}, f32[8,128]{1,0:T(8,128)}) custom-call(bf16[1024,128]{1,0:T(8,128)(2,1)S(1)} %get-tuple-element.140.xt_ref, bf16[128,1024]{1,0:T(8,128)(2,1)S(1)} %get-tuple-element.104.og_ref, ...), custom_call_target="tpu_custom_call", output_to_operand_aliasing={{0}: (17, {}), {1}: (18, {}), {2}: (19, {})} | custom-call | tf_op jit(solution)/shard_map/weight_grads/pallas_call | solution.py:400
  74.7 1.2 %finish.1 = bf16[32,1024]{1,0:T(8,128)(2,1)} custom-call(s32[3]{0:T(128)S(1)} %pad_add_fusion.place, f32[32,1024]{1,0:T(8,128)S(1)} %get-tuple-element.162.own_ref, bf16[32,1024]{1,0:T(8,128)(2,1)S(1)} %collective-permute-done.41.rest_0_, bf16[32,1024]{1,0:T(8,128)(2,1)S(1)} %collective-permute-done.42.rest_1_, ...), custom_call_target="tpu_custom_call" | custom-call | tf_op jit(solution)/shard_map/finish/pallas_call | solution.py:440
  (77 shorter events, 4.1 us)
Async XLA Ops:
  1.5 15.9 %collective-permute-start.5 = (bf16[2,32,1024]{2,1,0:T(8,128)(2,1)S(1)}, bf16[2,32,1024]{2,1,0:T(8,128)(2,1)S(1)}, u32[]{:S(2)}, u32[]{:S(2)}) collective-permute-start(bf16[2,32,1024]{2,1,0:T(8,128)(2,1)S(1)} %pad_maximum_fusion.both_ref), channel_id=1, source_target_pairs={{0,8},{4,12},{8,0},{12,4},{1,9},{5,13},{9,1},{13,5},{2,10},{6,14},... | collective-permute-start | bytes 393224 | tf_op jit(solution)/shard_map/ppermute | solution.py:478
  15.2 2.7 %collective-permute-start = (bf16[1,16,2048]{2,1,0:T(8,128)(2,1)S(1)}, bf16[1,16,2048]{2,1,0:T(8,128)(2,1)S(1)}, u32[]{:S(2)}, u32[]{:S(2)}) collective-permute-start(bf16[1,16,2048]{2,1,0:T(8,128)(2,1)S(1)} %get-tuple-element.94), channel_id=1, source_target_pairs={{0,1},{1,0},{2,3},{3,2},{4,5},{5,4},{6,7},{7,6},{8,9},{9,8},{10,11... | collective-permute-start | bytes 196616 | tf_op jit(solution)/shard_map/ppermute | solution.py:475
  15.3 2.6 %collective-permute-start.1 = (bf16[1,16,2048]{2,1,0:T(8,128)(2,1)S(1)}, bf16[1,16,2048]{2,1,0:T(8,128)(2,1)S(1)}, u32[]{:S(2)}, u32[]{:S(2)}) collective-permute-start(bf16[1,16,2048]{2,1,0:T(8,128)(2,1)S(1)} %get-tuple-element.95), channel_id=1, source_target_pairs={{0,1},{1,0},{2,3},{3,2},{4,5},{5,4},{6,7},{7,6},{8,9},{9,8},{10,11... | collective-permute-start | bytes 196616 | tf_op jit(solution)/shard_map/ppermute | solution.py:475
  15.7 2.1 %collective-permute-start.2 = (bf16[1,16,2048]{2,1,0:T(8,128)(2,1)S(1)}, bf16[1,16,2048]{2,1,0:T(8,128)(2,1)S(1)}, u32[]{:S(2)}, u32[]{:S(2)}) collective-permute-start(bf16[1,16,2048]{2,1,0:T(8,128)(2,1)S(1)} %get-tuple-element.96), channel_id=1, source_target_pairs={{0,1},{1,0},{2,3},{3,2},{4,5},{5,4},{6,7},{7,6},{8,9},{9,8},{10,11... | collective-permute-start | bytes 196616 | tf_op jit(solution)/shard_map/ppermute | solution.py:475
  15.8 10.5 %collective-permute-start.4 = (bf16[2,32,1024]{2,1,0:T(8,128)(2,1)S(1)}, bf16[2,32,1024]{2,1,0:T(8,128)(2,1)S(1)}, u32[]{:S(2)}, u32[]{:S(2)}) collective-permute-start(bf16[2,32,1024]{2,1,0:T(8,128)(2,1)S(1)} %pad_maximum_fusion.both_ref), channel_id=1, source_target_pairs={{0,4},{4,0},{8,12},{12,8},{1,5},{5,1},{9,13},{13,9},{2,6},{6,2},{1... | collective-permute-start | bytes 393224 | tf_op jit(solution)/shard_map/ppermute | solution.py:478
  17.4 9.0 %collective-permute-start.6 = (bf16[2,32,1024]{2,1,0:T(8,128)(2,1)S(1)}, bf16[2,32,1024]{2,1,0:T(8,128)(2,1)S(1)}, u32[]{:S(2)}, u32[]{:S(2)}) collective-permute-start(bf16[2,32,1024]{2,1,0:T(8,128)(2,1)S(1)} %collective-permute-done.5.rest_1_), channel_id=1, source_target_pairs={{0,4},{4,0},{8,12},{12,8},{1,5},{5,1},{9,13},{13,9},{2,6},{6,2},{1... | collective-permute-start | bytes 393224 | tf_op jit(solution)/shard_map/ppermute | solution.py:478
  23.4 2.9 %collective-permute-start.7 = (bf16[2,16,1536]{2,1,0:T(8,128)(2,1)S(1)}, bf16[2,16,1536]{2,1,0:T(8,128)(2,1)S(1)}, u32[]{:S(2)}, u32[]{:S(2)}) collective-permute-start(bf16[2,16,1536]{2,1,0:T(8,128)(2,1)S(1)} %get-tuple-element.101), channel_id=1, source_target_pairs={{0,1},{1,0},{2,3},{3,2},{4,5},{5,4},{6,7},{7,6},{8,9},{9,8},{10,11... | collective-permute-start | bytes 294920 | tf_op jit(solution)/shard_map/ppermute | solution.py:475
  23.5 9.9 %collective-permute-start.3 = (bf16[3,16,2048]{2,1,0:T(8,128)(2,1)S(1)}, bf16[3,16,2048]{2,1,0:T(8,128)(2,1)S(1)}, u32[]{:S(2)}, u32[]{:S(2)}) collective-permute-start(bf16[3,16,2048]{2,1,0:T(8,128)(2,1)S(1)} %sum_cores.6.rest_3_.sum_ref), channel_id=1, source_target_pairs={{0,2},{1,3},{2,0},{3,1},{4,6},{5,7},{6,4},{7,5},{8,10},{9,11},{10,... | collective-permute-start | bytes 589832 | tf_op jit(solution)/shard_map/ppermute | solution.py:482
  25.1 1.2 %collective-permute-start.8 = (bf16[1,16,1536]{2,1,0:T(8,128)(2,1)S(1)}, bf16[1,16,1536]{2,1,0:T(8,128)(2,1)S(1)}, u32[]{:S(2)}, u32[]{:S(2)}) collective-permute-start(bf16[1,16,1536]{2,1,0:T(8,128)(2,1)S(1)} %get-tuple-element.102), channel_id=1, source_target_pairs={{0,1},{1,0},{2,3},{3,2},{4,5},{5,4},{6,7},{7,6},{8,9},{9,8},{10,11... | collective-permute-start | bytes 147464 | tf_op jit(solution)/shard_map/ppermute | solution.py:475
  28.5 2.7 %collective-permute-start.10 = (bf16[1,48,1024]{2,1,0:T(8,128)(2,1)S(1)}, bf16[1,48,1024]{2,1,0:T(8,128)(2,1)S(1)}, u32[]{:S(2)}, u32[]{:S(2)}) collective-permute-start(bf16[1,48,1024]{2,1,0:T(8,128)(2,1)S(1)} %get-tuple-element.111), channel_id=1, source_target_pairs={{0,1},{1,0},{2,3},{3,2},{4,5},{5,4},{6,7},{7,6},{8,9},{9,8},{10,11... | collective-permute-start | bytes 294920 | tf_op jit(solution)/shard_map/ppermute | solution.py:475
  28.7 2.6 %collective-permute-start.11 = (bf16[1,48,1024]{2,1,0:T(8,128)(2,1)S(1)}, bf16[1,48,1024]{2,1,0:T(8,128)(2,1)S(1)}, u32[]{:S(2)}, u32[]{:S(2)}) collective-permute-start(bf16[1,48,1024]{2,1,0:T(8,128)(2,1)S(1)} %get-tuple-element.112), channel_id=1, source_target_pairs={{0,1},{1,0},{2,3},{3,2},{4,5},{5,4},{6,7},{7,6},{8,9},{9,8},{10,11... | collective-permute-start | bytes 294920 | tf_op jit(solution)/shard_map/ppermute | solution.py:475
  29.1 2.7 %collective-permute-start.9 = (bf16[1,48,1024]{2,1,0:T(8,128)(2,1)S(1)}, bf16[1,48,1024]{2,1,0:T(8,128)(2,1)S(1)}, u32[]{:S(2)}, u32[]{:S(2)}) collective-permute-start(bf16[1,48,1024]{2,1,0:T(8,128)(2,1)S(1)} %get-tuple-element.110), channel_id=1, source_target_pairs={{0,1},{1,0},{2,3},{3,2},{4,5},{5,4},{6,7},{7,6},{8,9},{9,8},{10,11... | collective-permute-start | bytes 294920 | tf_op jit(solution)/shard_map/ppermute | solution.py:475
  29.3 7.1 %collective-permute-start.14 = (bf16[3,16,1536]{2,1,0:T(8,128)(2,1)S(1)}, bf16[3,16,1536]{2,1,0:T(8,128)(2,1)S(1)}, u32[]{:S(2)}, u32[]{:S(2)}) collective-permute-start(bf16[3,16,1536]{2,1,0:T(8,128)(2,1)S(1)} %sum_cores.7.rest_3_.sum_ref), channel_id=1, source_target_pairs={{0,2},{1,3},{2,0},{3,1},{4,6},{5,7},{6,4},{7,5},{8,10},{9,11},{10,... | collective-permute-start | bytes 442376 | tf_op jit(solution)/shard_map/ppermute | solution.py:482
  31.3 3.8 %collective-permute-start.15 = (bf16[1,48,1024]{2,1,0:T(8,128)(2,1)S(1)}, bf16[1,48,1024]{2,1,0:T(8,128)(2,1)S(1)}, u32[]{:S(2)}, u32[]{:S(2)}) collective-permute-start(bf16[1,48,1024]{2,1,0:T(8,128)(2,1)S(1)} %get-tuple-element.120), channel_id=1, source_target_pairs={{0,1},{1,0},{2,3},{3,2},{4,5},{5,4},{6,7},{7,6},{8,9},{9,8},{10,11... | collective-permute-start | bytes 294920 | tf_op jit(solution)/shard_map/ppermute | solution.py:475
  31.4 4.2 %collective-permute-start.16 = (bf16[1,48,1024]{2,1,0:T(8,128)(2,1)S(1)}, bf16[1,48,1024]{2,1,0:T(8,128)(2,1)S(1)}, u32[]{:S(2)}, u32[]{:S(2)}) collective-permute-start(bf16[1,48,1024]{2,1,0:T(8,128)(2,1)S(1)} %get-tuple-element.121), channel_id=1, source_target_pairs={{0,1},{1,0},{2,3},{3,2},{4,5},{5,4},{6,7},{7,6},{8,9},{9,8},{10,11... | collective-permute-start | bytes 294920 | tf_op jit(solution)/shard_map/ppermute | solution.py:475
  31.9 10.3 %collective-permute-start.13 = (bf16[3,48,1024]{2,1,0:T(8,128)(2,1)S(1)}, bf16[3,48,1024]{2,1,0:T(8,128)(2,1)S(1)}, u32[]{:S(2)}, u32[]{:S(2)}) collective-permute-start(bf16[3,48,1024]{2,1,0:T(8,128)(2,1)S(1)} %sum_cores.8.rest_2_.rest_3_.sum_ref), channel_id=1, source_target_pairs={{0,2},{1,3},{2,0},{3,1},{4,6},{5,7},{6,4},{7,5},{8,10},{9,11},{10,... | collective-permute-start | bytes 884744 | tf_op jit(solution)/shard_map/ppermute | solution.py:482
  33.5 2.2 %collective-permute-start.17 = (bf16[1,48,1024]{2,1,0:T(8,128)(2,1)S(1)}, bf16[1,48,1024]{2,1,0:T(8,128)(2,1)S(1)}, u32[]{:S(2)}, u32[]{:S(2)}) collective-permute-start(bf16[1,48,1024]{2,1,0:T(8,128)(2,1)S(1)} %get-tuple-element.122), channel_id=1, source_target_pairs={{0,1},{1,0},{2,3},{3,2},{4,5},{5,4},{6,7},{7,6},{8,9},{9,8},{10,11... | collective-permute-start | bytes 294920 | tf_op jit(solution)/shard_map/ppermute | solution.py:475
  35.0 2.8 %collective-permute-start.21 = (bf16[1,48,1024]{2,1,0:T(8,128)(2,1)S(1)}, bf16[1,48,1024]{2,1,0:T(8,128)(2,1)S(1)}, u32[]{:S(2)}, u32[]{:S(2)}) collective-permute-start(bf16[1,48,1024]{2,1,0:T(8,128)(2,1)S(1)} %get-tuple-element.129), channel_id=1, source_target_pairs={{0,1},{1,0},{2,3},{3,2},{4,5},{5,4},{6,7},{7,6},{8,9},{9,8},{10,11... | collective-permute-start | bytes 294920 | tf_op jit(solution)/shard_map/ppermute | solution.py:475
  35.6 2.6 %collective-permute-start.22 = (bf16[1,48,1024]{2,1,0:T(8,128)(2,1)S(1)}, bf16[1,48,1024]{2,1,0:T(8,128)(2,1)S(1)}, u32[]{:S(2)}, u32[]{:S(2)}) collective-permute-start(bf16[1,48,1024]{2,1,0:T(8,128)(2,1)S(1)} %get-tuple-element.130), channel_id=1, source_target_pairs={{0,1},{1,0},{2,3},{3,2},{4,5},{5,4},{6,7},{7,6},{8,9},{9,8},{10,11... | collective-permute-start | bytes 294920 | tf_op jit(solution)/shard_map/ppermute | solution.py:475
  35.8 12.8 %collective-permute-start.27 = (bf16[3,48,1024]{2,1,0:T(8,128)(2,1)S(1)}, bf16[3,48,1024]{2,1,0:T(8,128)(2,1)S(1)}, u32[]{:S(2)}, u32[]{:S(2)}) collective-permute-start(bf16[3,48,1024]{2,1,0:T(8,128)(2,1)S(1)} %sum_cores.9.rest_2_.rest_3_.sum_ref), channel_id=1, source_target_pairs={{0,2},{1,3},{2,0},{3,1},{4,6},{5,7},{6,4},{7,5},{8,10},{9,11},{10,... | collective-permute-start | bytes 884744 | tf_op jit(solution)/shard_map/ppermute | solution.py:482
  36.4 2.0 %collective-permute-start.23 = (bf16[1,48,1024]{2,1,0:T(8,128)(2,1)S(1)}, bf16[1,48,1024]{2,1,0:T(8,128)(2,1)S(1)}, u32[]{:S(2)}, u32[]{:S(2)}) collective-permute-start(bf16[1,48,1024]{2,1,0:T(8,128)(2,1)S(1)} %get-tuple-element.131), channel_id=1, source_target_pairs={{0,1},{1,0},{2,3},{3,2},{4,5},{5,4},{6,7},{7,6},{8,9},{9,8},{10,11... | collective-permute-start | bytes 294920 | tf_op jit(solution)/shard_map/ppermute | solution.py:475
  37.8 2.1 %collective-permute-start.18 = (bf16[1,48,512]{2,1,0:T(8,128)(2,1)S(1)}, bf16[1,48,512]{2,1,0:T(8,128)(2,1)S(1)}, u32[]{:S(2)}, u32[]{:S(2)}) collective-permute-start(bf16[1,48,512]{2,1,0:T(8,128)(2,1)S(1)} %get-tuple-element.125), channel_id=1, source_target_pairs={{0,1},{1,0},{2,3},{3,2},{4,5},{5,4},{6,7},{7,6},{8,9},{9,8},{10,11... | collective-permute-start | bytes 147464 | tf_op jit(solution)/shard_map/ppermute | solution.py:475
  38.2 1.9 %collective-permute-start.19 = (bf16[1,48,512]{2,1,0:T(8,128)(2,1)S(1)}, bf16[1,48,512]{2,1,0:T(8,128)(2,1)S(1)}, u32[]{:S(2)}, u32[]{:S(2)}) collective-permute-start(bf16[1,48,512]{2,1,0:T(8,128)(2,1)S(1)} %get-tuple-element.126), channel_id=1, source_target_pairs={{0,1},{1,0},{2,3},{3,2},{4,5},{5,4},{6,7},{7,6},{8,9},{9,8},{10,11... | collective-permute-start | bytes 147464 | tf_op jit(solution)/shard_map/ppermute | solution.py:475
  38.4 17.2 %collective-permute-start.33 = (bf16[3,48,1024]{2,1,0:T(8,128)(2,1)S(1)}, bf16[3,48,1024]{2,1,0:T(8,128)(2,1)S(1)}, u32[]{:S(2)}, u32[]{:S(2)}) collective-permute-start(bf16[3,48,1024]{2,1,0:T(8,128)(2,1)S(1)} %sum_cores.10.rest_3_.sum_ref), channel_id=1, source_target_pairs={{0,2},{1,3},{2,0},{3,1},{4,6},{5,7},{6,4},{7,5},{8,10},{9,11},{10,... | collective-permute-start | bytes 884744 | tf_op jit(solution)/shard_map/ppermute | solution.py:482
  40.0 3.0 %collective-permute-start.12 = (bf16[16,2048]{1,0:T(8,128)(2,1)S(1)}, bf16[16,2048]{1,0:T(8,128)(2,1)S(1)}, u32[]{:S(2)}, u32[]{:S(2)}) collective-permute-start(bf16[16,2048]{1,0:T(8,128)(2,1)S(1)} %get-tuple-element.113.rest_0_.rest_4_), channel_id=1, source_target_pairs={{0,1},{1,0},{2,3},{3,2},{4,5},{5,4},{6,7},{7,6},{8,9},{9,8},{10,11... | collective-permute-start | bytes 196616 | tf_op jit(solution)/shard_map/ppermute | solution.py:475
  40.0 1.3 %collective-permute-start.20 = (bf16[1,48,512]{2,1,0:T(8,128)(2,1)S(1)}, bf16[1,48,512]{2,1,0:T(8,128)(2,1)S(1)}, u32[]{:S(2)}, u32[]{:S(2)}) collective-permute-start(bf16[1,48,512]{2,1,0:T(8,128)(2,1)S(1)} %get-tuple-element.127), channel_id=1, source_target_pairs={{0,1},{1,0},{2,3},{3,2},{4,5},{5,4},{6,7},{7,6},{8,9},{9,8},{10,11... | collective-permute-start | bytes 147464 | tf_op jit(solution)/shard_map/ppermute | solution.py:475
  42.4 1.8 %collective-permute-start.24 = (bf16[48,1024]{1,0:T(8,128)(2,1)S(1)}, bf16[48,1024]{1,0:T(8,128)(2,1)S(1)}, u32[]{:S(2)}, u32[]{:S(2)}) collective-permute-start(bf16[48,1024]{1,0:T(8,128)(2,1)S(1)} %get-tuple-element.132.rest_2_.rest_6_), channel_id=1, source_target_pairs={{0,1},{1,0},{2,3},{3,2},{4,5},{5,4},{6,7},{7,6},{8,9},{9,8},{10,11... | collective-permute-start | bytes 294920 | tf_op jit(solution)/shard_map/ppermute | solution.py:475
  42.5 1.4 %collective-permute-start.25 = (bf16[16,2048]{1,0:T(8,128)(2,1)S(1)}, bf16[16,2048]{1,0:T(8,128)(2,1)S(1)}, u32[]{:S(2)}, u32[]{:S(2)}) collective-permute-start(bf16[16,2048]{1,0:T(8,128)(2,1)S(1)} %get-tuple-element.133.rest_4_.rest_8_), channel_id=1, source_target_pairs={{0,1},{1,0},{2,3},{3,2},{4,5},{5,4},{6,7},{7,6},{8,9},{9,8},{10,11... | collective-permute-start | bytes 196616 | tf_op jit(solution)/shard_map/ppermute | solution.py:475
  43.0 1.4 %collective-permute-start.26 = (bf16[48,1024]{1,0:T(8,128)(2,1)S(1)}, bf16[48,1024]{1,0:T(8,128)(2,1)S(1)}, u32[]{:S(2)}, u32[]{:S(2)}) collective-permute-start(bf16[48,1024]{1,0:T(8,128)(2,1)S(1)} %get-tuple-element.134.rest_6_.rest_10_), channel_id=1, source_target_pairs={{0,1},{1,0},{2,3},{3,2},{4,5},{5,4},{6,7},{7,6},{8,9},{9,8},{10,11... | collective-permute-start | bytes 294920 | tf_op jit(solution)/shard_map/ppermute | solution.py:475
  43.9 5.5 %collective-permute-start.31 = (bf16[48,1024]{1,0:T(8,128)(2,1)S(1)}, bf16[48,1024]{1,0:T(8,128)(2,1)S(1)}, u32[]{:S(2)}, u32[]{:S(2)}) collective-permute-start(bf16[48,1024]{1,0:T(8,128)(2,1)S(1)} %get-tuple-element.142.rest_2_), channel_id=1, source_target_pairs={{0,1},{1,0},{2,3},{3,2},{4,5},{5,4},{6,7},{7,6},{8,9},{9,8},{10,11... | collective-permute-start | bytes 294920 | tf_op jit(solution)/shard_map/ppermute | solution.py:475
  44.2 5.1 %collective-permute-start.30 = (bf16[16,2048]{1,0:T(8,128)(2,1)S(1)}, bf16[16,2048]{1,0:T(8,128)(2,1)S(1)}, u32[]{:S(2)}, u32[]{:S(2)}) collective-permute-start(bf16[16,2048]{1,0:T(8,128)(2,1)S(1)} %get-tuple-element.141.rest_0_), channel_id=1, source_target_pairs={{0,1},{1,0},{2,3},{3,2},{4,5},{5,4},{6,7},{7,6},{8,9},{9,8},{10,11... | collective-permute-start | bytes 196616 | tf_op jit(solution)/shard_map/ppermute | solution.py:475
  48.7 5.3 %collective-permute-start.28 = (bf16[48,1024]{1,0:T(8,128)(2,1)S(1)}, bf16[48,1024]{1,0:T(8,128)(2,1)S(1)}, u32[]{:S(2)}, u32[]{:S(2)}) collective-permute-start(bf16[48,1024]{1,0:T(8,128)(2,1)S(1)} %get-tuple-element.138.rest_2_.rest_6_), channel_id=1, source_target_pairs={{0,1},{1,0},{2,3},{3,2},{4,5},{5,4},{6,7},{7,6},{8,9},{9,8},{10,11... | collective-permute-start | bytes 294920 | tf_op jit(solution)/shard_map/ppermute | solution.py:475
  48.8 5.3 %collective-permute-start.29 = (bf16[48,1024]{1,0:T(8,128)(2,1)S(1)}, bf16[48,1024]{1,0:T(8,128)(2,1)S(1)}, u32[]{:S(2)}, u32[]{:S(2)}) collective-permute-start(bf16[48,1024]{1,0:T(8,128)(2,1)S(1)} %get-tuple-element.139.rest_6_.rest_10_), channel_id=1, source_target_pairs={{0,1},{1,0},{2,3},{3,2},{4,5},{5,4},{6,7},{7,6},{8,9},{9,8},{10,11... | collective-permute-start | bytes 294920 | tf_op jit(solution)/shard_map/ppermute | solution.py:475
  49.3 7.2 %collective-permute-start.37 = (bf16[48,1024]{1,0:T(8,128)(2,1)S(1)}, bf16[48,1024]{1,0:T(8,128)(2,1)S(1)}, u32[]{:S(2)}, u32[]{:S(2)}) collective-permute-start(bf16[48,1024]{1,0:T(8,128)(2,1)S(1)} %get-tuple-element.151.rest_2_), channel_id=1, source_target_pairs={{0,1},{1,0},{2,3},{3,2},{4,5},{5,4},{6,7},{7,6},{8,9},{9,8},{10,11... | collective-permute-start | bytes 294920 | tf_op jit(solution)/shard_map/ppermute | solution.py:475
  49.4 12.6 %collective-permute-start.38 = (bf16[3,48,512]{2,1,0:T(8,128)(2,1)S(1)}, bf16[3,48,512]{2,1,0:T(8,128)(2,1)S(1)}, u32[]{:S(2)}, u32[]{:S(2)}) collective-permute-start(bf16[3,48,512]{2,1,0:T(8,128)(2,1)S(1)} %sum_cores.11.rest_1_.sum_ref), channel_id=1, source_target_pairs={{0,2},{1,3},{2,0},{3,1},{4,6},{5,7},{6,4},{7,5},{8,10},{9,11},{10,... | collective-permute-start | bytes 442376 | tf_op jit(solution)/shard_map/ppermute | solution.py:482
  55.8 4.7 %collective-permute-start.34 = (bf16[48,1024]{1,0:T(8,128)(2,1)S(1)}, bf16[48,1024]{1,0:T(8,128)(2,1)S(1)}, u32[]{:S(2)}, u32[]{:S(2)}) collective-permute-start(bf16[48,1024]{1,0:T(8,128)(2,1)S(1)} %get-tuple-element.148.rest_2_.rest_6_), channel_id=1, source_target_pairs={{0,1},{1,0},{2,3},{3,2},{4,5},{5,4},{6,7},{7,6},{8,9},{9,8},{10,11... | collective-permute-start | bytes 294920 | tf_op jit(solution)/shard_map/ppermute | solution.py:475
  56.0 4.5 %collective-permute-start.36 = (bf16[48,1024]{1,0:T(8,128)(2,1)S(1)}, bf16[48,1024]{1,0:T(8,128)(2,1)S(1)}, u32[]{:S(2)}, u32[]{:S(2)}) collective-permute-start(bf16[48,1024]{1,0:T(8,128)(2,1)S(1)} %get-tuple-element.150.rest_6_.rest_10_), channel_id=1, source_target_pairs={{0,1},{1,0},{2,3},{3,2},{4,5},{5,4},{6,7},{7,6},{8,9},{9,8},{10,11... | collective-permute-start | bytes 294920 | tf_op jit(solution)/shard_map/ppermute | solution.py:475
  56.3 4.1 %collective-permute-start.32 = (bf16[16,1536]{1,0:T(8,128)(2,1)S(1)}, bf16[16,1536]{1,0:T(8,128)(2,1)S(1)}, u32[]{:S(2)}, u32[]{:S(2)}) collective-permute-start(bf16[16,1536]{1,0:T(8,128)(2,1)S(1)} %get-tuple-element.146.rest_0_.rest_4_), channel_id=1, source_target_pairs={{0,1},{1,0},{2,3},{3,2},{4,5},{5,4},{6,7},{7,6},{8,9},{9,8},{10,11... | collective-permute-start | bytes 147464 | tf_op jit(solution)/shard_map/ppermute | solution.py:475
  56.5 4.0 %collective-permute-start.35 = (bf16[16,1536]{1,0:T(8,128)(2,1)S(1)}, bf16[16,1536]{1,0:T(8,128)(2,1)S(1)}, u32[]{:S(2)}, u32[]{:S(2)}) collective-permute-start(bf16[16,1536]{1,0:T(8,128)(2,1)S(1)} %get-tuple-element.149.rest_4_.rest_8_), channel_id=1, source_target_pairs={{0,1},{1,0},{2,3},{3,2},{4,5},{5,4},{6,7},{7,6},{8,9},{9,8},{10,11... | collective-permute-start | bytes 147464 | tf_op jit(solution)/shard_map/ppermute | solution.py:475
  62.1 1.3 %collective-permute-start.39 = (bf16[48,512]{1,0:T(8,128)(2,1)S(1)}, bf16[48,512]{1,0:T(8,128)(2,1)S(1)}, u32[]{:S(2)}, u32[]{:S(2)}) collective-permute-start(bf16[48,512]{1,0:T(8,128)(2,1)S(1)} %get-tuple-element.159.rest_2_.rest_6_), channel_id=1, source_target_pairs={{0,1},{1,0},{2,3},{3,2},{4,5},{5,4},{6,7},{7,6},{8,9},{9,8},{10,11... | collective-permute-start | bytes 147464 | tf_op jit(solution)/shard_map/ppermute | solution.py:475
  62.3 1.2 %collective-permute-start.40 = (bf16[48,512]{1,0:T(8,128)(2,1)S(1)}, bf16[48,512]{1,0:T(8,128)(2,1)S(1)}, u32[]{:S(2)}, u32[]{:S(2)}) collective-permute-start(bf16[48,512]{1,0:T(8,128)(2,1)S(1)} %get-tuple-element.160.rest_6_.rest_10_), channel_id=1, source_target_pairs={{0,1},{1,0},{2,3},{3,2},{4,5},{5,4},{6,7},{7,6},{8,9},{9,8},{10,11... | collective-permute-start | bytes 147464 | tf_op jit(solution)/shard_map/ppermute | solution.py:475
  62.7 6.2 %collective-permute-start.44 = (bf16[16,1536]{1,0:T(8,128)(2,1)S(1)}, bf16[16,1536]{1,0:T(8,128)(2,1)S(1)}, u32[]{:S(2)}, u32[]{:S(2)}) collective-permute-start(bf16[16,1536]{1,0:T(8,128)(2,1)S(1)} %get-tuple-element.164.rest_0_), channel_id=1, source_target_pairs={{0,1},{1,0},{2,3},{3,2},{4,5},{5,4},{6,7},{7,6},{8,9},{9,8},{10,11... | collective-permute-start | bytes 147464 | tf_op jit(solution)/shard_map/ppermute | solution.py:475
  62.8 6.0 %collective-permute-start.46 = (bf16[48,1024]{1,0:T(8,128)(2,1)S(1)}, bf16[48,1024]{1,0:T(8,128)(2,1)S(1)}, u32[]{:S(2)}, u32[]{:S(2)}) collective-permute-start(bf16[48,1024]{1,0:T(8,128)(2,1)S(1)} %get-tuple-element.166.rest_2_), channel_id=1, source_target_pairs={{0,1},{1,0},{2,3},{3,2},{4,5},{5,4},{6,7},{7,6},{8,9},{9,8},{10,11... | collective-permute-start | bytes 294920 | tf_op jit(solution)/shard_map/ppermute | solution.py:475
  64.4 10.3 %collective-permute-start.41 = (bf16[32,1024]{1,0:T(8,128)(2,1)S(1)}, bf16[32,1024]{1,0:T(8,128)(2,1)S(1)}, u32[]{:S(2)}, u32[]{:S(2)}) collective-permute-start(bf16[32,1024]{1,0:T(8,128)(2,1)S(1)} %get-tuple-element.180), channel_id=1, source_target_pairs={{0,4},{4,0},{8,12},{12,8},{1,5},{5,1},{9,13},{13,9},{2,6},{6,2},{1... | collective-permute-start | bytes 196616 | tf_op jit(solution)/shard_map/ppermute | solution.py:478
  66.0 8.7 %collective-permute-start.42 = (bf16[32,1024]{1,0:T(8,128)(2,1)S(1)}, bf16[32,1024]{1,0:T(8,128)(2,1)S(1)}, u32[]{:S(2)}, u32[]{:S(2)}) collective-permute-start(bf16[32,1024]{1,0:T(8,128)(2,1)S(1)} %get-tuple-element.179), channel_id=1, source_target_pairs={{0,8},{4,12},{8,0},{12,4},{1,9},{5,13},{9,1},{13,5},{2,10},{6,14},... | collective-permute-start | bytes 196616 | tf_op jit(solution)/shard_map/ppermute | solution.py:478
  66.3 8.3 %collective-permute-start.43 = (bf16[32,1024]{1,0:T(8,128)(2,1)S(1)}, bf16[32,1024]{1,0:T(8,128)(2,1)S(1)}, u32[]{:S(2)}, u32[]{:S(2)}) collective-permute-start(bf16[32,1024]{1,0:T(8,128)(2,1)S(1)} %get-tuple-element.178), channel_id=1, source_target_pairs={{0,12},{4,8},{8,4},{12,0},{1,13},{5,9},{9,5},{13,1},{2,14},{6,10},... | collective-permute-start | bytes 196616 | tf_op jit(solution)/shard_map/ppermute | solution.py:478
  68.8 3.6 %collective-permute-start.45 = (bf16[48,512]{1,0:T(8,128)(2,1)S(1)}, bf16[48,512]{1,0:T(8,128)(2,1)S(1)}, u32[]{:S(2)}, u32[]{:S(2)}) collective-permute-start(bf16[48,512]{1,0:T(8,128)(2,1)S(1)} %get-tuple-element.165.rest_2_), channel_id=1, source_target_pairs={{0,1},{1,0},{2,3},{3,2},{4,5},{5,4},{6,7},{7,6},{8,9},{9,8},{10,11... | collective-permute-start | bytes 147464 | tf_op jit(solution)/shard_map/ppermute | solution.py:475

commit v5 on v4

--- a/solution.py
+++ b/solution.py
@@ -376,29 +376,37 @@
     )(*prevs, in_vmem(wg), in_vmem(wu), *[p[1] for p in parts], *[p[2] for p in parts], *deps)
 
 
-def weight_grads_kernel(n, granule, xt_ref, og_ref, gk_ref, uk_ref, dk_ref, *rest):
+def weight_grads_kernel(n, n_own, begins, granule, xt_ref, og_ref, gk_ref, uk_ref, dk_ref, *rest):
     gate_ref, up_ref, down_ref, tok_ref = rest[-4:]
     tok_ref[...] = jnp.zeros_like(tok_ref)
-    hidden, gate_act, up_act = [
-        jnp.concatenate([p[...] for p in rest[k * n : (k + 1) * n]], axis=0) for k in range(3)
-    ]
+    acts = []
+    for k in range(3):
+        refs = rest[k * n : (k + 1) * n]
+        pieces = [p[...] for p in refs[:n_own]]
+        for j in range(2):
+            piece = refs[n_own + j][...]
+            for w in range(1, len(begins)):
+                piece = jnp.where(pl.program_id(0) >= begins[w], refs[n_own + 2 * w + j][...], piece)
+            pieces.append(piece)
+        acts.append(jnp.concatenate(pieces, axis=0))
+    hidden, gate_act, up_act = acts
     for act, keep, out_ref in ((gate_act, gk_ref, gate_ref), (up_act, uk_ref, up_ref)):
         value = jnp.dot(xt_ref[...], act, preferred_element_type=F32).astype(BF)
         out_ref[...] = mask_rows(value, keep[...], BLK)
     down_ref[...] = mask_rows(dot_tn(hidden, og_ref[...]).astype(BF), dk_ref[...], granule)
 
 
-def weight_grads(prev, xt, og, gk, uk, dk, weight_start, parts, starts, first, tiles, tile, units, granule, deps):
+def weight_grads(prev, xt, og, gk, uk, dk, weight_start, parts, maps, begins, first, tiles, tile, units, granule, deps):
     feats, rows = xt.shape
     span = tiles * tile
     n_prev = 0 if prev is None else 3
     base = 5 + 3 * len(parts)
 
-    def moved(s, i):
-        return (0, s + i)
+    def moved(s, least, most, i):
+        return (0, jnp.clip(s + i, least, most))
 
     return pl.pallas_call(
-        functools.partial(weight_grads_kernel, len(parts), granule),
+        functools.partial(weight_grads_kernel, len(parts), 2, begins, granule),
         out_shape=(
             pltpu.HBM((feats, units), BF),
             pltpu.HBM((feats, units), BF),
@@ -413,7 +421,7 @@
             pl.BlockSpec((uk.shape[0], tile), lambda i: (0, weight_start + i)),
             pl.BlockSpec((tile // granule * LANE, feats), lambda i: (weight_start + i, 0)),
         ]
-        + [pl.BlockSpec((p[0].shape[0], tile), functools.partial(moved, s)) for p, s in zip(parts, starts)] * 3
+        + [pl.BlockSpec((p[0].shape[0], tile), functools.partial(moved, *m)) for p, m in zip(parts, maps)] * 3
         + [ANY] * (n_prev + len(deps)),
         out_specs=[
             pl.BlockSpec((feats, tile), lambda i: (0, first + i)),
@@ -543,10 +551,16 @@
 
     grads, gt, pending = None, None, []
 
-    def flush(grads, work, deps):
-        first, size, g, offset, parts, starts = work
+    def flush(grads, works, deps):
+        first, _, g, offset, parts, _ = works[0]
+        total = sum(work[1] for work in works)
+        parts, maps, begins = list(parts[:2]), [(offset, offset, offset + total - 1)] * 2, []
+        for work in works:
+            begins.append(work[0] - first)
+            parts += work[4][2:]
+            maps += [(first - work[0], 0, work[1] - 1)] * 2
         *grads, tok = weight_grads(
-            grads, xt_all, og_all, *keeps, first, parts, starts, first, size, tile, units, granule, deps
+            grads, xt_all, og_all, *keeps, first, parts, maps, begins, first, total, tile, units, granule, deps
         )
         return grads, (tok,)
 
@@ -557,15 +571,19 @@
         parts = (*own_parts[g], mine, swap_cores(mine))
         last = c == len(far_chunks) - 1
         if pending and not (last and DEFER):
-            grads, deps = flush(grads, pending.pop(0), deps)
+            grads, deps = flush(grads, [pending.pop(0)], deps)
         offsets = (offset * tile, offset * tile, 0, 0)
         gt, *rest, tok = grad_tokens_of(
             gt, *groups[g][:2], offset * tile, parts, offsets, size * tile, own if last else 0, deps
         )
         deps = (tok,)
         pending.append((first, size, g, offset, parts, (offset, offset, 0, 0)))
-    for work in pending:
-        grads, deps = flush(grads, work, deps)
+    if len({work[2] for work in pending}) == 1:
+        pending = [pending]
+    else:
+        pending = [[work] for work in pending]
+    for works in pending:
+        grads, deps = flush(grads, works, deps)
 
     if n_row == 4:
         arrived = [flipped(gt[(d - 1) * own : d * own], d) for d in range(1, n_row)]

time: 76.2 us -> 76.4 us (level)
  waiting for transfers between devices: 6.73 us -> 7.92 us
  Pallas kernels: 41.8 us -> 40.8 us
    ppermute x35, waiting for transfers between devices: 3.22 us -> 4.44 us  [swap_cores(): return [lax.ppermute(value, 'col', core_swap) for value in values]]
    pallas_call x4 -> x3, Pallas kernels: 13 us -> 12 us  [weight_grads(): pl.pallas_call(functools.partial(weight_grads_kernel, len(parts), 2, begi...]
  transfers between devices with their start and end apart: 47 -> 47, of which waited for: 7 -> 8; matrix products, arithmetic and copies ran while one was open for 0% -> 0% of each run, Pallas kernels for 53% -> 52%
where the time goes in v5:
time: 76.4 us; the launch traced here: 76.1 us
  Pallas kernels  40.8 us (53%)
  starting transfers between devices  25.5 us (33%)
  waiting for transfers between devices  7.92 us (10%)
  other arithmetic  0.96 us (1%)
  between operations  0.91 us (1%)
    pallas_call x2, Pallas kernels, open_weights(): pl.pallas_call(functools.partial(open_kernel, len(deps), pieces, opener,...  15 us
    pallas_call x3, Pallas kernels, weight_grads(): pl.pallas_call(functools.partial(weight_grads_kernel, len(parts), 2, begi...  12 us
    ppermute x6, starting transfers between devices, flipped(): return lax.ppermute(value, 'row', [(i, i ^ d) for i in range(n_row)])  10.6 us
    ppermute x35, starting transfers between devices, swap_cores(): return [lax.ppermute(value, 'col', core_swap) for value in values]  8.02 us
    ppermute x6, starting transfers between devices, from_chips(): lax.ppermute(value, 'col', [(i, (i + 2 * d) % n_col) for i in range(n_col)])  6.9 us
    pallas_call x4, Pallas kernels, forward(): pl.pallas_call(functools.partial(forward_kernel, pieces, own, offset, spa...  5.57 us
    pallas_call x4, Pallas kernels, grad_tokens_of(): pl.pallas_call(kernel, out_shape=(*outs, TOKEN), in_specs=[VMEM] * (len(p...  5.27 us
    ppermute x35, waiting for transfers between devices, swap_cores(): return [lax.ppermute(value, 'col', core_swap) for value in values]  4.44 us
  transfers between devices with their start and end apart: 47, of which 8 were waited for; matrix products, arithmetic and copies ran while one was open for 0% of the time, Pallas kernels for 52%

profile of v5, /device:TPU:0, one launch (start us, length us, event | category | flops | bytes accessed | tf_op | source)
XLA Modules:
  0.0 76.1 jit_solution(2975045534980076715)
XLA Ops:
  0.6 0.9 %pad_maximum_fusion.both_ref = bf16[2,32,1024]{2,1,0:T(8,128)(2,1)S(1)} fusion(bf16[1,32,1024]{2,1,0:T(8,128)(2,1)} %bitcast.6, bf16[1,32,1024]{2,1,0:T(8,128)(2,1)} %bitcast.7), kind=kLoop, calls=%fused_computation | loop fusion | flops 65536 | bytes 262144 | tf_op jit(solution)/shard_map/stack | solution.py:494
  1.5 4.1 %collective-permute-start.5 = (bf16[2,32,1024]{2,1,0:T(8,128)(2,1)S(1)}, bf16[2,32,1024]{2,1,0:T(8,128)(2,1)S(1)}, u32[]{:S(2)}, u32[]{:S(2)}) collective-permute-start(bf16[2,32,1024]{2,1,0:T(8,128)(2,1)S(1)} %pad_maximum_fusion.both_ref), channel_id=1, source_target_pairs={{0,8},{4,12},{8,0},{12,4},{1,9},{5,13},{9,1},{13,5},{2,10},{6,14},... | collective-permute-start | bytes 393224 | tf_op jit(solution)/shard_map/ppermute | solution.py:486
  5.7 9.5 %open_weights.2 = (bf16[3,16,2048]{2,1,0:T(8,128)(2,1)S(1)}, bf16[1,16,2048]{2,1,0:T(8,128)(2,1)S(1)}, bf16[1,16,2048]{2,1,0:T(8,128)(2,1)S(1)}, bf16[1,16,2048]...) custom-call(s32[3]{0:T(128)S(1)} %pad_add_fusion.place, ...), custom_call_target="tpu_custom_call" | custom-call | tf_op jit(solution)/shard_map/open_weights/pallas_call | solution.py:184
  15.3 0.5 collective-permute-start.1
  15.8 1.6 %collective-permute-start.4 = (bf16[2,32,1024]{2,1,0:T(8,128)(2,1)S(1)}, bf16[2,32,1024]{2,1,0:T(8,128)(2,1)S(1)}, u32[]{:S(2)}, u32[]{:S(2)}) collective-permute-start(bf16[2,32,1024]{2,1,0:T(8,128)(2,1)S(1)} %pad_maximum_fusion.both_ref), channel_id=1, source_target_pairs={{0,4},{4,0},{8,12},{12,8},{1,5},{5,1},{9,13},{13,9},{2,6},{6,2},{1... | collective-permute-start | bytes 393224 | tf_op jit(solution)/shard_map/ppermute | solution.py:486
  17.4 0.4 collective-permute-start.6
  17.9 5.5 %open_weights.3 = (bf16[3,16,1536]{2,1,0:T(8,128)(2,1)S(1)}, bf16[2,16,1536]{2,1,0:T(8,128)(2,1)S(1)}, bf16[1,16,1536]{2,1,0:T(8,128)(2,1)S(1)}, bf16[1024,1536]...) custom-call(s32[3]{0:T(128)S(1)} %pad_add_fusion.place, ...), custom_call_target="tpu_custom_call" | custom-call | tf_op jit(solution)/shard_map/open_weights/pallas_call | solution.py:184
  23.5 1.6 %collective-permute-start.3 = (bf16[3,16,2048]{2,1,0:T(8,128)(2,1)S(1)}, bf16[3,16,2048]{2,1,0:T(8,128)(2,1)S(1)}, u32[]{:S(2)}, u32[]{:S(2)}) collective-permute-start(bf16[3,16,2048]{2,1,0:T(8,128)(2,1)S(1)} %sum_cores.6.rest_3_.sum_ref), channel_id=1, source_target_pairs={{0,2},{1,3},{2,0},{3,1},{4,6},{5,7},{6,4},{7,5},{8,10},{9,11},{10,... | collective-permute-start | bytes 589832 | tf_op jit(solution)/shard_map/ppermute | solution.py:490
  25.3 1.1 %collective-permute-done.8.rest_1_ = bf16[1,16,1536]{2,1,0:T(8,128)(2,1)S(1)} collective-permute-done((bf16[1,16,1536]{2,1,0:T(8,128)(2,1)S(1)}, bf16[1,16,1536]{2,1,0:T(8,128)(2,1)S(1)}, u32[]{:S(2)}, u32[]{:S(2)}) %collective-permute-start.8) | collective-permute-done | bytes 49184 | tf_op jit(solution)/shard_map/ppermute | solution.py:483
  26.4 0.7 all_tokens.1
  27.1 1.5 %forward.4 = (bf16[3,48,1024]{2,1,0:T(8,128)(2,1)S(1)}, bf16[1,48,1024]{2,1,0:T(8,128)(2,1)S(1)}, bf16[1,48,1024]{2,1,0:T(8,128)(2,1)S(1)}, bf16[1,48,1024]{2,1,0:T(8,128)(2,1)S(1)}, f32[8,128]{1,0:T(8,128)S(1)}) custom-call(bf16[128,1024]{1,0:T(8,128)(2,1)S(1)} %get-tuple-element.99.x_ref, bf16[128,1024]{1,0:T(8,128)(2,1)S(1)} %get-tuple-element.100.og_ref, ...), custom_call_target="tpu_custom_call" | custom-call | tf_op jit(solution)/shard_map/forward/pallas_call | solution.py:227
  28.5 0.2 collective-permute-start.10
  28.8 0.3 collective-permute-start.11
  29.3 0.5 collective-permute-start.14
  29.8 1.5 %forward.5 = (bf16[3,48,1024]{2,1,0:T(8,128)(2,1)S(1)}, bf16[1,48,1024]{2,1,0:T(8,128)(2,1)S(1)}, bf16[1,48,1024]{2,1,0:T(8,128)(2,1)S(1)}, bf16[1,48,1024]{2,1,0:T(8,128)(2,1)S(1)}, f32[8,128]{1,0:T(8,128)S(1)}) custom-call(bf16[128,1024]{1,0:T(8,128)(2,1)S(1)} %get-tuple-element.99.x_ref, bf16[128,1024]{1,0:T(8,128)(2,1)S(1)} %get-tuple-element.100.og_ref, ...), custom_call_target="tpu_custom_call" | custom-call | tf_op jit(solution)/shard_map/forward/pallas_call | solution.py:227
  31.4 0.4 collective-permute-start.16
  31.9 1.6 %collective-permute-start.13 = (bf16[3,48,1024]{2,1,0:T(8,128)(2,1)S(1)}, bf16[3,48,1024]{2,1,0:T(8,128)(2,1)S(1)}, u32[]{:S(2)}, u32[]{:S(2)}) collective-permute-start(bf16[3,48,1024]{2,1,0:T(8,128)(2,1)S(1)} %sum_cores.8.rest_2_.rest_3_.sum_ref), channel_id=1, source_target_pairs={{0,2},{1,3},{2,0},{3,1},{4,6},{5,7},{6,4},{7,5},{8,10},{9,11},{10,... | collective-permute-start | bytes 884744 | tf_op jit(solution)/shard_map/ppermute | solution.py:490
  33.6 1.4 %forward.6 = (bf16[3,48,1024]{2,1,0:T(8,128)(2,1)S(1)}, bf16[1,48,1024]{2,1,0:T(8,128)(2,1)S(1)}, bf16[1,48,1024]{2,1,0:T(8,128)(2,1)S(1)}, bf16[1,48,1024]{2,1,0:T(8,128)(2,1)S(1)}, f32[8,128]{1,0:T(8,128)S(1)}) custom-call(bf16[128,1024]{1,0:T(8,128)(2,1)S(1)} %get-tuple-element.99.x_ref, bf16[128,1024]{1,0:T(8,128)(2,1)S(1)} %get-tuple-element.100.og_ref, ...), custom_call_target="tpu_custom_call" | custom-call | tf_op jit(solution)/shard_map/forward/pallas_call | solution.py:227
  35.0 0.6 collective-permute-start.21
  35.8 0.6 collective-permute-start.27
  36.6 1.2 %forward.7 = (bf16[3,48,512]{2,1,0:T(8,128)(2,1)S(1)}, bf16[1,48,512]{2,1,0:T(8,128)(2,1)S(1)}, bf16[1,48,512]{2,1,0:T(8,128)(2,1)S(1)}, bf16[1,48,512]{2,1,0:T(8,128)(2,1)S(1)}, f32[8,128]{1,0:T(8,128)}) custom-call(bf16[128,1024]{1,0:T(8,128)(2,1)S(1)} %get-tuple-element.99.x_ref, bf16[128,1024]{1,0:T(8,128)(2,1)S(1)} %get-tuple-element.100.og_ref, ...), custom_call_target="tpu_custom_call" | custom-call | tf_op jit(solution)/shard_map/forward/pallas_call | solution.py:227
  37.9 0.4 collective-permute-start.18
  38.5 1.6 %collective-permute-start.33 = (bf16[3,48,1024]{2,1,0:T(8,128)(2,1)S(1)}, bf16[3,48,1024]{2,1,0:T(8,128)(2,1)S(1)}, u32[]{:S(2)}, u32[]{:S(2)}) collective-permute-start(bf16[3,48,1024]{2,1,0:T(8,128)(2,1)S(1)} %sum_cores.10.rest_3_.sum_ref), channel_id=1, source_target_pairs={{0,2},{1,3},{2,0},{3,1},{4,6},{5,7},{6,4},{7,5},{8,10},{9,11},{10,... | collective-permute-start | bytes 884744 | tf_op jit(solution)/shard_map/ppermute | solution.py:490
  40.1 0.4 collective-permute-start.20
  40.5 0.9 %collective-permute-done.20.rest_2_ = bf16[1,48,512]{2,1,0:T(8,128)(2,1)S(1)} collective-permute-done((bf16[1,48,512]{2,1,0:T(8,128)(2,1)S(1)}, bf16[1,48,512]{2,1,0:T(8,128)(2,1)S(1)}, u32[]{:S(2)}, u32[]{:S(2)}) %collective-permute-start.20) | collective-permute-done | bytes 49184 | tf_op jit(solution)/shard_map/ppermute | solution.py:483
  41.4 0.8 %collective-permute-done.13.rest_0_ = bf16[3,48,1024]{2,1,0:T(8,128)(2,1)S(1)} collective-permute-done((bf16[3,48,1024]{2,1,0:T(8,128)(2,1)S(1)}, bf16[3,48,1024]{2,1,0:T(8,128)(2,1)S(1)}, u32[]{:S(2)}, u32[]{:S(2)}) %collective-permute-start.13) | collective-permute-done | bytes 294944 | tf_op jit(solution)/shard_map/ppermute | solution.py:490
  42.5 0.5 collective-permute-start.25
  43.1 0.8 %collective-permute-done.25.rest_5_.rest_9_ = bf16[16,2048]{1,0:T(8,128)(2,1)S(1)} collective-permute-done((bf16[16,2048]{1,0:T(8,128)(2,1)S(1)}, bf16[16,2048]{1,0:T(8,128)(2,1)S(1)}, u32[]{:S(2)}, u32[]{:S(2)}) %collective-permute-start.25) | collective-permute-done | bytes 65568 | tf_op jit(solution)/shard_map/ppermute | solution.py:483
  43.9 0.4 collective-permute-start.31
  44.4 1.5 %grad_tokens.4 = (f32[128,1024]{1,0:T(8,128)S(1)}, f32[8,128]{1,0:T(8,128)S(1)}) custom-call(bf16[1024,2048]{1,0:T(8,128)(2,1)S(1)} %get-tuple-element.87.wg_ref, bf16[1024,2048]{1,0:T(8,128)(2,1)S(1)} %get-tuple-element.88.wu_ref, bf16[16,2048]{1,0:T(8,128)(2,1)S(1)} %get-tuple-element.109.rest_0_.rest_4_, ...), custom_call_target="tpu_custom_call" | custom-call | tf_op jit(solution)/shard_map/grad_tokens/pallas_call | solution.py:368
  45.9 2.6 %collective-permute-done.27.rest_0_ = bf16[3,48,1024]{2,1,0:T(8,128)(2,1)S(1)} collective-permute-done((bf16[3,48,1024]{2,1,0:T(8,128)(2,1)S(1)}, bf16[3,48,1024]{2,1,0:T(8,128)(2,1)S(1)}, u32[]{:S(2)}, u32[]{:S(2)}) %collective-permute-start.27) | collective-permute-done | bytes 294944 | tf_op jit(solution)/shard_map/ppermute | solution.py:490
  48.8 0.5 collective-permute-start.29
  49.4 1.1 %collective-permute-start.38 = (bf16[3,48,512]{2,1,0:T(8,128)(2,1)S(1)}, bf16[3,48,512]{2,1,0:T(8,128)(2,1)S(1)}, u32[]{:S(2)}, u32[]{:S(2)}) collective-permute-start(bf16[3,48,512]{2,1,0:T(8,128)(2,1)S(1)} %sum_cores.11.rest_1_.sum_ref), channel_id=1, source_target_pairs={{0,2},{1,3},{2,0},{3,1},{4,6},{5,7},{6,4},{7,5},{8,10},{9,11},{10,... | collective-permute-start | bytes 442376 | tf_op jit(solution)/shard_map/ppermute | solution.py:490
  50.5 3.6 %weight_grads.3 = (bf16[1024,3584]{1,0:T(8,128)(2,1)}, bf16[1024,3584]{1,0:T(8,128)(2,1)}, bf16[3584,1024]{1,0:T(8,128)(2,1)}, f32[8,128]{1,0:T(8,128)S(1)}) custom-call(bf16[1024,128]{1,0:T(8,128)(2,1)S(1)} %get-tuple-element.136.xt_ref, bf16[128,1024]{1,0:T(8,128)(2,1)S(1)} %get-tuple-element.100.og_ref, ...), custom_call_target="tpu_custom_call" | custom-call | tf_op jit(solution)/shard_map/weight_grads/pallas_call | solution.py:408
  54.1 1.5 %grad_tokens.5 = (f32[128,1024]{1,0:T(8,128)S(1)}, f32[8,128]{1,0:T(8,128)S(1)}) custom-call(f32[128,1024]{1,0:T(8,128)S(1)} %get-tuple-element.132.prev_ref, bf16[1024,2048]{1,0:T(8,128)(2,1)S(1)} %get-tuple-element.87.wg_ref, bf16[1024,2048]{1,0:T(8,128)(2,1)S(1)} %get-tuple-element.88.wu_ref, bf16[16,2048]{1,0:T(8,128)(2,1)S(1)} %get-tuple-element.109.rest_0_.rest_4_, ...), custom_call_target="tpu_custom_call" | custom-call | tf_op jit(solution)/shard_map/grad_tokens/pallas_call | solution.py:368
  56.0 0.3 collective-permute-start.36
  56.5 0.3 collective-permute-start.35
  56.8 3.6 %weight_grads.4 = (bf16[1024,3584]{1,0:T(8,128)(2,1)}, bf16[1024,3584]{1,0:T(8,128)(2,1)}, bf16[3584,1024]{1,0:T(8,128)(2,1)}, f32[8,128]{1,0:T(8,128)S(1)}) custom-call(bf16[1024,128]{1,0:T(8,128)(2,1)S(1)} %get-tuple-element.136.xt_ref, ...), custom_call_target="tpu_custom_call", output_to_operand_aliasing={{0}: (17, {}), {1}: (18, {}), {2}: (19, {})} | custom-call | tf_op jit(solution)/shard_map/weight_grads/pallas_call | solution.py:408
  60.5 1.5 %grad_tokens.6 = (f32[128,1024]{1,0:T(8,128)S(1)}, f32[8,128]{1,0:T(8,128)S(1)}) custom-call(f32[128,1024]{1,0:T(8,128)S(1)} %get-tuple-element.141.prev_ref, bf16[1024,1536]{1,0:T(8,128)(2,1)S(1)} %get-tuple-element.110.wg_ref, bf16[1024,1536]{1,0:T(8,128)(2,1)S(1)} %get-tuple-element.111.wu_ref, bf16[16,1536]{1,0:T(8,128)(2,1)S(1)} %get-tuple-element.142.rest_0_.rest_6_, ...), custom_call_target="tpu_custom_call" | custom-call | tf_op jit(solution)/shard_map/grad_tokens/pallas_call | solution.py:368
  62.3 0.3 collective-permute-start.40
  62.8 0.3 collective-permute-start.45
  63.5 0.8 %grad_tokens.7 = (bf16[96,1024]{1,0:T(8,128)(2,1)S(1)}, f32[32,1024]{1,0:T(8,128)S(1)}, f32[8,128]{1,0:T(8,128)S(1)}) custom-call(f32[128,1024]{1,0:T(8,128)S(1)} %get-tuple-element.153.prev_ref, bf16[1024,1536]{1,0:T(8,128)(2,1)S(1)} %get-tuple-element.110.wg_ref, bf16[1024,1536]{1,0:T(8,128)(2,1)S(1)} %get-tuple-element.111.wu_ref, ...), custom_call_target="tpu_custom_call" | custom-call | tf_op jit(solution)/shard_map/grad_tokens/pallas_call | solution.py:368
  64.3 1.6 %collective-permute-start.41 = (bf16[32,1024]{1,0:T(8,128)(2,1)S(1)}, bf16[32,1024]{1,0:T(8,128)(2,1)S(1)}, u32[]{:S(2)}, u32[]{:S(2)}) collective-permute-start(bf16[32,1024]{1,0:T(8,128)(2,1)S(1)} %get-tuple-element.172), channel_id=1, source_target_pairs={{0,4},{4,0},{8,12},{12,8},{1,5},{5,1},{9,13},{13,9},{2,6},{6,2},{1... | collective-permute-start | bytes 196616 | tf_op jit(solution)/shard_map/ppermute | solution.py:486
  66.0 0.3 collective-permute-start.42
  66.3 2.5 %collective-permute-start.43 = (bf16[32,1024]{1,0:T(8,128)(2,1)S(1)}, bf16[32,1024]{1,0:T(8,128)(2,1)S(1)}, u32[]{:S(2)}, u32[]{:S(2)}) collective-permute-start(bf16[32,1024]{1,0:T(8,128)(2,1)S(1)} %get-tuple-element.170), channel_id=1, source_target_pairs={{0,12},{4,8},{8,4},{12,0},{1,13},{5,9},{9,5},{13,1},{2,14},{6,10},... | collective-permute-start | bytes 196616 | tf_op jit(solution)/shard_map/ppermute | solution.py:486
  68.8 1.2 %collective-permute-done.46.rest_5_ = bf16[48,512]{1,0:T(8,128)(2,1)S(1)} collective-permute-done((bf16[48,512]{1,0:T(8,128)(2,1)S(1)}, bf16[48,512]{1,0:T(8,128)(2,1)S(1)}, u32[]{:S(2)}, u32[]{:S(2)}) %collective-permute-start.46) | collective-permute-done | bytes 49184 | tf_op jit(solution)/shard_map/ppermute | solution.py:483
  70.0 4.9 %weight_grads.5 = (bf16[1024,3584]{1,0:T(8,128)(2,1)}, bf16[1024,3584]{1,0:T(8,128)(2,1)}, bf16[3584,1024]{1,0:T(8,128)(2,1)}, f32[8,128]{1,0:T(8,128)}) custom-call(bf16[1024,128]{1,0:T(8,128)(2,1)S(1)} %get-tuple-element.136.xt_ref, bf16[128,1024]{1,0:T(8,128)(2,1)S(1)} %get-tuple-element.100.og_ref, ...), custom_call_target="tpu_custom_call", output_to_operand_aliasing={{0}: (23, {}), {1}: (24, {}), {2}: (25, {})} | custom-call | flops 1 | tf_op jit(solution)/shard_map/weight_grads/pallas_call | solution.py:408
  74.9 1.2 %finish.1 = bf16[32,1024]{1,0:T(8,128)(2,1)} custom-call(s32[3]{0:T(128)S(1)} %pad_add_fusion.place, f32[32,1024]{1,0:T(8,128)S(1)} %get-tuple-element.158.own_ref, bf16[32,1024]{1,0:T(8,128)(2,1)S(1)} %collective-permute-done.41.rest_0_, bf16[32,1024]{1,0:T(8,128)(2,1)S(1)} %collective-permute-done.42.rest_1_, ...), custom_call_target="tpu_custom_call" | custom-call | tf_op jit(solution)/shard_map/finish/pallas_call | solution.py:448
  (76 shorter events, 4.1 us)
Async XLA Ops:
  1.5 15.9 %collective-permute-start.5 = (bf16[2,32,1024]{2,1,0:T(8,128)(2,1)S(1)}, bf16[2,32,1024]{2,1,0:T(8,128)(2,1)S(1)}, u32[]{:S(2)}, u32[]{:S(2)}) collective-permute-start(bf16[2,32,1024]{2,1,0:T(8,128)(2,1)S(1)} %pad_maximum_fusion.both_ref), channel_id=1, source_target_pairs={{0,8},{4,12},{8,0},{12,4},{1,9},{5,13},{9,1},{13,5},{2,10},{6,14},... | collective-permute-start | bytes 393224 | tf_op jit(solution)/shard_map/ppermute | solution.py:486
  15.2 2.7 %collective-permute-start = (bf16[1,16,2048]{2,1,0:T(8,128)(2,1)S(1)}, bf16[1,16,2048]{2,1,0:T(8,128)(2,1)S(1)}, u32[]{:S(2)}, u32[]{:S(2)}) collective-permute-start(bf16[1,16,2048]{2,1,0:T(8,128)(2,1)S(1)} %get-tuple-element.90), channel_id=1, source_target_pairs={{0,1},{1,0},{2,3},{3,2},{4,5},{5,4},{6,7},{7,6},{8,9},{9,8},{10,11... | collective-permute-start | bytes 196616 | tf_op jit(solution)/shard_map/ppermute | solution.py:483
  15.3 2.6 %collective-permute-start.1 = (bf16[1,16,2048]{2,1,0:T(8,128)(2,1)S(1)}, bf16[1,16,2048]{2,1,0:T(8,128)(2,1)S(1)}, u32[]{:S(2)}, u32[]{:S(2)}) collective-permute-start(bf16[1,16,2048]{2,1,0:T(8,128)(2,1)S(1)} %get-tuple-element.91), channel_id=1, source_target_pairs={{0,1},{1,0},{2,3},{3,2},{4,5},{5,4},{6,7},{7,6},{8,9},{9,8},{10,11... | collective-permute-start | bytes 196616 | tf_op jit(solution)/shard_map/ppermute | solution.py:483
  15.7 2.1 %collective-permute-start.2 = (bf16[1,16,2048]{2,1,0:T(8,128)(2,1)S(1)}, bf16[1,16,2048]{2,1,0:T(8,128)(2,1)S(1)}, u32[]{:S(2)}, u32[]{:S(2)}) collective-permute-start(bf16[1,16,2048]{2,1,0:T(8,128)(2,1)S(1)} %get-tuple-element.92), channel_id=1, source_target_pairs={{0,1},{1,0},{2,3},{3,2},{4,5},{5,4},{6,7},{7,6},{8,9},{9,8},{10,11... | collective-permute-start | bytes 196616 | tf_op jit(solution)/shard_map/ppermute | solution.py:483
  15.8 10.5 %collective-permute-start.4 = (bf16[2,32,1024]{2,1,0:T(8,128)(2,1)S(1)}, bf16[2,32,1024]{2,1,0:T(8,128)(2,1)S(1)}, u32[]{:S(2)}, u32[]{:S(2)}) collective-permute-start(bf16[2,32,1024]{2,1,0:T(8,128)(2,1)S(1)} %pad_maximum_fusion.both_ref), channel_id=1, source_target_pairs={{0,4},{4,0},{8,12},{12,8},{1,5},{5,1},{9,13},{13,9},{2,6},{6,2},{1... | collective-permute-start | bytes 393224 | tf_op jit(solution)/shard_map/ppermute | solution.py:486
  17.4 9.0 %collective-permute-start.6 = (bf16[2,32,1024]{2,1,0:T(8,128)(2,1)S(1)}, bf16[2,32,1024]{2,1,0:T(8,128)(2,1)S(1)}, u32[]{:S(2)}, u32[]{:S(2)}) collective-permute-start(bf16[2,32,1024]{2,1,0:T(8,128)(2,1)S(1)} %collective-permute-done.5.rest_1_), channel_id=1, source_target_pairs={{0,4},{4,0},{8,12},{12,8},{1,5},{5,1},{9,13},{13,9},{2,6},{6,2},{1... | collective-permute-start | bytes 393224 | tf_op jit(solution)/shard_map/ppermute | solution.py:486
  23.4 2.9 %collective-permute-start.7 = (bf16[2,16,1536]{2,1,0:T(8,128)(2,1)S(1)}, bf16[2,16,1536]{2,1,0:T(8,128)(2,1)S(1)}, u32[]{:S(2)}, u32[]{:S(2)}) collective-permute-start(bf16[2,16,1536]{2,1,0:T(8,128)(2,1)S(1)} %get-tuple-element.97), channel_id=1, source_target_pairs={{0,1},{1,0},{2,3},{3,2},{4,5},{5,4},{6,7},{7,6},{8,9},{9,8},{10,11... | collective-permute-start | bytes 294920 | tf_op jit(solution)/shard_map/ppermute | solution.py:483
  23.5 10.0 %collective-permute-start.3 = (bf16[3,16,2048]{2,1,0:T(8,128)(2,1)S(1)}, bf16[3,16,2048]{2,1,0:T(8,128)(2,1)S(1)}, u32[]{:S(2)}, u32[]{:S(2)}) collective-permute-start(bf16[3,16,2048]{2,1,0:T(8,128)(2,1)S(1)} %sum_cores.6.rest_3_.sum_ref), channel_id=1, source_target_pairs={{0,2},{1,3},{2,0},{3,1},{4,6},{5,7},{6,4},{7,5},{8,10},{9,11},{10,... | collective-permute-start | bytes 589832 | tf_op jit(solution)/shard_map/ppermute | solution.py:490
  25.1 1.2 %collective-permute-start.8 = (bf16[1,16,1536]{2,1,0:T(8,128)(2,1)S(1)}, bf16[1,16,1536]{2,1,0:T(8,128)(2,1)S(1)}, u32[]{:S(2)}, u32[]{:S(2)}) collective-permute-start(bf16[1,16,1536]{2,1,0:T(8,128)(2,1)S(1)} %get-tuple-element.98), channel_id=1, source_target_pairs={{0,1},{1,0},{2,3},{3,2},{4,5},{5,4},{6,7},{7,6},{8,9},{9,8},{10,11... | collective-permute-start | bytes 147464 | tf_op jit(solution)/shard_map/ppermute | solution.py:483
  28.5 2.7 %collective-permute-start.10 = (bf16[1,48,1024]{2,1,0:T(8,128)(2,1)S(1)}, bf16[1,48,1024]{2,1,0:T(8,128)(2,1)S(1)}, u32[]{:S(2)}, u32[]{:S(2)}) collective-permute-start(bf16[1,48,1024]{2,1,0:T(8,128)(2,1)S(1)} %get-tuple-element.107), channel_id=1, source_target_pairs={{0,1},{1,0},{2,3},{3,2},{4,5},{5,4},{6,7},{7,6},{8,9},{9,8},{10,11... | collective-permute-start | bytes 294920 | tf_op jit(solution)/shard_map/ppermute | solution.py:483
  28.8 2.6 %collective-permute-start.11 = (bf16[1,48,1024]{2,1,0:T(8,128)(2,1)S(1)}, bf16[1,48,1024]{2,1,0:T(8,128)(2,1)S(1)}, u32[]{:S(2)}, u32[]{:S(2)}) collective-permute-start(bf16[1,48,1024]{2,1,0:T(8,128)(2,1)S(1)} %get-tuple-element.108), channel_id=1, source_target_pairs={{0,1},{1,0},{2,3},{3,2},{4,5},{5,4},{6,7},{7,6},{8,9},{9,8},{10,11... | collective-permute-start | bytes 294920 | tf_op jit(solution)/shard_map/ppermute | solution.py:483
  29.1 2.7 %collective-permute-start.9 = (bf16[1,48,1024]{2,1,0:T(8,128)(2,1)S(1)}, bf16[1,48,1024]{2,1,0:T(8,128)(2,1)S(1)}, u32[]{:S(2)}, u32[]{:S(2)}) collective-permute-start(bf16[1,48,1024]{2,1,0:T(8,128)(2,1)S(1)} %get-tuple-element.106), channel_id=1, source_target_pairs={{0,1},{1,0},{2,3},{3,2},{4,5},{5,4},{6,7},{7,6},{8,9},{9,8},{10,11... | collective-permute-start | bytes 294920 | tf_op jit(solution)/shard_map/ppermute | solution.py:483
  29.3 7.1 %collective-permute-start.14 = (bf16[3,16,1536]{2,1,0:T(8,128)(2,1)S(1)}, bf16[3,16,1536]{2,1,0:T(8,128)(2,1)S(1)}, u32[]{:S(2)}, u32[]{:S(2)}) collective-permute-start(bf16[3,16,1536]{2,1,0:T(8,128)(2,1)S(1)} %sum_cores.7.rest_3_.sum_ref), channel_id=1, source_target_pairs={{0,2},{1,3},{2,0},{3,1},{4,6},{5,7},{6,4},{7,5},{8,10},{9,11},{10,... | collective-permute-start | bytes 442376 | tf_op jit(solution)/shard_map/ppermute | solution.py:490
  31.3 3.8 %collective-permute-start.15 = (bf16[1,48,1024]{2,1,0:T(8,128)(2,1)S(1)}, bf16[1,48,1024]{2,1,0:T(8,128)(2,1)S(1)}, u32[]{:S(2)}, u32[]{:S(2)}) collective-permute-start(bf16[1,48,1024]{2,1,0:T(8,128)(2,1)S(1)} %get-tuple-element.116), channel_id=1, source_target_pairs={{0,1},{1,0},{2,3},{3,2},{4,5},{5,4},{6,7},{7,6},{8,9},{9,8},{10,11... | collective-permute-start | bytes 294920 | tf_op jit(solution)/shard_map/ppermute | solution.py:483
  31.4 4.2 %collective-permute-start.16 = (bf16[1,48,1024]{2,1,0:T(8,128)(2,1)S(1)}, bf16[1,48,1024]{2,1,0:T(8,128)(2,1)S(1)}, u32[]{:S(2)}, u32[]{:S(2)}) collective-permute-start(bf16[1,48,1024]{2,1,0:T(8,128)(2,1)S(1)} %get-tuple-element.117), channel_id=1, source_target_pairs={{0,1},{1,0},{2,3},{3,2},{4,5},{5,4},{6,7},{7,6},{8,9},{9,8},{10,11... | collective-permute-start | bytes 294920 | tf_op jit(solution)/shard_map/ppermute | solution.py:483
  31.9 10.3 %collective-permute-start.13 = (bf16[3,48,1024]{2,1,0:T(8,128)(2,1)S(1)}, bf16[3,48,1024]{2,1,0:T(8,128)(2,1)S(1)}, u32[]{:S(2)}, u32[]{:S(2)}) collective-permute-start(bf16[3,48,1024]{2,1,0:T(8,128)(2,1)S(1)} %sum_cores.8.rest_2_.rest_3_.sum_ref), channel_id=1, source_target_pairs={{0,2},{1,3},{2,0},{3,1},{4,6},{5,7},{6,4},{7,5},{8,10},{9,11},{10,... | collective-permute-start | bytes 884744 | tf_op jit(solution)/shard_map/ppermute | solution.py:490
  33.5 2.2 %collective-permute-start.17 = (bf16[1,48,1024]{2,1,0:T(8,128)(2,1)S(1)}, bf16[1,48,1024]{2,1,0:T(8,128)(2,1)S(1)}, u32[]{:S(2)}, u32[]{:S(2)}) collective-permute-start(bf16[1,48,1024]{2,1,0:T(8,128)(2,1)S(1)} %get-tuple-element.118), channel_id=1, source_target_pairs={{0,1},{1,0},{2,3},{3,2},{4,5},{5,4},{6,7},{7,6},{8,9},{9,8},{10,11... | collective-permute-start | bytes 294920 | tf_op jit(solution)/shard_map/ppermute | solution.py:483
  35.0 2.8 %collective-permute-start.21 = (bf16[1,48,1024]{2,1,0:T(8,128)(2,1)S(1)}, bf16[1,48,1024]{2,1,0:T(8,128)(2,1)S(1)}, u32[]{:S(2)}, u32[]{:S(2)}) collective-permute-start(bf16[1,48,1024]{2,1,0:T(8,128)(2,1)S(1)} %get-tuple-element.125), channel_id=1, source_target_pairs={{0,1},{1,0},{2,3},{3,2},{4,5},{5,4},{6,7},{7,6},{8,9},{9,8},{10,11... | collective-permute-start | bytes 294920 | tf_op jit(solution)/shard_map/ppermute | solution.py:483
  35.6 2.6 %collective-permute-start.22 = (bf16[1,48,1024]{2,1,0:T(8,128)(2,1)S(1)}, bf16[1,48,1024]{2,1,0:T(8,128)(2,1)S(1)}, u32[]{:S(2)}, u32[]{:S(2)}) collective-permute-start(bf16[1,48,1024]{2,1,0:T(8,128)(2,1)S(1)} %get-tuple-element.126), channel_id=1, source_target_pairs={{0,1},{1,0},{2,3},{3,2},{4,5},{5,4},{6,7},{7,6},{8,9},{9,8},{10,11... | collective-permute-start | bytes 294920 | tf_op jit(solution)/shard_map/ppermute | solution.py:483
  35.8 12.8 %collective-permute-start.27 = (bf16[3,48,1024]{2,1,0:T(8,128)(2,1)S(1)}, bf16[3,48,1024]{2,1,0:T(8,128)(2,1)S(1)}, u32[]{:S(2)}, u32[]{:S(2)}) collective-permute-start(bf16[3,48,1024]{2,1,0:T(8,128)(2,1)S(1)} %sum_cores.9.rest_2_.rest_3_.sum_ref), channel_id=1, source_target_pairs={{0,2},{1,3},{2,0},{3,1},{4,6},{5,7},{6,4},{7,5},{8,10},{9,11},{10,... | collective-permute-start | bytes 884744 | tf_op jit(solution)/shard_map/ppermute | solution.py:490
  36.4 2.0 %collective-permute-start.23 = (bf16[1,48,1024]{2,1,0:T(8,128)(2,1)S(1)}, bf16[1,48,1024]{2,1,0:T(8,128)(2,1)S(1)}, u32[]{:S(2)}, u32[]{:S(2)}) collective-permute-start(bf16[1,48,1024]{2,1,0:T(8,128)(2,1)S(1)} %get-tuple-element.127), channel_id=1, source_target_pairs={{0,1},{1,0},{2,3},{3,2},{4,5},{5,4},{6,7},{7,6},{8,9},{9,8},{10,11... | collective-permute-start | bytes 294920 | tf_op jit(solution)/shard_map/ppermute | solution.py:483
  37.9 2.1 %collective-permute-start.18 = (bf16[1,48,512]{2,1,0:T(8,128)(2,1)S(1)}, bf16[1,48,512]{2,1,0:T(8,128)(2,1)S(1)}, u32[]{:S(2)}, u32[]{:S(2)}) collective-permute-start(bf16[1,48,512]{2,1,0:T(8,128)(2,1)S(1)} %get-tuple-element.121), channel_id=1, source_target_pairs={{0,1},{1,0},{2,3},{3,2},{4,5},{5,4},{6,7},{7,6},{8,9},{9,8},{10,11... | collective-permute-start | bytes 147464 | tf_op jit(solution)/shard_map/ppermute | solution.py:483
  38.2 1.9 %collective-permute-start.19 = (bf16[1,48,512]{2,1,0:T(8,128)(2,1)S(1)}, bf16[1,48,512]{2,1,0:T(8,128)(2,1)S(1)}, u32[]{:S(2)}, u32[]{:S(2)}) collective-permute-start(bf16[1,48,512]{2,1,0:T(8,128)(2,1)S(1)} %get-tuple-element.122), channel_id=1, source_target_pairs={{0,1},{1,0},{2,3},{3,2},{4,5},{5,4},{6,7},{7,6},{8,9},{9,8},{10,11... | collective-permute-start | bytes 147464 | tf_op jit(solution)/shard_map/ppermute | solution.py:483
  38.5 17.1 %collective-permute-start.33 = (bf16[3,48,1024]{2,1,0:T(8,128)(2,1)S(1)}, bf16[3,48,1024]{2,1,0:T(8,128)(2,1)S(1)}, u32[]{:S(2)}, u32[]{:S(2)}) collective-permute-start(bf16[3,48,1024]{2,1,0:T(8,128)(2,1)S(1)} %sum_cores.10.rest_3_.sum_ref), channel_id=1, source_target_pairs={{0,2},{1,3},{2,0},{3,1},{4,6},{5,7},{6,4},{7,5},{8,10},{9,11},{10,... | collective-permute-start | bytes 884744 | tf_op jit(solution)/shard_map/ppermute | solution.py:490
  40.0 3.0 %collective-permute-start.12 = (bf16[16,2048]{1,0:T(8,128)(2,1)S(1)}, bf16[16,2048]{1,0:T(8,128)(2,1)S(1)}, u32[]{:S(2)}, u32[]{:S(2)}) collective-permute-start(bf16[16,2048]{1,0:T(8,128)(2,1)S(1)} %get-tuple-element.109.rest_0_.rest_4_), channel_id=1, source_target_pairs={{0,1},{1,0},{2,3},{3,2},{4,5},{5,4},{6,7},{7,6},{8,9},{9,8},{10,11... | collective-permute-start | bytes 196616 | tf_op jit(solution)/shard_map/ppermute | solution.py:483
  40.1 1.3 %collective-permute-start.20 = (bf16[1,48,512]{2,1,0:T(8,128)(2,1)S(1)}, bf16[1,48,512]{2,1,0:T(8,128)(2,1)S(1)}, u32[]{:S(2)}, u32[]{:S(2)}) collective-permute-start(bf16[1,48,512]{2,1,0:T(8,128)(2,1)S(1)} %get-tuple-element.123), channel_id=1, source_target_pairs={{0,1},{1,0},{2,3},{3,2},{4,5},{5,4},{6,7},{7,6},{8,9},{9,8},{10,11... | collective-permute-start | bytes 147464 | tf_op jit(solution)/shard_map/ppermute | solution.py:483
  42.4 1.8 %collective-permute-start.24 = (bf16[48,1024]{1,0:T(8,128)(2,1)S(1)}, bf16[48,1024]{1,0:T(8,128)(2,1)S(1)}, u32[]{:S(2)}, u32[]{:S(2)}) collective-permute-start(bf16[48,1024]{1,0:T(8,128)(2,1)S(1)} %get-tuple-element.128.rest_2_.rest_6_), channel_id=1, source_target_pairs={{0,1},{1,0},{2,3},{3,2},{4,5},{5,4},{6,7},{7,6},{8,9},{9,8},{10,11... | collective-permute-start | bytes 294920 | tf_op jit(solution)/shard_map/ppermute | solution.py:483
  42.5 1.4 %collective-permute-start.25 = (bf16[16,2048]{1,0:T(8,128)(2,1)S(1)}, bf16[16,2048]{1,0:T(8,128)(2,1)S(1)}, u32[]{:S(2)}, u32[]{:S(2)}) collective-permute-start(bf16[16,2048]{1,0:T(8,128)(2,1)S(1)} %get-tuple-element.129.rest_4_.rest_8_), channel_id=1, source_target_pairs={{0,1},{1,0},{2,3},{3,2},{4,5},{5,4},{6,7},{7,6},{8,9},{9,8},{10,11... | collective-permute-start | bytes 196616 | tf_op jit(solution)/shard_map/ppermute | solution.py:483
  43.0 1.4 %collective-permute-start.26 = (bf16[48,1024]{1,0:T(8,128)(2,1)S(1)}, bf16[48,1024]{1,0:T(8,128)(2,1)S(1)}, u32[]{:S(2)}, u32[]{:S(2)}) collective-permute-start(bf16[48,1024]{1,0:T(8,128)(2,1)S(1)} %get-tuple-element.130.rest_6_.rest_10_), channel_id=1, source_target_pairs={{0,1},{1,0},{2,3},{3,2},{4,5},{5,4},{6,7},{7,6},{8,9},{9,8},{10,11... | collective-permute-start | bytes 294920 | tf_op jit(solution)/shard_map/ppermute | solution.py:483
  43.9 5.5 %collective-permute-start.31 = (bf16[48,1024]{1,0:T(8,128)(2,1)S(1)}, bf16[48,1024]{1,0:T(8,128)(2,1)S(1)}, u32[]{:S(2)}, u32[]{:S(2)}) collective-permute-start(bf16[48,1024]{1,0:T(8,128)(2,1)S(1)} %get-tuple-element.138.rest_2_), channel_id=1, source_target_pairs={{0,1},{1,0},{2,3},{3,2},{4,5},{5,4},{6,7},{7,6},{8,9},{9,8},{10,11... | collective-permute-start | bytes 294920 | tf_op jit(solution)/shard_map/ppermute | solution.py:483
  44.3 5.1 %collective-permute-start.30 = (bf16[16,2048]{1,0:T(8,128)(2,1)S(1)}, bf16[16,2048]{1,0:T(8,128)(2,1)S(1)}, u32[]{:S(2)}, u32[]{:S(2)}) collective-permute-start(bf16[16,2048]{1,0:T(8,128)(2,1)S(1)} %get-tuple-element.137.rest_0_), channel_id=1, source_target_pairs={{0,1},{1,0},{2,3},{3,2},{4,5},{5,4},{6,7},{7,6},{8,9},{9,8},{10,11... | collective-permute-start | bytes 196616 | tf_op jit(solution)/shard_map/ppermute | solution.py:483
  48.7 5.3 %collective-permute-start.28 = (bf16[48,1024]{1,0:T(8,128)(2,1)S(1)}, bf16[48,1024]{1,0:T(8,128)(2,1)S(1)}, u32[]{:S(2)}, u32[]{:S(2)}) collective-permute-start(bf16[48,1024]{1,0:T(8,128)(2,1)S(1)} %get-tuple-element.134.rest_2_.rest_6_), channel_id=1, source_target_pairs={{0,1},{1,0},{2,3},{3,2},{4,5},{5,4},{6,7},{7,6},{8,9},{9,8},{10,11... | collective-permute-start | bytes 294920 | tf_op jit(solution)/shard_map/ppermute | solution.py:483
  48.8 5.2 %collective-permute-start.29 = (bf16[48,1024]{1,0:T(8,128)(2,1)S(1)}, bf16[48,1024]{1,0:T(8,128)(2,1)S(1)}, u32[]{:S(2)}, u32[]{:S(2)}) collective-permute-start(bf16[48,1024]{1,0:T(8,128)(2,1)S(1)} %get-tuple-element.135.rest_6_.rest_10_), channel_id=1, source_target_pairs={{0,1},{1,0},{2,3},{3,2},{4,5},{5,4},{6,7},{7,6},{8,9},{9,8},{10,11... | collective-permute-start | bytes 294920 | tf_op jit(solution)/shard_map/ppermute | solution.py:483
  49.3 7.2 %collective-permute-start.37 = (bf16[48,1024]{1,0:T(8,128)(2,1)S(1)}, bf16[48,1024]{1,0:T(8,128)(2,1)S(1)}, u32[]{:S(2)}, u32[]{:S(2)}) collective-permute-start(bf16[48,1024]{1,0:T(8,128)(2,1)S(1)} %get-tuple-element.147.rest_2_), channel_id=1, source_target_pairs={{0,1},{1,0},{2,3},{3,2},{4,5},{5,4},{6,7},{7,6},{8,9},{9,8},{10,11... | collective-permute-start | bytes 294920 | tf_op jit(solution)/shard_map/ppermute | solution.py:483
  49.4 12.5 %collective-permute-start.38 = (bf16[3,48,512]{2,1,0:T(8,128)(2,1)S(1)}, bf16[3,48,512]{2,1,0:T(8,128)(2,1)S(1)}, u32[]{:S(2)}, u32[]{:S(2)}) collective-permute-start(bf16[3,48,512]{2,1,0:T(8,128)(2,1)S(1)} %sum_cores.11.rest_1_.sum_ref), channel_id=1, source_target_pairs={{0,2},{1,3},{2,0},{3,1},{4,6},{5,7},{6,4},{7,5},{8,10},{9,11},{10,... | collective-permute-start | bytes 442376 | tf_op jit(solution)/shard_map/ppermute | solution.py:490
  55.8 4.7 %collective-permute-start.34 = (bf16[48,1024]{1,0:T(8,128)(2,1)S(1)}, bf16[48,1024]{1,0:T(8,128)(2,1)S(1)}, u32[]{:S(2)}, u32[]{:S(2)}) collective-permute-start(bf16[48,1024]{1,0:T(8,128)(2,1)S(1)} %get-tuple-element.144.rest_2_.rest_8_), channel_id=1, source_target_pairs={{0,1},{1,0},{2,3},{3,2},{4,5},{5,4},{6,7},{7,6},{8,9},{9,8},{10,11... | collective-permute-start | bytes 294920 | tf_op jit(solution)/shard_map/ppermute | solution.py:483
  56.0 4.5 %collective-permute-start.36 = (bf16[48,1024]{1,0:T(8,128)(2,1)S(1)}, bf16[48,1024]{1,0:T(8,128)(2,1)S(1)}, u32[]{:S(2)}, u32[]{:S(2)}) collective-permute-start(bf16[48,1024]{1,0:T(8,128)(2,1)S(1)} %get-tuple-element.146.rest_6_.rest_14_), channel_id=1, source_target_pairs={{0,1},{1,0},{2,3},{3,2},{4,5},{5,4},{6,7},{7,6},{8,9},{9,8},{10,11... | collective-permute-start | bytes 294920 | tf_op jit(solution)/shard_map/ppermute | solution.py:483
  56.3 4.1 %collective-permute-start.32 = (bf16[16,1536]{1,0:T(8,128)(2,1)S(1)}, bf16[16,1536]{1,0:T(8,128)(2,1)S(1)}, u32[]{:S(2)}, u32[]{:S(2)}) collective-permute-start(bf16[16,1536]{1,0:T(8,128)(2,1)S(1)} %get-tuple-element.142.rest_0_.rest_6_), channel_id=1, source_target_pairs={{0,1},{1,0},{2,3},{3,2},{4,5},{5,4},{6,7},{7,6},{8,9},{9,8},{10,11... | collective-permute-start | bytes 147464 | tf_op jit(solution)/shard_map/ppermute | solution.py:483
  56.5 3.9 %collective-permute-start.35 = (bf16[16,1536]{1,0:T(8,128)(2,1)S(1)}, bf16[16,1536]{1,0:T(8,128)(2,1)S(1)}, u32[]{:S(2)}, u32[]{:S(2)}) collective-permute-start(bf16[16,1536]{1,0:T(8,128)(2,1)S(1)} %get-tuple-element.145.rest_4_.rest_12_), channel_id=1, source_target_pairs={{0,1},{1,0},{2,3},{3,2},{4,5},{5,4},{6,7},{7,6},{8,9},{9,8},{10,11... | collective-permute-start | bytes 147464 | tf_op jit(solution)/shard_map/ppermute | solution.py:483
  62.0 1.3 %collective-permute-start.39 = (bf16[48,512]{1,0:T(8,128)(2,1)S(1)}, bf16[48,512]{1,0:T(8,128)(2,1)S(1)}, u32[]{:S(2)}, u32[]{:S(2)}) collective-permute-start(bf16[48,512]{1,0:T(8,128)(2,1)S(1)} %get-tuple-element.155.rest_2_.rest_10_), channel_id=1, source_target_pairs={{0,1},{1,0},{2,3},{3,2},{4,5},{5,4},{6,7},{7,6},{8,9},{9,8},{10,11... | collective-permute-start | bytes 147464 | tf_op jit(solution)/shard_map/ppermute | solution.py:483
  62.3 1.2 %collective-permute-start.40 = (bf16[48,512]{1,0:T(8,128)(2,1)S(1)}, bf16[48,512]{1,0:T(8,128)(2,1)S(1)}, u32[]{:S(2)}, u32[]{:S(2)}) collective-permute-start(bf16[48,512]{1,0:T(8,128)(2,1)S(1)} %get-tuple-element.156.rest_6_.rest_16_), channel_id=1, source_target_pairs={{0,1},{1,0},{2,3},{3,2},{4,5},{5,4},{6,7},{7,6},{8,9},{9,8},{10,11... | collective-permute-start | bytes 147464 | tf_op jit(solution)/shard_map/ppermute | solution.py:483
  62.6 6.2 %collective-permute-start.44 = (bf16[16,1536]{1,0:T(8,128)(2,1)S(1)}, bf16[16,1536]{1,0:T(8,128)(2,1)S(1)}, u32[]{:S(2)}, u32[]{:S(2)}) collective-permute-start(bf16[16,1536]{1,0:T(8,128)(2,1)S(1)} %get-tuple-element.160.rest_0_), channel_id=1, source_target_pairs={{0,1},{1,0},{2,3},{3,2},{4,5},{5,4},{6,7},{7,6},{8,9},{9,8},{10,11... | collective-permute-start | bytes 147464 | tf_op jit(solution)/shard_map/ppermute | solution.py:483
  62.8 6.0 %collective-permute-start.45 = (bf16[48,1024]{1,0:T(8,128)(2,1)S(1)}, bf16[48,1024]{1,0:T(8,128)(2,1)S(1)}, u32[]{:S(2)}, u32[]{:S(2)}) collective-permute-start(bf16[48,1024]{1,0:T(8,128)(2,1)S(1)} %get-tuple-element.161.rest_2_), channel_id=1, source_target_pairs={{0,1},{1,0},{2,3},{3,2},{4,5},{5,4},{6,7},{7,6},{8,9},{9,8},{10,11... | collective-permute-start | bytes 294920 | tf_op jit(solution)/shard_map/ppermute | solution.py:483
  64.3 10.6 %collective-permute-start.41 = (bf16[32,1024]{1,0:T(8,128)(2,1)S(1)}, bf16[32,1024]{1,0:T(8,128)(2,1)S(1)}, u32[]{:S(2)}, u32[]{:S(2)}) collective-permute-start(bf16[32,1024]{1,0:T(8,128)(2,1)S(1)} %get-tuple-element.172), channel_id=1, source_target_pairs={{0,4},{4,0},{8,12},{12,8},{1,5},{5,1},{9,13},{13,9},{2,6},{6,2},{1... | collective-permute-start | bytes 196616 | tf_op jit(solution)/shard_map/ppermute | solution.py:486
  66.0 8.9 %collective-permute-start.42 = (bf16[32,1024]{1,0:T(8,128)(2,1)S(1)}, bf16[32,1024]{1,0:T(8,128)(2,1)S(1)}, u32[]{:S(2)}, u32[]{:S(2)}) collective-permute-start(bf16[32,1024]{1,0:T(8,128)(2,1)S(1)} %get-tuple-element.171), channel_id=1, source_target_pairs={{0,8},{4,12},{8,0},{12,4},{1,9},{5,13},{9,1},{13,5},{2,10},{6,14},... | collective-permute-start | bytes 196616 | tf_op jit(solution)/shard_map/ppermute | solution.py:486
  66.3 8.6 %collective-permute-start.43 = (bf16[32,1024]{1,0:T(8,128)(2,1)S(1)}, bf16[32,1024]{1,0:T(8,128)(2,1)S(1)}, u32[]{:S(2)}, u32[]{:S(2)}) collective-permute-start(bf16[32,1024]{1,0:T(8,128)(2,1)S(1)} %get-tuple-element.170), channel_id=1, source_target_pairs={{0,12},{4,8},{8,4},{12,0},{1,13},{5,9},{9,5},{13,1},{2,14},{6,10},... | collective-permute-start | bytes 196616 | tf_op jit(solution)/shard_map/ppermute | solution.py:486
  68.8 1.2 %collective-permute-start.46 = (bf16[48,512]{1,0:T(8,128)(2,1)S(1)}, bf16[48,512]{1,0:T(8,128)(2,1)S(1)}, u32[]{:S(2)}, u32[]{:S(2)}) collective-permute-start(bf16[48,512]{1,0:T(8,128)(2,1)S(1)} %get-tuple-element.162.rest_4_), channel_id=1, source_target_pairs={{0,1},{1,0},{2,3},{3,2},{4,5},{5,4},{6,7},{7,6},{8,9},{9,8},{10,11... | collective-permute-start | bytes 147464 | tf_op jit(solution)/shard_map/ppermute | solution.py:483
